TPU v7x, 512 devices: a whole 4x8x8 slice. The times are simulated.
512 devices in a mesh: replica: 16 (over y_lo, x), fsdp: 32 (over z, y_hi, core).
Axes of the slice: x: 4, y: 8 (y_hi: 2, y_lo: 4; y = y_hi * 4 + y_lo), z: 8, core: 2. Of those that a mesh axis runs over, the one named last changes fastest.
Arguments:
- base_weights: float32 [8192, 1024], P('fsdp'), may hold values from -5 to 5, as said below
- inner_weights: bfloat16 [16, 8192, 1024], P('replica', 'fsdp'), may hold values from -12 to 12, as said below
- momentum: float32 [8192, 1024], P(('fsdp', 'replica')), may hold values from -1 to 1
Outputs:
- new_base: float32 [8192, 1024], P('fsdp')
- new_momentum: float32 [8192, 1024], P(('fsdp', 'replica'))
- new_inner: bfloat16 [16, 8192, 1024], P('replica', 'fsdp')
Inputs may be any that keep to these rules, and one draw needn't show every extreme that they name: `base_weights`: the shared outer weights, multiples of 2 ** -16. `inner_weights`: each replica's weights after its inner steps, multiples of 2 ** -16.
All inputs are finite; a program needn't handle non-finite values.
Results may differ from a plain program's by a relative error of at most 0.0015.
Values may be sent and summed in bfloat16 or wider, within the bound.
No kernel may reach another device: no remote copies, remote signals or barrier semaphores. Data moves between devices by JAX's collectives and lax.ppermute only.
A program may use at most 64 MiB of HBM per device.

v0:
```python
import functools

import jax
import jax.numpy as jnp
from jax import lax
from jax.sharding import Mesh
from jax.sharding import PartitionSpec as P

D = 8192
KVW = 1024
BLOCK = 128
REPLICA = ("replica_0", "replica_1")
REPLICA_FSDP = ("replica_0", "replica_1", "fsdp_0", "fsdp_1", "fsdp_2")
FSDP = ("fsdp_0", "fsdp_1", "fsdp_2")
FSDP_REPLICA = ("fsdp_0", "fsdp_1", "fsdp_2", "replica_0", "replica_1")


code_limit = 448.0
outer_rate = 0.7
outer_momentum = 0.9
blend_share = 0.5
clip_rms = 0.02
epsilon = 1e-06
smallest_normal = 0.015625


def split_up(value, dim, devices):
    dims = value.shape
    blocks = value.reshape(*dims[:dim], devices, dims[dim] // devices, *dims[dim + 1 :])
    return jnp.moveaxis(blocks, dim, 0)


def summed_on_arrival(value, axis, dim):
    blocks = split_up(value, dim, lax.axis_size(axis))
    arrived = lax.all_to_all(blocks, axis, split_axis=0, concat_axis=0, tiled=True)
    return arrived.astype(jnp.float32).sum(axis=0)


def over_axes(value, axes):
    return functools.reduce(lax.psum, axes, value)


def from_everyone(value, axis):
    copies = jnp.broadcast_to(value, (lax.axis_size(axis), *value.shape))
    return lax.all_to_all(copies, axis, split_axis=0, concat_axis=0, tiled=True)


def in_order(blocks, dim):
    dims = list(blocks.shape[1:])
    dims[dim] *= blocks.shape[0]
    return jnp.moveaxis(blocks, 0, dim).reshape(dims)


def gathered_copies(value, axis, dim):
    blocks = from_everyone(value, axis)
    return in_order(blocks, dim)


def power_two(exponent):
    unit_ones = jnp.ones_like(exponent)
    upward = jnp.left_shift(unit_ones, jnp.maximum(exponent, 0)).astype(jnp.float32)
    downward = jnp.left_shift(unit_ones, jnp.maximum(-exponent, 0)).astype(jnp.float32)
    return upward / downward


def exponent_above(target):
    estimate = jnp.ceil(jnp.log2(target)).astype(jnp.int32)
    estimate = jnp.where(target <= power_two(estimate - 1), estimate - 1, estimate)
    return jnp.where(target > power_two(estimate), estimate + 1, estimate)


def exponent_below(target):
    estimate = jnp.floor(jnp.log2(target)).astype(jnp.int32)
    estimate = jnp.where(target >= power_two(estimate + 1), estimate + 1, estimate)
    return jnp.where(target < power_two(estimate), estimate - 1, estimate)


def encode(deltas):
    shaped = deltas.reshape(deltas.shape[0], deltas.shape[1] // BLOCK, BLOCK)
    block_peaks = jnp.max(jnp.abs(shaped), axis=2)
    scales = power_two(exponent_above((block_peaks + epsilon) / code_limit))
    code_units = shaped / scales[:, :, None]
    magnitude = jnp.abs(code_units)
    quantum = power_two(exponent_below(jnp.maximum(magnitude, smallest_normal)) - 3)
    steps_count = jnp.floor(magnitude / quantum + 0.5)
    code_values = (jnp.where(code_units < 0, -steps_count, steps_count) * quantum).astype(
        jnp.bfloat16
    )
    return (code_values, scales)


def shards(base_weights, inner_weights, momentum):
    replicas = lax.axis_size(REPLICA)
    local_rows, columns_all = base_weights.shape
    owned_rows = local_rows // replicas
    replica_copy = inner_weights[0]
    deltas = base_weights - replica_copy.astype(jnp.float32)
    code_values, scales = encode(deltas)
    decoded = (code_values.astype(jnp.float32) * scales[:, :, None]).reshape(
        local_rows, columns_all
    )
    summed = summed_on_arrival(decoded.astype(jnp.bfloat16), REPLICA, 0)
    outer_grad = summed / replicas
    owner_index = lax.axis_index(REPLICA)
    base_owned = lax.dynamic_slice_in_dim(base_weights, owner_index * owned_rows, owned_rows, 0)
    grad_sq = over_axes(jnp.sum(outer_grad * outer_grad), REPLICA_FSDP)
    clip_factor = jnp.minimum(1.0, clip_rms / jnp.sqrt(grad_sq / (D * KVW) + epsilon))
    step_term = clip_factor * outer_grad
    new_momentum = outer_momentum * momentum + step_term
    owned_base = base_owned - outer_rate * (step_term + outer_momentum * new_momentum)
    new_base = gathered_copies(owned_base, REPLICA, 0)
    blended = blend_share * replica_copy.astype(jnp.float32) + (1.0 - blend_share) * new_base
    new_inner = blended.astype(jnp.bfloat16)
    return (new_base, new_momentum, new_inner[None])


def solution(mesh):
    torus = Mesh(
        mesh.devices.reshape(4, 4, 8, 2, 2),
        ("replica_0", "replica_1", "fsdp_0", "fsdp_1", "fsdp_2"),
    )
    placed = (P(FSDP, None), P(REPLICA, FSDP, None), P(FSDP_REPLICA, None))
    return jax.shard_map(
        shards,
        mesh=torus,
        in_specs=placed,
        out_specs=(P(FSDP, None), P(FSDP_REPLICA, None), P(REPLICA, FSDP, None)),
        check_vma=False,
    )
```

profile of v0, /device:TPU:8, one launch (start us, length us, event | category | flops | bytes accessed | tf_op | source)
XLA Modules:
  0.0 120.4 jit_solution(13715347763153442673)
XLA Ops:
  0.6 1.5 %abs_bitcast_fusion = f32[32,8,8,128]{3,1,2,0:T(8,128)S(1)} fusion(f32[256,1024]{1,0:T(8,128)} %param.3, bf16[1,256,1024]{2,1,0:T(8,128)(2,1)} %param.4), kind=kLoop, calls=%fused_computation.29 | loop fusion | flops 786432 | bytes 2621440
  2.1 0.2 copy.9
  2.4 0.3 reduce_max.9
  2.7 0.1 copy.7
  2.8 0.1 convert_divide_fusion
  2.8 0.1 copy.8
  3.0 0.3 div.71
  3.3 0.3 copy-done.1
  3.6 0.5 copy-done
  4.1 3.0 %fusion.13 = bf16[256,1024]{1,0:T(8,128)(2,1)} fusion(f32[32,8,8,128]{3,2,1,0:T(8,128)S(1)} %bitcast.28, f32[256,1024]{1,0:T(8,128)S(1)} %copy-done.1, bf16[1,256,1024]{2,1,0:T(8,128)(2,1)S(1)} %copy-done), kind=kLoop, calls=%fused_computation.22 | loop fusion | flops 13369344 | bytes 3145728 | tf_op jit(solution)/shard_map/convert_element_type | solution.py:102
  7.1 9.2 %all-to-all-start = ((bf16[16,16,1024]{2,1,0:T(8,128)(2,1)}), bf16[16,16,1024]{2,1,0:T(8,128)(2,1)S(1)}, u32[]{:S(2)}, u32[]{:S(2)}) async-start(bf16[16,16,1024]{2,1,0:T(8,128)(2,1)} %bitcast.1), calls=%async_computation | async-start | bytes 1048576 | tf_op jit(solution)/shard_map/all_to_all | solution.py:35
  16.3 13.4 %all-to-all-done = bf16[16,16,1024]{2,1,0:T(8,128)(2,1)S(1)} async-done(((bf16[16,16,1024]{2,1,0:T(8,128)(2,1)}), bf16[16,16,1024]{2,1,0:T(8,128)(2,1)S(1)}, u32[]{:S(2)}, u32[]{:S(2)}) %all-to-all-start) | async-done | bytes 524320 | tf_op jit(solution)/shard_map/all_to_all | solution.py:35
  29.8 0.1 convert_reduce_fusion
  29.8 0.6 multiply_reduce_fusion
  30.5 9.7 %psum.35 = f32[]{:T(128)} all-reduce(f32[]{:T(128)} %multiply_reduce_fusion), channel_id=1, replica_groups=mesh['replica_0'=4,'replica_1'=4,'fsdp_0'=8,'fsdp_1'=2,'fsdp_2'=2] {'rep..., use_global_device_ids=true, to_apply=%region_3.4 | all-reduce | flops 1 | bytes 8 | tf_op jit(solution)/shard_map/psum | solution.py:40
  40.1 9.6 %psum.36 = f32[]{:T(128)} all-reduce(f32[]{:T(128)} %psum.35), channel_id=1, replica_groups=mesh['replica_0'=4,'replica_1'=4,'fsdp_0'=8,'fsdp_1'=2,'fsdp_2'=2] {'rep..., use_global_device_ids=true, to_apply=%region_4.5 | all-reduce | flops 1 | bytes 8 | tf_op jit(solution)/shard_map/psum | solution.py:40
  49.7 23.7 %psum.37 = f32[]{:T(128)} all-reduce(f32[]{:T(128)} %psum.36), channel_id=1, replica_groups=mesh['replica_0'=4,'replica_1'=4,'fsdp_0'=8,'fsdp_1'=2,'fsdp_2'=2] {'fsd..., use_global_device_ids=true, to_apply=%region_5.6 | all-reduce | flops 1 | bytes 8 | tf_op jit(solution)/shard_map/psum | solution.py:40
  73.4 9.5 %psum.38 = f32[]{:T(128)} all-reduce(f32[]{:T(128)} %psum.37), channel_id=1, replica_groups=mesh['replica_0'=4,'replica_1'=4,'fsdp_0'=8,'fsdp_1'=2,'fsdp_2'=2] {'fsd..., use_global_device_ids=true, to_apply=%region_6.7 | all-reduce | flops 1 | bytes 8 | tf_op jit(solution)/shard_map/psum | solution.py:40
  82.9 3.1 %psum.39 = f32[]{:T(128)} all-reduce(f32[]{:T(128)} %psum.38), channel_id=1, replica_groups=mesh['replica_0'=4,'replica_1'=4,'fsdp_0'=8,'fsdp_1'=2,'fsdp_2'=2] {'fsd..., use_global_device_ids=true, to_apply=%region_7.8 | all-reduce | flops 1 | bytes 8 | tf_op jit(solution)/shard_map/psum | solution.py:40
  86.7 0.7 multiply_subtract_fusion
  87.3 0.1 broadcast_in_dim.2
  87.4 31.1 %all_to_all.10 = f32[16,16,1024]{2,1,0:T(8,128)S(1)} all-to-all(f32[16,16,1024]{2,1,0:T(8,128)S(1)} %broadcast_in_dim.2), channel_id=1, replica_groups=mesh['replica_0'=4,'replica_1'=4,'fsdp_0'=8,'fsdp_1'=2,'fsdp_2'=2] {'rep..., dimensions={0} | all-to-all | bytes 2097152 | tf_op jit(solution)/shard_map/all_to_all | solution.py:45
  118.5 0.9 fusion.2
  119.5 1.0 copy.13
  (4 shorter events, 0.0 us)
Async XLA Ops:
  2.3 1.2 %copy-start.1 = (f32[256,1024]{1,0:T(8,128)S(1)}, f32[256,1024]{1,0:T(8,128)}, u32[]{:S(2)}) copy-start(f32[256,1024]{1,0:T(8,128)} %param.3) | copy-start | bytes 3145732
  3.0 1.1 copy-start
  7.1 22.6 %all-to-all-start = ((bf16[16,16,1024]{2,1,0:T(8,128)(2,1)}), bf16[16,16,1024]{2,1,0:T(8,128)(2,1)S(1)}, u32[]{:S(2)}, u32[]{:S(2)}) async-start(bf16[16,16,1024]{2,1,0:T(8,128)(2,1)} %bitcast.1), calls=%async_computation | async-start | bytes 1048576 | tf_op jit(solution)/shard_map/all_to_all | solution.py:35
  29.8 56.8 %copy-start.2 = (f32[16,1024]{1,0:T(8,128)S(1)}, f32[16,1024]{1,0:T(8,128)}, u32[]{:S(2)}) copy-start(f32[16,1024]{1,0:T(8,128)} %param.5) | copy-start | bytes 196612
where the time goes:
time: 121 us; the launch traced here: 120 us
  blocking collectives  86.6 us (72%)
  waiting for transfers between devices  13.4 us (11%)
  starting transfers between devices  9.21 us (8%)
  other arithmetic  7.23 us (6%)
  local copies, waits for them, and re-layouts  2.59 us (2%)
  between operations  1.41 us (1%)
    psum x5, blocking collectives, over_axes(): return functools.reduce(lax.psum, axes, value)  55.5 us
    all_to_all x1, blocking collectives, from_everyone(): return lax.all_to_all(copies, axis, split_axis=0, concat_axis=0, tiled=True)  31.1 us
    all_to_all x1, waiting for transfers between devices, summed_on_arrival(): lax.all_to_all(blocks, axis, split_axis=0, concat_axis=0, tiled=True)  13.4 us
    all_to_all x1, starting transfers between devices, summed_on_arrival(): lax.all_to_all(blocks, axis, split_axis=0, concat_axis=0, tiled=True)  9.21 us
    convert_element_type x1, other arithmetic, shards(): summed = summed_on_arrival(decoded.astype(jnp.bfloat16), REPLICA, 0)  3.03 us
  transfers between devices with their start and end apart: 1, of which 1 were waited for; matrix products, arithmetic and copies ran while one was open for 0% of the time, Pallas kernels for 0%

commit v1 on v0

v1 whole, which is shorter than its diff:
```python
import jax
import jax.numpy as jnp
from jax import lax
from jax.experimental import pallas as pl
from jax.experimental.pallas import tpu as pltpu
from jax.sharding import Mesh
from jax.sharding import PartitionSpec as P

D = 8192
KVW = 1024
BLOCK = 128
REPLICA = ("replica_0", "replica_1")
FSDP = ("fsdp_0", "fsdp_1", "fsdp_2")
FSDP_REPLICA = ("fsdp_0", "fsdp_1", "fsdp_2", "replica_0", "replica_1")
PLANE = ("replica_1", "fsdp_0")
RING = ("fsdp_1", "replica_0", "fsdp_2")

code_limit = 448.0
outer_rate = 0.7
outer_momentum = 0.9
blend_share = 0.5
clip_rms = 0.02
epsilon = 1e-06
smallest_normal = 0.015625

step_unit = 1024.0


def exchanged(blocks, axis):
    return lax.all_to_all(blocks, axis, split_axis=0, concat_axis=0, tiled=True)


def to_everyone(value, axis):
    copies = jnp.broadcast_to(value, (lax.axis_size(axis), *value.shape))
    return exchanged(copies, axis)


def smallest_scale(peaks):
    target = peaks * (1.0 / code_limit)
    spread = target * (2.0**23 + 1.0)
    scale = spread - (spread - target)
    scale = jnp.where(code_limit * scale < peaks, 2.0 * scale, scale)
    return jnp.where(code_limit * (0.5 * scale) >= peaks, 0.5 * scale, scale)


def encode_kernel(base_ref, inner_ref, decoded_ref):
    for at in range(0, base_ref.shape[1], BLOCK):
        columns = pl.ds(at, BLOCK)
        deltas = base_ref[:, columns] - inner_ref[:, columns].astype(jnp.float32)
        magnitude = jnp.abs(deltas)
        scale = smallest_scale(jnp.max(magnitude, axis=1, keepdims=True) + epsilon)
        beyond = deltas * (1.0 + 2.0**-23)
        spread = beyond * (2.0**20 + 1.0)
        normal = spread - (spread - beyond)
        anchor = scale * (1.5 * 2.0**14)
        small = (beyond + anchor) - anchor
        decoded = jnp.where(magnitude < scale * smallest_normal, small, normal)
        decoded_ref[:, columns] = decoded.astype(decoded_ref.dtype)


def decoded_deltas(base_weights, replica_copy):
    rows, columns = base_weights.shape
    tall = 64
    spec = pl.BlockSpec((tall, columns), lambda i: (i, 0))
    return pl.pallas_call(
        encode_kernel,
        grid=(rows // tall,),
        in_specs=[spec, spec],
        out_specs=spec,
        out_shape=jax.ShapeDtypeStruct((rows, columns), jnp.bfloat16),
        cost_estimate=pl.CostEstimate(
            flops=20 * rows * columns, bytes_accessed=8 * rows * columns, transcendentals=0
        ),
    )(base_weights, replica_copy)


def partial_squares(value):
    rows, columns = value.shape
    tiles = (value * value).reshape(rows // 8, 8, columns // 128, 128)
    return tiles.sum(axis=(0, 2))


def shards(base_weights, inner_weights, momentum):
    replicas = lax.axis_size(REPLICA)
    local_rows, columns = base_weights.shape
    owned_rows = local_rows // replicas
    replica_copy = inner_weights[0]
    decoded = decoded_deltas(base_weights, replica_copy)
    arrived = exchanged(decoded.reshape(replicas, owned_rows, columns), REPLICA)
    outer_grad = arrived.astype(jnp.float32).sum(axis=0) / replicas
    squares = to_everyone(partial_squares(outer_grad), PLANE).sum(axis=0)
    grad_sq = to_everyone(squares, RING).sum()
    clip_factor = jnp.minimum(1.0, clip_rms / jnp.sqrt(grad_sq / (D * KVW) + epsilon))
    step_term = clip_factor * outer_grad
    new_momentum = outer_momentum * momentum + step_term
    step = outer_rate * (step_term + outer_momentum * new_momentum)
    steps = to_everyone((step * step_unit).astype(jnp.float16), REPLICA)
    steps = steps.reshape(local_rows, columns).astype(jnp.float32) * (1.0 / step_unit)
    new_base = base_weights - steps
    blended = blend_share * replica_copy.astype(jnp.float32) + (1.0 - blend_share) * new_base
    return (new_base, new_momentum, blended.astype(jnp.bfloat16)[None])


def solution(mesh):
    torus = Mesh(
        mesh.devices.reshape(4, 4, 8, 2, 2),
        ("replica_0", "replica_1", "fsdp_0", "fsdp_1", "fsdp_2"),
    )
    return jax.shard_map(
        shards,
        mesh=torus,
        in_specs=(P(FSDP, None), P(REPLICA, FSDP, None), P(FSDP_REPLICA, None)),
        out_specs=(P(FSDP, None), P(FSDP_REPLICA, None), P(REPLICA, FSDP, None)),
        check_vma=False,
    )
```

time: 121 us -> 85.5 us (0.71)
  waiting for transfers between devices: 13.4 us -> 0 us
  blocking collectives: 86.6 us -> 75.8 us
  starting transfers between devices: 9.21 us -> 0 us
  other arithmetic: 7.23 us -> 2.93 us
  Pallas kernels: 0 us -> 3.9 us
  local copies, waits for them, and re-layouts: 2.59 us -> 0.98 us
    psum x5 -> x0, blocking collectives: 55.5 us -> none  [over_axes(): return functools.reduce(lax.psum, axes, value)]
    all_to_all x1 -> x4, blocking collectives: 31.1 us -> 75.8 us  [exchanged(): return lax.all_to_all(blocks, axis, split_axis=0, concat_axis=0, tiled=True)]
    all_to_all x1 -> x0, waiting for transfers between devices: 13.4 us -> none  [summed_on_arrival(): lax.all_to_all(blocks, axis, split_axis=0, concat_axis=0, tiled=True)]
    all_to_all x1 -> x0, starting transfers between devices: 9.21 us -> none  [summed_on_arrival(): lax.all_to_all(blocks, axis, split_axis=0, concat_axis=0, tiled=True)]
    pallas_call x0 -> x1, Pallas kernels: none -> 3.9 us  [decoded_deltas(): pl.pallas_call(encode_kernel, grid=(rows // tall,), in_specs=[spec, spec]...]
    convert_element_type x2 -> x1, other arithmetic: 3.98 us -> 0.65 us  [shards(): steps = to_everyone((step * step_unit).astype(jnp.float16), REPLICA)]
    unnamed x1 -> x0, other arithmetic: 1.5 us -> none
    broadcast_in_dim x0 -> x1, other arithmetic: none -> 1.41 us  [shards(): return (new_base, new_momentum, blended.astype(jnp.bfloat16)[None])]
  transfers between devices with their start and end apart: 1 -> 0, of which waited for: 1 -> 0; matrix products, arithmetic and copies ran while one was open for 0% -> 0% of each run, Pallas kernels for 0% -> 0%
where the time goes in v1:
time: 85.5 us; the launch traced here: 85 us
  blocking collectives  75.8 us (89%)
  Pallas kernels  3.9 us (5%)
  other arithmetic  2.93 us (3%)
  between operations  1.38 us (2%)
  local copies, waits for them, and re-layouts  0.98 us (1%)
    all_to_all x4, blocking collectives, exchanged(): return lax.all_to_all(blocks, axis, split_axis=0, concat_axis=0, tiled=True)  75.8 us
    pallas_call x1, Pallas kernels, decoded_deltas(): pl.pallas_call(encode_kernel, grid=(rows // tall,), in_specs=[spec, spec]...  3.9 us

profile of v1, /device:TPU:8, one launch (start us, length us, event | category | flops | bytes accessed | tf_op | source)
XLA Modules:
  0.0 85.0 jit_solution(13104382788489277778)
XLA Ops:
  0.6 3.9 %shard_map.58 = bf16[256,1024]{1,0:T(8,128)(2,1)} custom-call(f32[256,1024]{1,0:T(8,128)} %base_ref.1, bf16[256,1024]{1,0:T(8,128)(2,1)} %bitcast.11), custom_call_target="tpu_custom_call" | custom-call | flops 5242880 | bytes 2097152 | tf_op jit(solution)/shard_map/pallas_call | solution.py:65
  4.5 22.6 %all_to_all.20 = bf16[16,16,1024]{2,1,0:T(8,128)(2,1)S(1)} all-to-all(bf16[16,16,1024]{2,1,0:T(8,128)(2,1)} %bitcast.10), channel_id=1, replica_groups=mesh['replica_0'=4,'replica_1'=4,'fsdp_0'=8,'fsdp_1'=2,'fsdp_2'=2] {'rep..., dimensions={0} | all-to-all | bytes 1048576 | tf_op jit(solution)/shard_map/all_to_all | solution.py:30
  27.2 0.1 convert_reduce_fusion
  27.3 22.1 %all_to_all.21 = f32[32,8,128]{2,1,0:T(8,128)S(1)} all-to-all(f32[32,8,128]{2,1,0:T(8,128)S(1)} %broadcast_in_dim.12), channel_id=1, replica_groups=mesh['replica_0'=4,'replica_1'=4,'fsdp_0'=8,'fsdp_1'=2,'fsdp_2'=2] {'rep..., dimensions={0} | all-to-all | bytes 262144 | tf_op jit(solution)/shard_map/all_to_all | solution.py:30
  49.4 11.5 %all_to_all.22 = f32[16,8,128]{2,1,0:T(8,128)S(1)} all-to-all(f32[16,8,128]{2,1,0:T(8,128)S(1)} %broadcast_in_dim.13), channel_id=1, replica_groups=mesh['replica_0'=4,'replica_1'=4,'fsdp_0'=8,'fsdp_1'=2,'fsdp_2'=2] {'fsd..., dimensions={0} | all-to-all | bytes 131072 | tf_op jit(solution)/shard_map/all_to_all | solution.py:30
  60.9 0.0 copy-start.2
  60.9 0.6 reduce_sum.39
  62.2 0.0 copy-done.2
  62.2 0.6 multiply_convert_fusion.1
  62.8 0.1 broadcast_in_dim.14
  62.9 0.0 copy-start
  62.9 19.6 %all_to_all.23 = f16[16,16,1024]{2,1,0:T(8,128)(2,1)S(1)} all-to-all(f16[16,16,1024]{2,1,0:T(8,128)(2,1)S(1)} %broadcast_in_dim.14), channel_id=1, replica_groups=mesh['replica_0'=4,'replica_1'=4,'fsdp_0'=8,'fsdp_1'=2,'fsdp_2'=2] {'rep..., dimensions={0} | all-to-all | bytes 1048576 | tf_op jit(solution)/shard_map/all_to_all | solution.py:30
  82.6 0.0 copy-start.1
  82.6 0.1 convert_multiply_fusion
  82.7 0.0 copy-done
  82.7 0.9 %copy-done.1 = bf16[1,256,1024]{2,1,0:T(8,128)(2,1)S(1)} copy-done((bf16[1,256,1024]{2,1,0:T(8,128)(2,1)S(1)}, bf16[1,256,1024]{2,1,0:T(8,128)(2,1)}, u32[]{:S(2)}) %copy-start.1) | copy-done | bytes 524312
  83.6 1.4 %fusion = (bf16[1,256,1024]{2,1,0:T(8,128)(2,1)}, f32[256,1024]{1,0:T(8,128)}) fusion(bf16[1,256,1024]{2,1,0:T(8,128)(2,1)S(1)} %copy-done.1, f32[256,1024]{1,0:T(8,128)S(1)} %copy-done, f32[16,16,1024]{2,1,0:T(8,128)S(1)} %convert_multiply_fusion), kind=kLoop, calls=%fused_computation.4 | loop fusion | flops 1310720 | bytes 4194304 | tf_op jit(solution)/shard_map/broadcast_in_dim | solution.py:101
  (4 shorter events, 0.1 us)
Async XLA Ops:
  60.9 1.3 %copy-start.2 = (f32[16,1024]{1,0:T(8,128)S(1)}, f32[16,1024]{1,0:T(8,128)}, u32[]{:S(2)}) copy-start(f32[16,1024]{1,0:T(8,128)} %param.5) | copy-start | bytes 196612
  62.9 19.8 %copy-start = (f32[256,1024]{1,0:T(8,128)S(1)}, f32[256,1024]{1,0:T(8,128)}, u32[]{:S(2)}) copy-start(f32[256,1024]{1,0:T(8,128)} %base_ref.1) | copy-start | bytes 3145732
  82.6 1.0 %copy-start.1 = (bf16[1,256,1024]{2,1,0:T(8,128)(2,1)S(1)}, bf16[1,256,1024]{2,1,0:T(8,128)(2,1)}, u32[]{:S(2)}) copy-start(bf16[1,256,1024]{2,1,0:T(8,128)(2,1)} %param.4) | copy-start | bytes 1572868

commit v2 on v1

--- a/solution.py
+++ b/solution.py
@@ -12,9 +12,6 @@
 REPLICA = ("replica_0", "replica_1")
 FSDP = ("fsdp_0", "fsdp_1", "fsdp_2")
 FSDP_REPLICA = ("fsdp_0", "fsdp_1", "fsdp_2", "replica_0", "replica_1")
-PLANE = ("replica_1", "fsdp_0")
-RING = ("fsdp_1", "replica_0", "fsdp_2")
-
 code_limit = 448.0
 outer_rate = 0.7
 outer_momentum = 0.9
@@ -23,7 +20,8 @@
 epsilon = 1e-06
 smallest_normal = 0.015625
 
-step_unit = 1024.0
+grad_unit = 2048.0
+momentum_unit = 32768.0
 
 
 def exchanged(blocks, axis):
@@ -80,23 +78,52 @@
     return tiles.sum(axis=(0, 2))
 
 
+def in_half(value, unit):
+    return (value.astype(jnp.float32) * unit).astype(jnp.float16)
+
+
+def from_half(value, unit):
+    return value.astype(jnp.float32) * (1.0 / unit)
+
+
 def shards(base_weights, inner_weights, momentum):
     replicas = lax.axis_size(REPLICA)
+    lines, line = lax.axis_size(REPLICA[0]), lax.axis_size(REPLICA[1])
     local_rows, columns = base_weights.shape
     owned_rows = local_rows // replicas
+    share = columns // line
     replica_copy = inner_weights[0]
+
     decoded = decoded_deltas(base_weights, replica_copy)
-    arrived = exchanged(decoded.reshape(replicas, owned_rows, columns), REPLICA)
-    outer_grad = arrived.astype(jnp.float32).sum(axis=0) / replicas
-    squares = to_everyone(partial_squares(outer_grad), PLANE).sum(axis=0)
-    grad_sq = to_everyone(squares, RING).sum()
+    quarters = jnp.moveaxis(in_half(momentum, momentum_unit).reshape(owned_rows, line, share), 1, 0)
+    quarters = jnp.broadcast_to(quarters, (lines, line, owned_rows, share))
+    sent = jnp.concatenate(
+        [
+            in_half(decoded, grad_unit).reshape(replicas, owned_rows, columns),
+            quarters.reshape(replicas, owned_rows, share),
+        ],
+        axis=2,
+    )
+    arrived = exchanged(sent, REPLICA)
+    outer_grad = arrived[:, :, :columns].astype(jnp.float32).sum(axis=0) * (
+        1.0 / (grad_unit * replicas)
+    )
+    quarter = from_half(arrived[:, :, columns:], momentum_unit).reshape(local_rows, share)
+    all_quarters = lax.all_gather(quarter, REPLICA[1], axis=0, tiled=False)
+
+    grads = to_everyone(in_half(outer_grad, grad_unit), REPLICA).reshape(local_rows, columns)
+    squares = partial_squares(from_half(grads, grad_unit))
+    all_squares = to_everyone(squares, FSDP)
+    all_momentum = jnp.moveaxis(all_quarters, 0, 1).reshape(local_rows, columns)
+    start = lax.optimization_barrier(
+        base_weights - (outer_rate * outer_momentum * outer_momentum) * all_momentum
+    )
+
+    grad_sq = all_squares.sum()
     clip_factor = jnp.minimum(1.0, clip_rms / jnp.sqrt(grad_sq / (D * KVW) + epsilon))
-    step_term = clip_factor * outer_grad
-    new_momentum = outer_momentum * momentum + step_term
-    step = outer_rate * (step_term + outer_momentum * new_momentum)
-    steps = to_everyone((step * step_unit).astype(jnp.float16), REPLICA)
-    steps = steps.reshape(local_rows, columns).astype(jnp.float32) * (1.0 / step_unit)
-    new_base = base_weights - steps
+    new_momentum = outer_momentum * momentum + clip_factor * outer_grad
+    rate = (outer_rate * (1.0 + outer_momentum) / grad_unit) * clip_factor
+    new_base = start - rate * grads.astype(jnp.float32)
     blended = blend_share * replica_copy.astype(jnp.float32) + (1.0 - blend_share) * new_base
     return (new_base, new_momentum, blended.astype(jnp.bfloat16)[None])
 

time: 85.5 us -> 102 us (1.19)
  blocking collectives: 75.8 us -> 52.8 us
  between operations: 1.38 us -> 14.8 us
  waiting for transfers between devices: 0 us -> 13.4 us
  starting transfers between devices: 0 us -> 5.17 us
  other arithmetic: 2.93 us -> 7.69 us
  local copies, waits for them, and re-layouts: 0.98 us -> 3.02 us
    all_to_all x4 -> x2, blocking collectives: 75.8 us -> 52.8 us  [exchanged(): return lax.all_to_all(blocks, axis, split_axis=0, concat_axis=0, tiled=True)]
    all_to_all x0 -> x1, waiting for transfers between devices: none -> 13.3 us  [exchanged(): return lax.all_to_all(blocks, axis, split_axis=0, concat_axis=0, tiled=True)]
    all_to_all x0 -> x1, starting transfers between devices: none -> 5.14 us  [exchanged(): return lax.all_to_all(blocks, axis, split_axis=0, concat_axis=0, tiled=True)]
    convert_element_type x1 -> x3, other arithmetic: 0.65 us -> 2.02 us  [in_half(): return (value.astype(jnp.float32) * unit).astype(jnp.float16)]
    unnamed x0 -> x1, other arithmetic: none -> 1.33 us
    unnamed x6, local copies, waits for them, and re-layouts: 0.91 us -> 1.97 us
  transfers between devices with their start and end apart: 0 -> 2, of which waited for: 0 -> 1; matrix products, arithmetic and copies ran while one was open for 0% -> 3% of each run, Pallas kernels for 0% -> 0%
where the time goes in v2:
time: 102 us; the launch traced here: 101 us
  blocking collectives  52.8 us (52%)
  between operations  14.8 us (15%)
  waiting for transfers between devices  13.4 us (13%)
  other arithmetic  7.69 us (8%)
  starting transfers between devices  5.17 us (5%)
  Pallas kernels  3.91 us (4%)
  local copies, waits for them, and re-layouts  3.02 us (3%)
    all_to_all x2, blocking collectives, exchanged(): return lax.all_to_all(blocks, axis, split_axis=0, concat_axis=0, tiled=True)  52.8 us
    all_to_all x1, waiting for transfers between devices, exchanged(): return lax.all_to_all(blocks, axis, split_axis=0, concat_axis=0, tiled=True)  13.3 us
    all_to_all x1, starting transfers between devices, exchanged(): return lax.all_to_all(blocks, axis, split_axis=0, concat_axis=0, tiled=True)  5.14 us
    pallas_call x1, Pallas kernels, decoded_deltas(): pl.pallas_call(encode_kernel, grid=(rows // tall,), in_specs=[spec, spec]...  3.91 us
  transfers between devices with their start and end apart: 2, of which 1 were waited for; matrix products, arithmetic and copies ran while one was open for 3% of the time, Pallas kernels for 0%

profile of v2, /device:TPU:8, one launch (start us, length us, event | category | flops | bytes accessed | tf_op | source)
XLA Modules:
  0.0 100.8 jit_solution(8860248417527727287)
XLA Ops:
  7.2 0.9 multiply_convert_fusion.3
  8.1 3.9 %shard_map.58 = bf16[256,1024]{1,0:T(8,128)(2,1)} custom-call(f32[256,1024]{1,0:T(8,128)} %base_ref.1, bf16[256,1024]{1,0:T(8,128)(2,1)} %bitcast.19), custom_call_target="tpu_custom_call" | custom-call | flops 5242880 | bytes 2097152 | tf_op jit(solution)/shard_map/pallas_call | solution.py:63
  12.0 1.2 %multiply_convert_fusion.1 = f16[256,1024]{1,0:T(8,128)(2,1)S(1)} fusion(bf16[256,1024]{1,0:T(8,128)(2,1)} %shard_map.58), kind=kLoop, calls=%fused_computation.7 | loop fusion | flops 786432 | bytes 1048576 | tf_op jit(solution)/shard_map/convert_element_type | solution.py:82
  13.2 0.2 pad_maximum_fusion
  13.3 25.5 %all_to_all.15 = f16[16,16,1280]{2,1,0:T(8,128)(2,1)S(1)} all-to-all(f16[16,16,1280]{2,1,0:T(8,128)(2,1)S(1)} %pad_maximum_fusion), channel_id=1, replica_groups=mesh['replica_0'=4,'replica_1'=4,'fsdp_0'=8,'fsdp_1'=2,'fsdp_2'=2] {'rep..., dimensions={0} | all-to-all | bytes 1310720 | tf_op jit(solution)/shard_map/all_to_all | solution.py:28
  38.8 0.1 convert_reduce_fusion
  38.9 0.9 broadcast_in_dim.13
  39.8 5.1 %all-to-all-start.1 = ((f16[16,16,1024]{2,1,0:T(8,128)(2,1)}), f16[16,16,1024]{2,1,0:T(8,128)(2,1)S(1)}, u32[]{:S(2)}, u32[]{:S(2)}) async-start(f16[16,16,1024]{2,1,0:T(8,128)(2,1)} %broadcast_in_dim.13), calls=%async_computation.1 | async-start | bytes 1048576 | tf_op jit(solution)/shard_map/all_to_all | solution.py:28
  44.9 0.0 all-gather.2.cloned.1.call-start
  45.0 0.7 convert_multiply_fusion.2
  45.7 13.3 %all-to-all-done.1 = f16[16,16,1024]{2,1,0:T(8,128)(2,1)S(1)} async-done(((f16[16,16,1024]{2,1,0:T(8,128)(2,1)}), f16[16,16,1024]{2,1,0:T(8,128)(2,1)S(1)}, u32[]{:S(2)}, u32[]{:S(2)}) %all-to-all-start.1) | async-done | bytes 524320 | tf_op jit(solution)/shard_map/all_to_all | solution.py:28
  59.1 0.1 fusion
  59.2 0.3 reduce_sum.28
  59.5 27.3 %all_to_all.16 = f32[32,8,128]{2,1,0:T(8,128)S(1)} all-to-all(f32[32,8,128]{2,1,0:T(8,128)S(1)} %broadcast_in_dim.14), channel_id=1, replica_groups=mesh['replica_0'=4,'replica_1'=4,'fsdp_0'=8,'fsdp_1'=2,'fsdp_2'=2] {'fsd..., dimensions={0} | all-to-all | bytes 262144 | tf_op jit(solution)/shard_map/all_to_all | solution.py:28
  86.8 0.6 reduce_sum.29
  88.1 0.6 multiply_add_fusion
  88.8 0.1 convert_multiply_fusion
  88.9 0.0 all-gather.2.cloned.1.call-done
  88.9 1.3 %multiply_bitcast_fusion = f32[4,32,8,256]{3,2,1,0:T(8,128)S(1)} fusion(f32[4,256,256]{2,1,0:T(8,128)} %all-gather.2.cloned.1.call-done), kind=kLoop, calls=%fused_computation.6 | loop fusion | flops 262144 | bytes 2097152
  90.3 0.1 copy.11
  90.4 1.1 %copy-done = f32[256,1024]{1,0:T(8,128)S(1)} copy-done((f32[256,1024]{1,0:T(8,128)S(1)}, f32[256,1024]{1,0:T(8,128)}, u32[]{:S(2)}) %copy-start) | copy-done | bytes 1048600
  91.5 0.2 sub.6
  91.7 0.9 copy-done.1
  92.5 1.4 %fusion.1 = (bf16[1,256,1024]{2,1,0:T(8,128)(2,1)}, f32[256,1024]{1,0:T(8,128)}) fusion(bf16[1,256,1024]{2,1,0:T(8,128)(2,1)S(1)} %copy-done.1, f32[256,1024]{1,0:T(8,128)S(1)} %sub.6, f32[16,16,1024]{2,1,0:T(8,128)S(1)} %convert_multiply_fusion), kind=kLoop, calls=%fused_computation.9 | loop fusion | flops 1310720 | bytes 4194304 | tf_op jit(solution)/shard_map/broadcast_in_dim | solution.py:128
  (10 shorter events, 0.1 us)
Async XLA Ops:
  39.8 19.3 %all-to-all-start.1 = ((f16[16,16,1024]{2,1,0:T(8,128)(2,1)}), f16[16,16,1024]{2,1,0:T(8,128)(2,1)S(1)}, u32[]{:S(2)}, u32[]{:S(2)}) async-start(f16[16,16,1024]{2,1,0:T(8,128)(2,1)} %broadcast_in_dim.13), calls=%async_computation.1 | async-start | bytes 1048576 | tf_op jit(solution)/shard_map/all_to_all | solution.py:28
  44.9 44.0 %all-gather.2.cloned.1.call-start = ((), (), s32[]{:S(2)}) async-start(), calls=%async_computation.3 | async-start | bytes 1310720 | tf_op jit(solution)/shard_map/all_gather | solution.py:112
  86.8 1.3 %copy-start.2 = (f32[16,1024]{1,0:T(8,128)S(1)}, f32[16,1024]{1,0:T(8,128)}, u32[]{:S(2)}) copy-start(f32[16,1024]{1,0:T(8,128)} %param.5) | copy-start | bytes 196612
  90.3 1.2 %copy-start = (f32[256,1024]{1,0:T(8,128)S(1)}, f32[256,1024]{1,0:T(8,128)}, u32[]{:S(2)}) copy-start(f32[256,1024]{1,0:T(8,128)} %base_ref.1) | copy-start | bytes 3145732
  91.5 1.0 %copy-start.1 = (bf16[1,256,1024]{2,1,0:T(8,128)(2,1)S(1)}, bf16[1,256,1024]{2,1,0:T(8,128)(2,1)}, u32[]{:S(2)}) copy-start(bf16[1,256,1024]{2,1,0:T(8,128)(2,1)} %param.4) | copy-start | bytes 1572868
Sparse Core Ops, SparseCore 0:
  48.4 31.2 all-gather.1

commit v3 on v1

--- a/solution.py
+++ b/solution.py
@@ -14,7 +14,6 @@
 FSDP_REPLICA = ("fsdp_0", "fsdp_1", "fsdp_2", "replica_0", "replica_1")
 PLANE = ("replica_1", "fsdp_0")
 RING = ("fsdp_1", "replica_0", "fsdp_2")
-
 code_limit = 448.0
 outer_rate = 0.7
 outer_momentum = 0.9
@@ -23,7 +22,8 @@
 epsilon = 1e-06
 smallest_normal = 0.015625
 
-step_unit = 1024.0
+grad_unit = 2048.0
+momentum_unit = 32768.0
 
 
 def exchanged(blocks, axis):
@@ -80,23 +80,70 @@
     return tiles.sum(axis=(0, 2))
 
 
+def in_half(value, unit):
+    return (value.astype(jnp.float32) * unit).astype(jnp.float16)
+
+
+def from_half(value, unit):
+    return value.astype(jnp.float32) * (1.0 / unit)
+
+
+def swapped(value, axis, bit):
+    return lax.ppermute(value, axis, [(i, i ^ bit) for i in range(lax.axis_size(axis))])
+
+
+def gathered(value, axis):
+    place = lax.axis_index(axis)
+    upper, odd = place >= 2, (place & 1) == 1
+    other = swapped(value, axis, 2)
+    halves = jnp.stack([jnp.where(upper, other, value), jnp.where(upper, value, other)])
+    other = swapped(halves, axis, 1)
+    evens, odds = jnp.where(odd, other, halves), jnp.where(odd, halves, other)
+    return jnp.stack([evens[0], odds[0], evens[1], odds[1]])
+
+
+def beside(task, value):
+    shape = jax.eval_shape(task, value)
+    held = value.reshape(-1)[0].astype(jnp.float32) < 1e30
+    return lax.cond(held, task, lambda v: jnp.zeros(shape.shape, shape.dtype), value)
+
+
+def in_rows(blocks):
+    return jnp.swapaxes(blocks, 0, 1).reshape(-1, blocks.shape[-1])
+
+
 def shards(base_weights, inner_weights, momentum):
     replicas = lax.axis_size(REPLICA)
     local_rows, columns = base_weights.shape
     owned_rows = local_rows // replicas
     replica_copy = inner_weights[0]
-    decoded = decoded_deltas(base_weights, replica_copy)
+    together = lax.optimization_barrier
+
+    decoded, momenta = together(
+        (decoded_deltas(base_weights, replica_copy), in_half(momentum, momentum_unit))
+    )
     arrived = exchanged(decoded.reshape(replicas, owned_rows, columns), REPLICA)
+    momenta = beside(lambda v: gathered(gathered(v, REPLICA[0]), REPLICA[1]), momenta)
+    arrived, momenta = together((arrived, momenta))
     outer_grad = arrived.astype(jnp.float32).sum(axis=0) / replicas
-    squares = to_everyone(partial_squares(outer_grad), PLANE).sum(axis=0)
-    grad_sq = to_everyone(squares, RING).sum()
+
+    squares, grads = together((partial_squares(outer_grad), in_half(outer_grad, grad_unit)))
+    squares = to_everyone(squares, PLANE)
+    grads = beside(lambda v: gathered(v, REPLICA[0]), grads)
+    squares, grads = together((squares, grads))
+    squares, grads = together((squares.sum(axis=0), grads))
+    squares = to_everyone(squares, RING)
+    grads = beside(lambda v: gathered(v, REPLICA[1]), grads)
+    squares, grads = together((squares, grads))
+
+    grad_sq = squares.sum()
     clip_factor = jnp.minimum(1.0, clip_rms / jnp.sqrt(grad_sq / (D * KVW) + epsilon))
-    step_term = clip_factor * outer_grad
-    new_momentum = outer_momentum * momentum + step_term
-    step = outer_rate * (step_term + outer_momentum * new_momentum)
-    steps = to_everyone((step * step_unit).astype(jnp.float16), REPLICA)
-    steps = steps.reshape(local_rows, columns).astype(jnp.float32) * (1.0 / step_unit)
-    new_base = base_weights - steps
+    new_momentum = outer_momentum * momentum + clip_factor * outer_grad
+    start = base_weights - (
+        outer_rate * outer_momentum * outer_momentum / momentum_unit
+    ) * in_rows(momenta).astype(jnp.float32)
+    rate = (outer_rate * (1.0 + outer_momentum) / grad_unit) * clip_factor
+    new_base = start - rate * in_rows(grads).astype(jnp.float32)
     blended = blend_share * replica_copy.astype(jnp.float32) + (1.0 - blend_share) * new_base
     return (new_base, new_momentum, blended.astype(jnp.bfloat16)[None])
 

time: 85.5 us -> 113 us (1.32)
  the two profiles are of different devices: /device:TPU:8 before, /device:TPU:2 now
where the time goes in v3:
time: 113 us; the launch traced here: 112 us
  starting transfers between devices  50.2 us (44%)
  waiting for transfers between devices  44.4 us (39%)
  other arithmetic  5.16 us (5%)
  local copies, waits for them, and re-layouts  4.57 us (4%)
  Pallas kernels  3.9 us (3%)
  between operations  3.46 us (3%)
    ppermute x8, waiting for transfers between devices, swapped(): lax.ppermute(value, axis, [(i, i ^ bit) for i in range(lax.axis_size(axis...  44.4 us
    all_to_all x3, starting transfers between devices, exchanged(): return lax.all_to_all(blocks, axis, split_axis=0, concat_axis=0, tiled=True)  27.2 us
    ppermute x8, starting transfers between devices, swapped(): lax.ppermute(value, axis, [(i, i ^ bit) for i in range(lax.axis_size(axis...  23 us
    pallas_call x1, Pallas kernels, decoded_deltas(): pl.pallas_call(encode_kernel, grid=(rows // tall,), in_specs=[spec, spec]...  3.9 us
  transfers between devices with their start and end apart: 11, of which 8 were waited for; matrix products, arithmetic and copies ran while one was open for 3% of the time, Pallas kernels for 0%

profile of v3, /device:TPU:2, one launch (start us, length us, event | category | flops | bytes accessed | tf_op | source)
XLA Modules:
  0.0 111.9 jit_solution(379233414910565673)
XLA Ops:
  1.5 3.9 %shard_map.58 = bf16[256,1024]{1,0:T(8,128)(2,1)} custom-call(f32[256,1024]{1,0:T(8,128)} %base_ref.1, bf16[256,1024]{1,0:T(8,128)(2,1)} %bitcast.44), custom_call_target="tpu_custom_call" | custom-call | flops 5242880 | bytes 2097152 | tf_op jit(solution)/shard_map/pallas_call | solution.py:65
  5.4 9.3 %all-to-all-start = ((bf16[16,16,1024]{2,1,0:T(8,128)(2,1)}), bf16[16,16,1024]{2,1,0:T(8,128)(2,1)S(1)}, u32[]{:S(2)}, u32[]{:S(2)}) async-start(bf16[16,16,1024]{2,1,0:T(8,128)(2,1)} %bitcast.45), calls=%async_computation | async-start | bytes 1048576 | tf_op jit(solution)/shard_map/all_to_all | solution.py:30
  15.8 36.4 %conditional.3 = (f16[4,4,16,1024]{3,2,1,0:T(8,128)(2,1)S(1)}) conditional(s32[]{:T(128)} %bitcast.10, () %tuple.33, f16[16,1024]{1,0:T(8,128)(2,1)S(1)} %multiply_convert_fusion.2), branch_computations={%region_0.0_spmd, %region_1.2_spmd} | conditional | flops 1998860 | bytes 7209256 | solution.py:108
  15.9 4.3 %collective-permute-start = (f16[16,1024]{1,0:T(8,128)(2,1)S(1)}, f16[16,1024]{1,0:T(8,128)(2,1)S(1)}, u32[]{:S(2)}, u32[]{:S(2)}) collective-permute-start(f16[16,1024]{1,0:T(8,128)(2,1)S(1)} %param.1), channel_id=1, source_target_pairs={{0,256},{128,384},{256,0},{384,128},{1,257},{129,385},{257,1},{385... | collective-permute-start | bytes 98312 | tf_op jit(solution)/shard_map/cond/branch_1_fun/ppermute | solution.py:92
  20.2 8.4 %collective-permute-done = f16[16,1024]{1,0:T(8,128)(2,1)S(1)} collective-permute-done((f16[16,1024]{1,0:T(8,128)(2,1)S(1)}, f16[16,1024]{1,0:T(8,128)(2,1)S(1)}, u32[]{:S(2)}, u32[]{:S(2)}) %collective-permute-start) | collective-permute-done | bytes 32800 | tf_op jit(solution)/shard_map/cond/branch_1_fun/ppermute | solution.py:92
  28.7 1.9 %collective-permute-start.1 = (f16[2,16,1024]{2,1,0:T(8,128)(2,1)S(1)}, f16[2,16,1024]{2,1,0:T(8,128)(2,1)S(1)}, u32[]{:S(2)}, u32[]{:S(2)}) collective-permute-start(f16[2,16,1024]{2,1,0:T(8,128)(2,1)S(1)} %pad_maximum_fusion.3), channel_id=1, source_target_pairs={{0,128},{128,0},{256,384},{384,256},{1,129},{129,1},{257,385},{385... | collective-permute-start | bytes 196616 | tf_op jit(solution)/shard_map/cond/branch_1_fun/ppermute | solution.py:92
  30.6 4.2 %collective-permute-done.1 = f16[2,16,1024]{2,1,0:T(8,128)(2,1)S(1)} collective-permute-done((f16[2,16,1024]{2,1,0:T(8,128)(2,1)S(1)}, f16[2,16,1024]{2,1,0:T(8,128)(2,1)S(1)}, u32[]{:S(2)}, u32[]{:S(2)}) %collective-permute-start.1) | collective-permute-done | bytes 65568 | tf_op jit(solution)/shard_map/cond/branch_1_fun/ppermute | solution.py:92
  35.0 4.0 %collective-permute-start.2 = (f16[4,16,1024]{2,1,0:T(8,128)(2,1)S(1)}, f16[4,16,1024]{2,1,0:T(8,128)(2,1)S(1)}, u32[]{:S(2)}, u32[]{:S(2)}) collective-permute-start(f16[4,16,1024]{2,1,0:T(8,128)(2,1)S(1)} %pad_maximum_fusion.2), channel_id=1, source_target_pairs={{0,64},{32,96},{64,0},{96,32},{1,65},{33,97},{65,1},{97,33},{2,66}... | collective-permute-start | bytes 393224 | tf_op jit(solution)/shard_map/cond/branch_1_fun/ppermute | solution.py:92
  39.0 4.4 %collective-permute-done.2 = f16[4,16,1024]{2,1,0:T(8,128)(2,1)S(1)} collective-permute-done((f16[4,16,1024]{2,1,0:T(8,128)(2,1)S(1)}, f16[4,16,1024]{2,1,0:T(8,128)(2,1)S(1)}, u32[]{:S(2)}, u32[]{:S(2)}) %collective-permute-start.2) | collective-permute-done | bytes 131104 | tf_op jit(solution)/shard_map/cond/branch_1_fun/ppermute | solution.py:92
  43.5 2.5 %collective-permute-start.3 = (f16[2,4,16,1024]{3,2,1,0:T(8,128)(2,1)S(1)}, f16[2,4,16,1024]{3,2,1,0:T(8,128)(2,1)S(1)}, u32[]{:S(2)}, u32[]{:S(2)}) collective-permute-start(f16[2,4,16,1024]{3,2,1,0:T(8,128)(2,1)S(1)} %pad_maximum_fusion.1), channel_id=1, source_target_pairs={{0,32},{32,0},{64,96},{96,64},{1,33},{33,1},{65,97},{97,65},{2,34}... | collective-permute-start | bytes 786440 | tf_op jit(solution)/shard_map/cond/branch_1_fun/ppermute | solution.py:92
  46.0 5.8 %collective-permute-done.3 = f16[2,4,16,1024]{3,2,1,0:T(8,128)(2,1)S(1)} collective-permute-done((f16[2,4,16,1024]{3,2,1,0:T(8,128)(2,1)S(1)}, f16[2,4,16,1024]{3,2,1,0:T(8,128)(2,1)S(1)}, u32[]{:S(2)}, u32[]{:S(2)}) %collective-permute-start.3) | collective-permute-done | bytes 262176 | tf_op jit(solution)/shard_map/cond/branch_1_fun/ppermute | solution.py:92
  53.0 13.4 %all-to-all-start.1 = ((f32[32,8,128]{2,1,0:T(8,128)}), f32[32,8,128]{2,1,0:T(8,128)S(1)}, u32[]{:S(2)}, u32[]{:S(2)}) async-start(f32[32,8,128]{2,1,0:T(8,128)} %broadcast_in_dim.9), calls=%async_computation.1 | async-start | bytes 262144 | tf_op jit(solution)/shard_map/all_to_all | solution.py:30
  67.6 13.1 %conditional.4 = (f16[4,16,1024]{2,1,0:T(8,128)(2,1)S(1)}) conditional(s32[]{:T(128)} %bitcast.14, () %tuple.36, f16[16,1024]{1,0:T(8,128)(2,1)S(1)} %multiply_convert_fusion.1), branch_computations={%region_4.5_spmd, %region_5.6_spmd} | conditional | flops 360454 | bytes 1441944 | solution.py:108
  67.6 1.9 %collective-permute-start.4 = (f16[16,1024]{1,0:T(8,128)(2,1)S(1)}, f16[16,1024]{1,0:T(8,128)(2,1)S(1)}, u32[]{:S(2)}, u32[]{:S(2)}) collective-permute-start(f16[16,1024]{1,0:T(8,128)(2,1)S(1)} %param.3), channel_id=1, source_target_pairs={{0,256},{128,384},{256,0},{384,128},{1,257},{129,385},{257,1},{385... | collective-permute-start | bytes 98312 | tf_op jit(solution)/shard_map/cond/branch_1_fun/ppermute | solution.py:92
  69.6 4.8 %collective-permute-done.4 = f16[16,1024]{1,0:T(8,128)(2,1)S(1)} collective-permute-done((f16[16,1024]{1,0:T(8,128)(2,1)S(1)}, f16[16,1024]{1,0:T(8,128)(2,1)S(1)}, u32[]{:S(2)}, u32[]{:S(2)}) %collective-permute-start.4) | collective-permute-done | bytes 32800 | tf_op jit(solution)/shard_map/cond/branch_1_fun/ppermute | solution.py:92
  74.5 2.2 %collective-permute-start.5 = (f16[2,16,1024]{2,1,0:T(8,128)(2,1)S(1)}, f16[2,16,1024]{2,1,0:T(8,128)(2,1)S(1)}, u32[]{:S(2)}, u32[]{:S(2)}) collective-permute-start(f16[2,16,1024]{2,1,0:T(8,128)(2,1)S(1)} %pad_maximum_fusion.5), channel_id=1, source_target_pairs={{0,128},{128,0},{256,384},{384,256},{1,129},{129,1},{257,385},{385... | collective-permute-start | bytes 196616 | tf_op jit(solution)/shard_map/cond/branch_1_fun/ppermute | solution.py:92
  76.7 4.0 %collective-permute-done.5 = f16[2,16,1024]{2,1,0:T(8,128)(2,1)S(1)} collective-permute-done((f16[2,16,1024]{2,1,0:T(8,128)(2,1)S(1)}, f16[2,16,1024]{2,1,0:T(8,128)(2,1)S(1)}, u32[]{:S(2)}, u32[]{:S(2)}) %collective-permute-start.5) | collective-permute-done | bytes 65568 | tf_op jit(solution)/shard_map/cond/branch_1_fun/ppermute | solution.py:92
  81.4 4.5 %all-to-all-start.2 = ((f32[16,8,128]{2,1,0:T(8,128)}), f32[16,8,128]{2,1,0:T(8,128)S(1)}, u32[]{:S(2)}, u32[]{:S(2)}) async-start(f32[16,8,128]{2,1,0:T(8,128)} %broadcast_in_dim.10), calls=%async_computation.2 | async-start | bytes 131072 | tf_op jit(solution)/shard_map/all_to_all | solution.py:30
  87.4 19.5 %conditional.5 = (f16[4,4,16,1024]{3,2,1,0:T(8,128)(2,1)S(1)}) conditional(s32[]{:T(128)} %bitcast.15, () %tuple.39, f16[4,16,1024]{2,1,0:T(8,128)(2,1)S(1)} %get-tuple-element.80), branch_computations={%region_7.8_spmd, %region_8.9_spmd} | conditional | flops 1441798 | bytes 5767320 | solution.py:108
  87.4 4.0 %collective-permute-start.6 = (f16[4,16,1024]{2,1,0:T(8,128)(2,1)S(1)}, f16[4,16,1024]{2,1,0:T(8,128)(2,1)S(1)}, u32[]{:S(2)}, u32[]{:S(2)}) collective-permute-start(f16[4,16,1024]{2,1,0:T(8,128)(2,1)S(1)} %param.5), channel_id=1, source_target_pairs={{0,64},{32,96},{64,0},{96,32},{1,65},{33,97},{65,1},{97,33},{2,66}... | collective-permute-start | bytes 393224 | tf_op jit(solution)/shard_map/cond/branch_1_fun/ppermute | solution.py:92
  91.4 5.2 %collective-permute-done.6 = f16[4,16,1024]{2,1,0:T(8,128)(2,1)S(1)} collective-permute-done((f16[4,16,1024]{2,1,0:T(8,128)(2,1)S(1)}, f16[4,16,1024]{2,1,0:T(8,128)(2,1)S(1)}, u32[]{:S(2)}, u32[]{:S(2)}) %collective-permute-start.6) | collective-permute-done | bytes 131104 | tf_op jit(solution)/shard_map/cond/branch_1_fun/ppermute | solution.py:92
  96.8 2.2 %collective-permute-start.7 = (f16[2,4,16,1024]{3,2,1,0:T(8,128)(2,1)S(1)}, f16[2,4,16,1024]{3,2,1,0:T(8,128)(2,1)S(1)}, u32[]{:S(2)}, u32[]{:S(2)}) collective-permute-start(f16[2,4,16,1024]{3,2,1,0:T(8,128)(2,1)S(1)} %pad_maximum_fusion.7), channel_id=1, source_target_pairs={{0,32},{32,0},{64,96},{96,64},{1,33},{33,1},{65,97},{97,65},{2,34}... | collective-permute-start | bytes 786440 | tf_op jit(solution)/shard_map/cond/branch_1_fun/ppermute | solution.py:92
  99.0 7.5 %collective-permute-done.7 = f16[2,4,16,1024]{3,2,1,0:T(8,128)(2,1)S(1)} collective-permute-done((f16[2,4,16,1024]{3,2,1,0:T(8,128)(2,1)S(1)}, f16[2,4,16,1024]{3,2,1,0:T(8,128)(2,1)S(1)}, u32[]{:S(2)}, u32[]{:S(2)}) %collective-permute-start.7) | collective-permute-done | bytes 262176 | tf_op jit(solution)/shard_map/cond/branch_1_fun/ppermute | solution.py:92
  110.4 1.5 %fusion = (bf16[1,256,1024]{2,1,0:T(8,128)(2,1)}, f32[256,1024]{1,0:T(8,128)}) fusion(bf16[1,256,1024]{2,1,0:T(8,128)(2,1)S(1)} %copy-done.1, f32[4,4,16,1024]{3,2,1,0:T(8,128)S(1)} %copy.7, f32[256,1024]{1,0:T(8,128)S(1)} %copy-done, f32[4,4,16,1024]{3,2,1,0:T(8,128)S(1)} %copy.6), kind=kLoop, calls=%fused_computation.30 | loop fusion | flops 1572864 | bytes 5242880 | tf_op jit(solution)/shard_map/broadcast_in_dim | solution.py:148
  (49 shorter events, 8.2 us)
Async XLA Ops:
  5.4 46.8 %all-to-all-start = ((bf16[16,16,1024]{2,1,0:T(8,128)(2,1)}), bf16[16,16,1024]{2,1,0:T(8,128)(2,1)S(1)}, u32[]{:S(2)}, u32[]{:S(2)}) async-start(bf16[16,16,1024]{2,1,0:T(8,128)(2,1)} %bitcast.45), calls=%async_computation | async-start | bytes 1048576 | tf_op jit(solution)/shard_map/all_to_all | solution.py:30
  15.9 12.8 %collective-permute-start = (f16[16,1024]{1,0:T(8,128)(2,1)S(1)}, f16[16,1024]{1,0:T(8,128)(2,1)S(1)}, u32[]{:S(2)}, u32[]{:S(2)}) collective-permute-start(f16[16,1024]{1,0:T(8,128)(2,1)S(1)} %param.1), channel_id=1, source_target_pairs={{0,256},{128,384},{256,0},{384,128},{1,257},{129,385},{257,1},{385... | collective-permute-start | bytes 98312 | tf_op jit(solution)/shard_map/cond/branch_1_fun/ppermute | solution.py:92
  28.7 6.2 %collective-permute-start.1 = (f16[2,16,1024]{2,1,0:T(8,128)(2,1)S(1)}, f16[2,16,1024]{2,1,0:T(8,128)(2,1)S(1)}, u32[]{:S(2)}, u32[]{:S(2)}) collective-permute-start(f16[2,16,1024]{2,1,0:T(8,128)(2,1)S(1)} %pad_maximum_fusion.3), channel_id=1, source_target_pairs={{0,128},{128,0},{256,384},{384,256},{1,129},{129,1},{257,385},{385... | collective-permute-start | bytes 196616 | tf_op jit(solution)/shard_map/cond/branch_1_fun/ppermute | solution.py:92
  35.0 8.4 %collective-permute-start.2 = (f16[4,16,1024]{2,1,0:T(8,128)(2,1)S(1)}, f16[4,16,1024]{2,1,0:T(8,128)(2,1)S(1)}, u32[]{:S(2)}, u32[]{:S(2)}) collective-permute-start(f16[4,16,1024]{2,1,0:T(8,128)(2,1)S(1)} %pad_maximum_fusion.2), channel_id=1, source_target_pairs={{0,64},{32,96},{64,0},{96,32},{1,65},{33,97},{65,1},{97,33},{2,66}... | collective-permute-start | bytes 393224 | tf_op jit(solution)/shard_map/cond/branch_1_fun/ppermute | solution.py:92
  43.5 8.3 %collective-permute-start.3 = (f16[2,4,16,1024]{3,2,1,0:T(8,128)(2,1)S(1)}, f16[2,4,16,1024]{3,2,1,0:T(8,128)(2,1)S(1)}, u32[]{:S(2)}, u32[]{:S(2)}) collective-permute-start(f16[2,4,16,1024]{3,2,1,0:T(8,128)(2,1)S(1)} %pad_maximum_fusion.1), channel_id=1, source_target_pairs={{0,32},{32,0},{64,96},{96,64},{1,33},{33,1},{65,97},{97,65},{2,34}... | collective-permute-start | bytes 786440 | tf_op jit(solution)/shard_map/cond/branch_1_fun/ppermute | solution.py:92
  53.0 27.7 %all-to-all-start.1 = ((f32[32,8,128]{2,1,0:T(8,128)}), f32[32,8,128]{2,1,0:T(8,128)S(1)}, u32[]{:S(2)}, u32[]{:S(2)}) async-start(f32[32,8,128]{2,1,0:T(8,128)} %broadcast_in_dim.9), calls=%async_computation.1 | async-start | bytes 262144 | tf_op jit(solution)/shard_map/all_to_all | solution.py:30
  67.6 6.8 %collective-permute-start.4 = (f16[16,1024]{1,0:T(8,128)(2,1)S(1)}, f16[16,1024]{1,0:T(8,128)(2,1)S(1)}, u32[]{:S(2)}, u32[]{:S(2)}) collective-permute-start(f16[16,1024]{1,0:T(8,128)(2,1)S(1)} %param.3), channel_id=1, source_target_pairs={{0,256},{128,384},{256,0},{384,128},{1,257},{129,385},{257,1},{385... | collective-permute-start | bytes 98312 | tf_op jit(solution)/shard_map/cond/branch_1_fun/ppermute | solution.py:92
  74.5 6.2 %collective-permute-start.5 = (f16[2,16,1024]{2,1,0:T(8,128)(2,1)S(1)}, f16[2,16,1024]{2,1,0:T(8,128)(2,1)S(1)}, u32[]{:S(2)}, u32[]{:S(2)}) collective-permute-start(f16[2,16,1024]{2,1,0:T(8,128)(2,1)S(1)} %pad_maximum_fusion.5), channel_id=1, source_target_pairs={{0,128},{128,0},{256,384},{384,256},{1,129},{129,1},{257,385},{385... | collective-permute-start | bytes 196616 | tf_op jit(solution)/shard_map/cond/branch_1_fun/ppermute | solution.py:92
  81.4 25.5 %all-to-all-start.2 = ((f32[16,8,128]{2,1,0:T(8,128)}), f32[16,8,128]{2,1,0:T(8,128)S(1)}, u32[]{:S(2)}, u32[]{:S(2)}) async-start(f32[16,8,128]{2,1,0:T(8,128)} %broadcast_in_dim.10), calls=%async_computation.2 | async-start | bytes 131072 | tf_op jit(solution)/shard_map/all_to_all | solution.py:30
  87.4 9.2 %collective-permute-start.6 = (f16[4,16,1024]{2,1,0:T(8,128)(2,1)S(1)}, f16[4,16,1024]{2,1,0:T(8,128)(2,1)S(1)}, u32[]{:S(2)}, u32[]{:S(2)}) collective-permute-start(f16[4,16,1024]{2,1,0:T(8,128)(2,1)S(1)} %param.5), channel_id=1, source_target_pairs={{0,64},{32,96},{64,0},{96,32},{1,65},{33,97},{65,1},{97,33},{2,66}... | collective-permute-start | bytes 393224 | tf_op jit(solution)/shard_map/cond/branch_1_fun/ppermute | solution.py:92
  96.8 9.7 %collective-permute-start.7 = (f16[2,4,16,1024]{3,2,1,0:T(8,128)(2,1)S(1)}, f16[2,4,16,1024]{3,2,1,0:T(8,128)(2,1)S(1)}, u32[]{:S(2)}, u32[]{:S(2)}) collective-permute-start(f16[2,4,16,1024]{3,2,1,0:T(8,128)(2,1)S(1)} %pad_maximum_fusion.7), channel_id=1, source_target_pairs={{0,32},{32,0},{64,96},{96,64},{1,33},{33,1},{65,97},{97,65},{2,34}... | collective-permute-start | bytes 786440 | tf_op jit(solution)/shard_map/cond/branch_1_fun/ppermute | solution.py:92
  106.9 1.3 %copy-start.2 = (f32[16,1024]{1,0:T(8,128)S(1)}, f32[16,1024]{1,0:T(8,128)}, u32[]{:S(2)}) copy-start(f32[16,1024]{1,0:T(8,128)} %param.11) | copy-start | bytes 196612
  109.0 1.2 %copy-start = (f32[256,1024]{1,0:T(8,128)S(1)}, f32[256,1024]{1,0:T(8,128)}, u32[]{:S(2)}) copy-start(f32[256,1024]{1,0:T(8,128)} %base_ref.1) | copy-start | bytes 3145732
  109.0 1.3 %copy-start.1 = (bf16[1,256,1024]{2,1,0:T(8,128)(2,1)S(1)}, bf16[1,256,1024]{2,1,0:T(8,128)(2,1)}, u32[]{:S(2)}) copy-start(bf16[1,256,1024]{2,1,0:T(8,128)(2,1)} %param.10) | copy-start | bytes 1572868

commit v4 on v3

--- a/solution.py
+++ b/solution.py
@@ -12,8 +12,6 @@
 REPLICA = ("replica_0", "replica_1")
 FSDP = ("fsdp_0", "fsdp_1", "fsdp_2")
 FSDP_REPLICA = ("fsdp_0", "fsdp_1", "fsdp_2", "replica_0", "replica_1")
-PLANE = ("replica_1", "fsdp_0")
-RING = ("fsdp_1", "replica_0", "fsdp_2")
 code_limit = 448.0
 outer_rate = 0.7
 outer_momentum = 0.9
@@ -88,28 +86,25 @@
     return value.astype(jnp.float32) * (1.0 / unit)
 
 
-def swapped(value, axis, bit):
-    return lax.ppermute(value, axis, [(i, i ^ bit) for i in range(lax.axis_size(axis))])
-
-
 def gathered(value, axis):
-    place = lax.axis_index(axis)
-    upper, odd = place >= 2, (place & 1) == 1
-    other = swapped(value, axis, 2)
-    halves = jnp.stack([jnp.where(upper, other, value), jnp.where(upper, value, other)])
-    other = swapped(halves, axis, 1)
-    evens, odds = jnp.where(odd, other, halves), jnp.where(odd, halves, other)
-    return jnp.stack([evens[0], odds[0], evens[1], odds[1]])
+    size, place = lax.axis_size(axis), lax.axis_index(axis)
+    seen = [value] + [
+        lax.ppermute(value, axis, [(i, (i + far) % size) for i in range(size)])
+        for far in range(1, size)
+    ]
+    ordered = []
+    for at in range(size):
+        block = seen[0]
+        for far in range(1, size):
+            block = jnp.where(lax.rem(place - at + size, size) == far, seen[far], block)
+        ordered.append(block)
+    return jnp.stack(ordered)
 
 
 def beside(task, value):
     shape = jax.eval_shape(task, value)
     held = value.reshape(-1)[0].astype(jnp.float32) < 1e30
     return lax.cond(held, task, lambda v: jnp.zeros(shape.shape, shape.dtype), value)
-
-
-def in_rows(blocks):
-    return jnp.swapaxes(blocks, 0, 1).reshape(-1, blocks.shape[-1])
 
 
 def shards(base_weights, inner_weights, momentum):
@@ -123,27 +118,26 @@
         (decoded_deltas(base_weights, replica_copy), in_half(momentum, momentum_unit))
     )
     arrived = exchanged(decoded.reshape(replicas, owned_rows, columns), REPLICA)
-    momenta = beside(lambda v: gathered(gathered(v, REPLICA[0]), REPLICA[1]), momenta)
+    momenta = beside(lambda v: gathered(v, REPLICA[0]), momenta)
     arrived, momenta = together((arrived, momenta))
     outer_grad = arrived.astype(jnp.float32).sum(axis=0) / replicas
 
-    squares, grads = together((partial_squares(outer_grad), in_half(outer_grad, grad_unit)))
-    squares = to_everyone(squares, PLANE)
-    grads = beside(lambda v: gathered(v, REPLICA[0]), grads)
-    squares, grads = together((squares, grads))
-    squares, grads = together((squares.sum(axis=0), grads))
-    squares = to_everyone(squares, RING)
-    grads = beside(lambda v: gathered(v, REPLICA[1]), grads)
-    squares, grads = together((squares, grads))
+    grads, momenta = together((in_half(outer_grad, grad_unit), momenta))
+    grads = to_everyone(grads, REPLICA).reshape(local_rows, columns)
+    momenta = beside(lambda v: gathered(v, REPLICA[1]), momenta)
+    grads, momenta = together((grads, momenta))
 
+    squares = to_everyone(partial_squares(from_half(grads, grad_unit)), FSDP)
+    momenta = jnp.swapaxes(momenta, 0, 1).reshape(local_rows, columns)
+    start = together(
+        base_weights
+        - (outer_rate * outer_momentum * outer_momentum) * from_half(momenta, momentum_unit)
+    )
     grad_sq = squares.sum()
     clip_factor = jnp.minimum(1.0, clip_rms / jnp.sqrt(grad_sq / (D * KVW) + epsilon))
     new_momentum = outer_momentum * momentum + clip_factor * outer_grad
-    start = base_weights - (
-        outer_rate * outer_momentum * outer_momentum / momentum_unit
-    ) * in_rows(momenta).astype(jnp.float32)
     rate = (outer_rate * (1.0 + outer_momentum) / grad_unit) * clip_factor
-    new_base = start - rate * in_rows(grads).astype(jnp.float32)
+    new_base = start - rate * grads.astype(jnp.float32)
     blended = blend_share * replica_copy.astype(jnp.float32) + (1.0 - blend_share) * new_base
     return (new_base, new_momentum, blended.astype(jnp.bfloat16)[None])
 

time: 113 us -> 85.7 us (0.76)
  the two profiles are of different devices: /device:TPU:2 before, /device:TPU:16 now
where the time goes in v4:
time: 85.7 us; the launch traced here: 85 us
  starting transfers between devices  48.8 us (57%)
  waiting for transfers between devices  20.9 us (24%)
  other arithmetic  4.68 us (5%)
  Pallas kernels  3.9 us (5%)
  local copies, waits for them, and re-layouts  3.83 us (4%)
  between operations  2.74 us (3%)
    all_to_all x3, starting transfers between devices, exchanged(): return lax.all_to_all(blocks, axis, split_axis=0, concat_axis=0, tiled=True)  28.6 us
    ppermute x6, starting transfers between devices, gathered(): lax.ppermute(value, axis, [(i, (i + far) % size) for i in range(size)])  20.2 us
    all_to_all x3, waiting for transfers between devices, exchanged(): return lax.all_to_all(blocks, axis, split_axis=0, concat_axis=0, tiled=True)  14.7 us
    ppermute x6, waiting for transfers between devices, gathered(): lax.ppermute(value, axis, [(i, (i + far) % size) for i in range(size)])  6.21 us
    pallas_call x1, Pallas kernels, decoded_deltas(): pl.pallas_call(encode_kernel, grid=(rows // tall,), in_specs=[spec, spec]...  3.9 us
  transfers between devices with their start and end apart: 9, of which 5 were waited for; matrix products, arithmetic and copies ran while one was open for 2% of the time, Pallas kernels for 0%

profile of v4, /device:TPU:16, one launch (start us, length us, event | category | flops | bytes accessed | tf_op | source)
XLA Modules:
  0.0 85.0 jit_solution(10309669182128105606)
XLA Ops:
  0.6 0.9 %multiply_convert_fusion.2 = f16[16,1024]{1,0:T(8,128)(2,1)S(1)} fusion(f32[16,1024]{1,0:T(8,128)} %param.9), kind=kLoop, calls=%fused_computation.23 | loop fusion | flops 32768 | bytes 98304 | tf_op jit(solution)/shard_map/convert_element_type | solution.py:82
  1.5 3.9 %shard_map.58 = bf16[256,1024]{1,0:T(8,128)(2,1)} custom-call(f32[256,1024]{1,0:T(8,128)} %base_ref.1, bf16[256,1024]{1,0:T(8,128)(2,1)} %bitcast.39), custom_call_target="tpu_custom_call" | custom-call | flops 5242880 | bytes 2097152 | tf_op jit(solution)/shard_map/pallas_call | solution.py:63
  5.4 9.1 %all-to-all-start = ((bf16[16,16,1024]{2,1,0:T(8,128)(2,1)}), bf16[16,16,1024]{2,1,0:T(8,128)(2,1)S(1)}, u32[]{:S(2)}, u32[]{:S(2)}) async-start(bf16[16,16,1024]{2,1,0:T(8,128)(2,1)} %bitcast.38), calls=%async_computation | async-start | bytes 1048576 | tf_op jit(solution)/shard_map/all_to_all | solution.py:28
  15.7 11.8 %conditional.2 = (f16[4,16,1024]{2,1,0:T(8,128)(2,1)S(1)}) conditional(s32[]{:T(128)} %bitcast.10, () %tuple.25, f16[16,1024]{1,0:T(8,128)(2,1)S(1)} %multiply_convert_fusion.2), branch_computations={%region_0.0_spmd, %region_1.2_spmd} | conditional | flops 393259 | bytes 918084 | solution.py:107
  15.7 3.4 %collective-permute-start.2 = (f16[16,1024]{1,0:T(8,128)(2,1)S(1)}, f16[16,1024]{1,0:T(8,128)(2,1)S(1)}, u32[]{:S(2)}, u32[]{:S(2)}) collective-permute-start(f16[16,1024]{1,0:T(8,128)(2,1)S(1)} %param.1), channel_id=1, source_target_pairs={{0,128},{128,256},{256,384},{384,0},{1,129},{129,257},{257,385},{3... | collective-permute-start | bytes 98312 | tf_op jit(solution)/shard_map/cond/branch_1_fun/ppermute | solution.py:92
  19.1 2.4 %collective-permute-start.1 = (f16[16,1024]{1,0:T(8,128)(2,1)S(1)}, f16[16,1024]{1,0:T(8,128)(2,1)S(1)}, u32[]{:S(2)}, u32[]{:S(2)}) collective-permute-start(f16[16,1024]{1,0:T(8,128)(2,1)S(1)} %param.1), channel_id=1, source_target_pairs={{0,256},{128,384},{256,0},{384,128},{1,257},{129,385},{257,1},{385... | collective-permute-start | bytes 98312 | tf_op jit(solution)/shard_map/cond/branch_1_fun/ppermute | solution.py:92
  21.5 3.0 %collective-permute-start = (f16[16,1024]{1,0:T(8,128)(2,1)S(1)}, f16[16,1024]{1,0:T(8,128)(2,1)S(1)}, u32[]{:S(2)}, u32[]{:S(2)}) collective-permute-start(f16[16,1024]{1,0:T(8,128)(2,1)S(1)} %param.1), channel_id=1, source_target_pairs={{0,384},{128,0},{256,128},{384,256},{1,385},{129,1},{257,129},{385... | collective-permute-start | bytes 98312 | tf_op jit(solution)/shard_map/cond/branch_1_fun/ppermute | solution.py:92
  24.6 2.7 %collective-permute-done.2 = f16[16,1024]{1,0:T(8,128)(2,1)S(1)} collective-permute-done((f16[16,1024]{1,0:T(8,128)(2,1)S(1)}, f16[16,1024]{1,0:T(8,128)(2,1)S(1)}, u32[]{:S(2)}, u32[]{:S(2)}) %collective-permute-start.2) | collective-permute-done | bytes 32800 | tf_op jit(solution)/shard_map/cond/branch_1_fun/ppermute | solution.py:92
  27.5 1.9 %all-to-all-done = bf16[16,16,1024]{2,1,0:T(8,128)(2,1)S(1)} async-done(((bf16[16,16,1024]{2,1,0:T(8,128)(2,1)}), bf16[16,16,1024]{2,1,0:T(8,128)(2,1)S(1)}, u32[]{:S(2)}, u32[]{:S(2)}) %all-to-all-start) | async-done | bytes 524320 | tf_op jit(solution)/shard_map/all_to_all | solution.py:28
  29.5 0.9 %broadcast_in_dim.9 = f16[16,16,1024]{2,1,0:T(8,128)(2,1)} broadcast(f16[16,1024]{1,0:T(8,128)(2,1)S(1)} %multiply_convert_fusion.1), dimensions={1,2} | broadcast | bytes 557056 | tf_op jit(solution)/shard_map/broadcast_in_dim | solution.py:32
  30.3 7.4 %all-to-all-start.1 = ((f16[16,16,1024]{2,1,0:T(8,128)(2,1)}), f16[16,16,1024]{2,1,0:T(8,128)(2,1)S(1)}, u32[]{:S(2)}, u32[]{:S(2)}) async-start(f16[16,16,1024]{2,1,0:T(8,128)(2,1)} %broadcast_in_dim.9), calls=%async_computation.1 | async-start | bytes 1048576 | tf_op jit(solution)/shard_map/all_to_all | solution.py:28
  39.0 15.2 %conditional.3 = (f16[4,4,16,1024]{3,2,1,0:T(8,128)(2,1)S(1)}) conditional(s32[]{:T(128)} %bitcast.12, () %tuple.28, f16[4,16,1024]{2,1,0:T(8,128)(2,1)S(1)} %get-tuple-element.37), branch_computations={%region_3.4_spmd, %region_4.5_spmd} | conditional | flops 1572907 | bytes 3670596 | solution.py:107
  39.0 3.4 %collective-permute-start.5 = (f16[4,16,1024]{2,1,0:T(8,128)(2,1)S(1)}, f16[4,16,1024]{2,1,0:T(8,128)(2,1)S(1)}, u32[]{:S(2)}, u32[]{:S(2)}) collective-permute-start(f16[4,16,1024]{2,1,0:T(8,128)(2,1)S(1)} %param.3), channel_id=1, source_target_pairs={{0,32},{32,64},{64,96},{96,0},{1,33},{33,65},{65,97},{97,1},{2,34}... | collective-permute-start | bytes 393224 | tf_op jit(solution)/shard_map/cond/branch_1_fun/ppermute | solution.py:92
  42.4 4.6 %collective-permute-start.4 = (f16[4,16,1024]{2,1,0:T(8,128)(2,1)S(1)}, f16[4,16,1024]{2,1,0:T(8,128)(2,1)S(1)}, u32[]{:S(2)}, u32[]{:S(2)}) collective-permute-start(f16[4,16,1024]{2,1,0:T(8,128)(2,1)S(1)} %param.3), channel_id=1, source_target_pairs={{0,64},{32,96},{64,0},{96,32},{1,65},{33,97},{65,1},{97,33},{2,66}... | collective-permute-start | bytes 393224 | tf_op jit(solution)/shard_map/cond/branch_1_fun/ppermute | solution.py:92
  47.0 3.4 %collective-permute-start.3 = (f16[4,16,1024]{2,1,0:T(8,128)(2,1)S(1)}, f16[4,16,1024]{2,1,0:T(8,128)(2,1)S(1)}, u32[]{:S(2)}, u32[]{:S(2)}) collective-permute-start(f16[4,16,1024]{2,1,0:T(8,128)(2,1)S(1)} %param.3), channel_id=1, source_target_pairs={{0,96},{32,0},{64,32},{96,64},{1,97},{33,1},{65,33},{97,65},{2,98}... | collective-permute-start | bytes 393224 | tf_op jit(solution)/shard_map/cond/branch_1_fun/ppermute | solution.py:92
  50.4 1.2 %collective-permute-done.4 = f16[4,16,1024]{2,1,0:T(8,128)(2,1)S(1)} collective-permute-done((f16[4,16,1024]{2,1,0:T(8,128)(2,1)S(1)}, f16[4,16,1024]{2,1,0:T(8,128)(2,1)S(1)}, u32[]{:S(2)}, u32[]{:S(2)}) %collective-permute-start.4) | collective-permute-done | bytes 131104 | tf_op jit(solution)/shard_map/cond/branch_1_fun/ppermute | solution.py:92
  51.7 2.2 %collective-permute-done.3 = f16[4,16,1024]{2,1,0:T(8,128)(2,1)S(1)} collective-permute-done((f16[4,16,1024]{2,1,0:T(8,128)(2,1)S(1)}, f16[4,16,1024]{2,1,0:T(8,128)(2,1)S(1)}, u32[]{:S(2)}, u32[]{:S(2)}) %collective-permute-start.3) | collective-permute-done | bytes 131104 | tf_op jit(solution)/shard_map/cond/branch_1_fun/ppermute | solution.py:92
  54.5 0.7 broadcast_in_dim.10
  55.2 12.1 %all-to-all-start.2 = ((f32[32,8,128]{2,1,0:T(8,128)}), f32[32,8,128]{2,1,0:T(8,128)S(1)}, u32[]{:S(2)}, u32[]{:S(2)}) async-start(f32[32,8,128]{2,1,0:T(8,128)} %broadcast_in_dim.10), calls=%async_computation.2 | async-start | bytes 262144 | tf_op jit(solution)/shard_map/all_to_all | solution.py:28
  67.5 1.1 %copy-done = f32[256,1024]{1,0:T(8,128)S(1)} copy-done((f32[256,1024]{1,0:T(8,128)S(1)}, f32[256,1024]{1,0:T(8,128)}, u32[]{:S(2)}) %copy-start) | copy-done | bytes 1048600
  68.9 12.7 %all-to-all-done.2 = f32[32,8,128]{2,1,0:T(8,128)S(1)} async-done(((f32[32,8,128]{2,1,0:T(8,128)}), f32[32,8,128]{2,1,0:T(8,128)S(1)}, u32[]{:S(2)}, u32[]{:S(2)}) %all-to-all-start.2) | async-done | bytes 131104 | tf_op jit(solution)/shard_map/all_to_all | solution.py:28
  81.6 0.6 reduce_sum.29
  82.9 0.6 multiply_add_fusion
  83.6 1.4 %fusion.4 = (bf16[1,256,1024]{2,1,0:T(8,128)(2,1)}, f32[256,1024]{1,0:T(8,128)}) fusion(bf16[1,256,1024]{2,1,0:T(8,128)(2,1)S(1)} %copy-done.1, f32[256,1024]{1,0:T(8,128)S(1)} %bitcast_subtract_fusion, f16[256,1024]{1,0:T(8,128)(2,1)S(1)} %bitcast.37, f32[]{:T(128)S(6)} %mul_shard_map.3), kind=kLoop, calls=%fused_computation.20 | loop fusion | flops 1835008 | bytes 3670020 | tf_op jit(solution)/shard_map/broadcast_in_dim | solution.py:142
  (23 shorter events, 2.4 us)
Async XLA Ops:
  5.4 24.0 %all-to-all-start = ((bf16[16,16,1024]{2,1,0:T(8,128)(2,1)}), bf16[16,16,1024]{2,1,0:T(8,128)(2,1)S(1)}, u32[]{:S(2)}, u32[]{:S(2)}) async-start(bf16[16,16,1024]{2,1,0:T(8,128)(2,1)} %bitcast.38), calls=%async_computation | async-start | bytes 1048576 | tf_op jit(solution)/shard_map/all_to_all | solution.py:28
  15.7 11.6 %collective-permute-start.2 = (f16[16,1024]{1,0:T(8,128)(2,1)S(1)}, f16[16,1024]{1,0:T(8,128)(2,1)S(1)}, u32[]{:S(2)}, u32[]{:S(2)}) collective-permute-start(f16[16,1024]{1,0:T(8,128)(2,1)S(1)} %param.1), channel_id=1, source_target_pairs={{0,128},{128,256},{256,384},{384,0},{1,129},{129,257},{257,385},{3... | collective-permute-start | bytes 98312 | tf_op jit(solution)/shard_map/cond/branch_1_fun/ppermute | solution.py:92
  19.1 8.2 %collective-permute-start.1 = (f16[16,1024]{1,0:T(8,128)(2,1)S(1)}, f16[16,1024]{1,0:T(8,128)(2,1)S(1)}, u32[]{:S(2)}, u32[]{:S(2)}) collective-permute-start(f16[16,1024]{1,0:T(8,128)(2,1)S(1)} %param.1), channel_id=1, source_target_pairs={{0,256},{128,384},{256,0},{384,128},{1,257},{129,385},{257,1},{385... | collective-permute-start | bytes 98312 | tf_op jit(solution)/shard_map/cond/branch_1_fun/ppermute | solution.py:92
  21.5 5.8 %collective-permute-start = (f16[16,1024]{1,0:T(8,128)(2,1)S(1)}, f16[16,1024]{1,0:T(8,128)(2,1)S(1)}, u32[]{:S(2)}, u32[]{:S(2)}) collective-permute-start(f16[16,1024]{1,0:T(8,128)(2,1)S(1)} %param.1), channel_id=1, source_target_pairs={{0,384},{128,0},{256,128},{384,256},{1,385},{129,1},{257,129},{385... | collective-permute-start | bytes 98312 | tf_op jit(solution)/shard_map/cond/branch_1_fun/ppermute | solution.py:92
  30.3 23.9 %all-to-all-start.1 = ((f16[16,16,1024]{2,1,0:T(8,128)(2,1)}), f16[16,16,1024]{2,1,0:T(8,128)(2,1)S(1)}, u32[]{:S(2)}, u32[]{:S(2)}) async-start(f16[16,16,1024]{2,1,0:T(8,128)(2,1)} %broadcast_in_dim.9), calls=%async_computation.1 | async-start | bytes 1048576 | tf_op jit(solution)/shard_map/all_to_all | solution.py:28
  39.0 11.4 %collective-permute-start.5 = (f16[4,16,1024]{2,1,0:T(8,128)(2,1)S(1)}, f16[4,16,1024]{2,1,0:T(8,128)(2,1)S(1)}, u32[]{:S(2)}, u32[]{:S(2)}) collective-permute-start(f16[4,16,1024]{2,1,0:T(8,128)(2,1)S(1)} %param.3), channel_id=1, source_target_pairs={{0,32},{32,64},{64,96},{96,0},{1,33},{33,65},{65,97},{97,1},{2,34}... | collective-permute-start | bytes 393224 | tf_op jit(solution)/shard_map/cond/branch_1_fun/ppermute | solution.py:92
  42.4 9.3 %collective-permute-start.4 = (f16[4,16,1024]{2,1,0:T(8,128)(2,1)S(1)}, f16[4,16,1024]{2,1,0:T(8,128)(2,1)S(1)}, u32[]{:S(2)}, u32[]{:S(2)}) collective-permute-start(f16[4,16,1024]{2,1,0:T(8,128)(2,1)S(1)} %param.3), channel_id=1, source_target_pairs={{0,64},{32,96},{64,0},{96,32},{1,65},{33,97},{65,1},{97,33},{2,66}... | collective-permute-start | bytes 393224 | tf_op jit(solution)/shard_map/cond/branch_1_fun/ppermute | solution.py:92
  47.0 6.9 %collective-permute-start.3 = (f16[4,16,1024]{2,1,0:T(8,128)(2,1)S(1)}, f16[4,16,1024]{2,1,0:T(8,128)(2,1)S(1)}, u32[]{:S(2)}, u32[]{:S(2)}) collective-permute-start(f16[4,16,1024]{2,1,0:T(8,128)(2,1)S(1)} %param.3), channel_id=1, source_target_pairs={{0,96},{32,0},{64,32},{96,64},{1,97},{33,1},{65,33},{97,65},{2,98}... | collective-permute-start | bytes 393224 | tf_op jit(solution)/shard_map/cond/branch_1_fun/ppermute | solution.py:92
  55.2 26.4 %all-to-all-start.2 = ((f32[32,8,128]{2,1,0:T(8,128)}), f32[32,8,128]{2,1,0:T(8,128)S(1)}, u32[]{:S(2)}, u32[]{:S(2)}) async-start(f32[32,8,128]{2,1,0:T(8,128)} %broadcast_in_dim.10), calls=%async_computation.2 | async-start | bytes 262144 | tf_op jit(solution)/shard_map/all_to_all | solution.py:28
  67.4 1.2 %copy-start = (f32[256,1024]{1,0:T(8,128)S(1)}, f32[256,1024]{1,0:T(8,128)}, u32[]{:S(2)}) copy-start(f32[256,1024]{1,0:T(8,128)} %base_ref.1) | copy-start | bytes 3145732
  68.7 14.9 %copy-start.1 = (bf16[1,256,1024]{2,1,0:T(8,128)(2,1)S(1)}, bf16[1,256,1024]{2,1,0:T(8,128)(2,1)}, u32[]{:S(2)}) copy-start(bf16[1,256,1024]{2,1,0:T(8,128)(2,1)} %param.8) | copy-start | bytes 1572868
  68.9 14.1 %copy-start.2 = (f32[16,1024]{1,0:T(8,128)S(1)}, f32[16,1024]{1,0:T(8,128)}, u32[]{:S(2)}) copy-start(f32[16,1024]{1,0:T(8,128)} %param.9) | copy-start | bytes 196612

commit v5 on v1

v5 whole, which is shorter than its diff:
```python
import jax
import jax.numpy as jnp
from jax import lax
from jax.experimental import pallas as pl
from jax.experimental.pallas import tpu as pltpu
from jax.sharding import Mesh
from jax.sharding import PartitionSpec as P

D = 8192
KVW = 1024
BLOCK = 128
REPLICA = ("replica_0", "replica_1")
FSDP = ("fsdp_0", "fsdp_1", "fsdp_2")
FSDP_REPLICA = ("fsdp_0", "fsdp_1", "fsdp_2", "replica_0", "replica_1")
code_limit = 448.0
outer_rate = 0.7
outer_momentum = 0.9
blend_share = 0.5
clip_rms = 0.02
epsilon = 1e-06
smallest_normal = 0.015625

sum_unit = 512.0
grad_unit = 2048.0
momentum_unit = 32768.0


def exchanged(blocks, axis):
    return lax.all_to_all(blocks, axis, split_axis=0, concat_axis=0, tiled=True)


def to_everyone(value, axis):
    copies = jnp.broadcast_to(value, (lax.axis_size(axis), *value.shape))
    return exchanged(copies, axis)


def smallest_scale(peaks):
    target = peaks * (1.0 / code_limit)
    spread = target * (2.0**23 + 1.0)
    scale = spread - (spread - target)
    scale = jnp.where(code_limit * scale < peaks, 2.0 * scale, scale)
    return jnp.where(code_limit * (0.5 * scale) >= peaks, 0.5 * scale, scale)


def encoded(base_block, inner_block):
    deltas = base_block - inner_block.astype(jnp.float32)
    magnitude = jnp.abs(deltas)
    scale = smallest_scale(jnp.max(magnitude, axis=1, keepdims=True) + epsilon)
    beyond = deltas * (1.0 + 2.0**-23)
    spread = beyond * (2.0**20 + 1.0)
    normal = spread - (spread - beyond)
    anchor = scale * (1.5 * 2.0**14)
    small = (beyond + anchor) - anchor
    return jnp.where(magnitude < scale * smallest_normal, small, normal)


def encode_kernel(base_ref, inner_ref, decoded_ref):
    across, along, rows, columns = decoded_ref.shape
    for at in range(0, columns, BLOCK):
        lanes = pl.ds(at, BLOCK)
        decoded = encoded(base_ref[:, lanes], inner_ref[:, lanes]).astype(decoded_ref.dtype)
        for y in range(along):
            for x in range(across):
                first = (y * across + x) * rows
                decoded_ref[x, y, :, lanes] = decoded[first : first + rows]


def decoded_deltas(base_weights, replica_copy, along, across):
    rows, columns = base_weights.shape
    steps = 2
    tall = rows // steps
    owned_rows = rows // (along * across)
    spec = pl.BlockSpec((tall, columns), lambda i: (i, 0))
    return pl.pallas_call(
        encode_kernel,
        grid=(steps,),
        in_specs=[spec, spec],
        out_specs=pl.BlockSpec(
            (across, along // steps, owned_rows, columns), lambda i: (0, i, 0, 0)
        ),
        out_shape=jax.ShapeDtypeStruct((across, along, owned_rows, columns), jnp.bfloat16),
        cost_estimate=pl.CostEstimate(
            flops=20 * rows * columns, bytes_accessed=8 * rows * columns, transcendentals=0
        ),
    )(base_weights, replica_copy)


def partial_squares(value):
    rows, columns = value.shape
    tiles = (value * value).reshape(rows // 8, 8, columns // 128, 128)
    return tiles.sum(axis=(0, 2))


def in_half(value, unit):
    return (value.astype(jnp.float32) * unit).astype(jnp.float16)


def from_half(value, unit):
    return value.astype(jnp.float32) * (1.0 / unit)


def shards(base_weights, inner_weights, momentum):
    along, across = lax.axis_size(REPLICA[0]), lax.axis_size(REPLICA[1])
    replicas = along * across
    local_rows, columns = base_weights.shape
    owned_rows = local_rows // replicas
    line_rows = along * owned_rows
    replica_copy = inner_weights[0]

    decoded = decoded_deltas(base_weights, replica_copy, along, across)
    arrived = exchanged(decoded.reshape(across, line_rows, columns), REPLICA[1])
    sums = arrived.astype(jnp.float32).sum(axis=0)

    sent = jnp.concatenate([in_half(sums, sum_unit), in_half(momentum, momentum_unit)])
    arrived = to_everyone(sent, REPLICA[0])
    outer_grad = arrived[:, :line_rows].astype(jnp.float32).sum(axis=0) * (
        1.0 / (sum_unit * replicas)
    )
    momenta = arrived[:, line_rows:].reshape(line_rows, columns)
    owned_grad = lax.dynamic_slice_in_dim(
        outer_grad, lax.axis_index(REPLICA[0]) * owned_rows, owned_rows, 0
    )

    everyones = to_everyone(jnp.stack([in_half(outer_grad, grad_unit), momenta]), REPLICA[1])
    everyones = everyones.reshape(across, 2, along, owned_rows, columns)
    grads, momenta = jnp.moveaxis(everyones, (1, 2), (0, 1)).reshape(2, local_rows, columns)

    squares = to_everyone(partial_squares(from_half(everyones[:, 0].reshape(local_rows, columns), grad_unit)), FSDP)
    start = lax.optimization_barrier(
        base_weights
        - (outer_rate * outer_momentum * outer_momentum) * from_half(momenta, momentum_unit)
    )
    grad_sq = squares.sum()
    clip_factor = jnp.minimum(1.0, clip_rms / jnp.sqrt(grad_sq / (D * KVW) + epsilon))
    new_momentum = outer_momentum * momentum + clip_factor * owned_grad
    rate = (outer_rate * (1.0 + outer_momentum) / grad_unit) * clip_factor
    new_base = start - rate * grads.astype(jnp.float32)
    blended = blend_share * replica_copy.astype(jnp.float32) + (1.0 - blend_share) * new_base
    return (new_base, new_momentum, blended.astype(jnp.bfloat16)[None])


def solution(mesh):
    torus = Mesh(
        mesh.devices.reshape(4, 4, 8, 2, 2),
        ("replica_0", "replica_1", "fsdp_0", "fsdp_1", "fsdp_2"),
    )
    return jax.shard_map(
        shards,
        mesh=torus,
        in_specs=(P(FSDP, None), P(REPLICA, FSDP, None), P(FSDP_REPLICA, None)),
        out_specs=(P(FSDP, None), P(FSDP_REPLICA, None), P(REPLICA, FSDP, None)),
        check_vma=False,
    )
```

time: 85.5 us -> 90.1 us (1.054)
  the two profiles are of different devices: /device:TPU:8 before, /device:TPU:1 now
where the time goes in v5:
time: 90.1 us; the launch traced here: 89.7 us
  blocking collectives  36.3 us (40%)
  starting transfers between devices  22.8 us (25%)
  waiting for transfers between devices  19.3 us (21%)
  other arithmetic  3.74 us (4%)
  local copies, waits for them, and re-layouts  3.09 us (3%)
  Pallas kernels  2.95 us (3%)
  between operations  1.45 us (2%)
    all_to_all x2, blocking collectives, exchanged(): return lax.all_to_all(blocks, axis, split_axis=0, concat_axis=0, tiled=True)  36.3 us
    all_to_all x2, starting transfers between devices, exchanged(): return lax.all_to_all(blocks, axis, split_axis=0, concat_axis=0, tiled=True)  22.8 us
    all_to_all x2, waiting for transfers between devices, exchanged(): return lax.all_to_all(blocks, axis, split_axis=0, concat_axis=0, tiled=True)  19.3 us
    pallas_call x1, Pallas kernels, decoded_deltas(): pl.pallas_call(encode_kernel, grid=(steps,), in_specs=[spec, spec], out_s...  2.95 us
    unnamed x6, local copies, waits for them, and re-layouts  2.01 us
  transfers between devices with their start and end apart: 2, of which 2 were waited for; matrix products, arithmetic and copies ran while one was open for 0% of the time, Pallas kernels for 0%

profile of v5, /device:TPU:1, one launch (start us, length us, event | category | flops | bytes accessed | tf_op | source)
XLA Modules:
  0.0 89.7 jit_solution(6281554466178849584)
XLA Ops:
  0.6 3.0 %shard_map.58 = bf16[4,4,16,1024]{3,2,1,0:T(8,128)(2,1)} custom-call(f32[256,1024]{1,0:T(8,128)} %base_ref.1, bf16[256,1024]{1,0:T(8,128)(2,1)} %bitcast.26), custom_call_target="tpu_custom_call" | custom-call | flops 5242880 | bytes 2097152 | tf_op jit(solution)/shard_map/pallas_call | solution.py:74
  3.6 5.0 %all-to-all-start = ((bf16[4,64,1024]{2,1,0:T(8,128)(2,1)}), bf16[4,64,1024]{2,1,0:T(8,128)(2,1)S(1)}, u32[]{:S(2)}, u32[]{:S(2)}) async-start(bf16[4,64,1024]{2,1,0:T(8,128)(2,1)} %bitcast.25), calls=%async_computation | async-start | bytes 1048576 | tf_op jit(solution)/shard_map/all_to_all | solution.py:29
  8.6 6.9 %all-to-all-done = bf16[4,64,1024]{2,1,0:T(8,128)(2,1)S(1)} async-done(((bf16[4,64,1024]{2,1,0:T(8,128)(2,1)}), bf16[4,64,1024]{2,1,0:T(8,128)(2,1)S(1)}, u32[]{:S(2)}, u32[]{:S(2)}) %all-to-all-start) | async-done | bytes 524320 | tf_op jit(solution)/shard_map/all_to_all | solution.py:29
  15.5 0.1 convert_reduce_fusion.1
  15.7 0.1 broadcast_in_dim.12
  15.7 21.4 %all_to_all.20 = f16[4,80,1024]{2,1,0:T(8,128)(2,1)S(1)} all-to-all(f16[4,80,1024]{2,1,0:T(8,128)(2,1)S(1)} %broadcast_in_dim.12), channel_id=1, replica_groups=mesh['replica_0'=4,'replica_1'=4,'fsdp_0'=8,'fsdp_1'=2,'fsdp_2'=2] {'rep..., dimensions={0} | all-to-all | bytes 1310720 | tf_op jit(solution)/shard_map/all_to_all | solution.py:29
  37.1 0.1 convert_reduce_fusion
  37.3 0.1 pad_maximum_fusion
  37.4 0.1 broadcast_in_dim.13
  37.5 15.0 %all_to_all.21 = f16[4,2,64,1024]{3,2,1,0:T(8,128)(2,1)S(1)} all-to-all(f16[4,2,64,1024]{3,2,1,0:T(8,128)(2,1)S(1)} %broadcast_in_dim.13), channel_id=1, replica_groups=mesh['replica_0'=4,'replica_1'=4,'fsdp_0'=8,'fsdp_1'=2,'fsdp_2'=2] {'rep..., dimensions={0} | all-to-all | bytes 2097152 | tf_op jit(solution)/shard_map/all_to_all | solution.py:29
  52.4 0.1 multiply_multiply_fusion
  52.6 0.2 bitcast_reduce_fusion
  52.8 0.7 broadcast_in_dim.14
  53.4 17.8 %all-to-all-start.3 = ((f32[32,8,128]{2,1,0:T(8,128)}), f32[32,8,128]{2,1,0:T(8,128)S(1)}, u32[]{:S(2)}, u32[]{:S(2)}) async-start(f32[32,8,128]{2,1,0:T(8,128)} %broadcast_in_dim.14), calls=%async_computation.3 | async-start | bytes 262144 | tf_op jit(solution)/shard_map/all_to_all | solution.py:29
  71.3 12.4 %all-to-all-done.3 = f32[32,8,128]{2,1,0:T(8,128)S(1)} async-done(((f32[32,8,128]{2,1,0:T(8,128)}), f32[32,8,128]{2,1,0:T(8,128)S(1)}, u32[]{:S(2)}, u32[]{:S(2)}) %all-to-all-start.3) | async-done | bytes 131104 | tf_op jit(solution)/shard_map/all_to_all | solution.py:29
  83.6 0.6 reduce_sum.39
  85.0 0.6 fusion.3
  85.6 0.3 convert_multiply_fusion
  85.9 0.1 copy.9
  86.0 0.1 copy.8
  86.1 1.1 %copy-done = f32[256,1024]{1,0:T(8,128)S(1)} copy-done((f32[256,1024]{1,0:T(8,128)S(1)}, f32[256,1024]{1,0:T(8,128)}, u32[]{:S(2)}) %copy-start) | copy-done | bytes 1048600
  87.2 0.1 bitcast_subtract_fusion.1
  87.4 0.9 copy-done.1
  88.3 1.4 %fusion = (bf16[1,256,1024]{2,1,0:T(8,128)(2,1)}, f32[256,1024]{1,0:T(8,128)}) fusion(bf16[1,256,1024]{2,1,0:T(8,128)(2,1)S(1)} %copy-done.1, f32[256,1024]{1,0:T(8,128)S(1)} %bitcast_subtract_fusion.1, f32[1,4,4,16,1024]{4,3,2,1,0:T(8,128)S(1)} %copy.9), kind=kLoop, calls=%fused_computation.9 | loop fusion | flops 1310720 | bytes 4194304 | tf_op jit(solution)/shard_map/broadcast_in_dim | solution.py:139
  (9 shorter events, 0.1 us)
Async XLA Ops:
  3.6 5.0 %copy-start.2 = (f32[16,1024]{1,0:T(8,128)S(1)}, f32[16,1024]{1,0:T(8,128)}, u32[]{:S(2)}) copy-start(f32[16,1024]{1,0:T(8,128)} %param.5) | copy-start | bytes 196612
  3.6 11.9 %all-to-all-start = ((bf16[4,64,1024]{2,1,0:T(8,128)(2,1)}), bf16[4,64,1024]{2,1,0:T(8,128)(2,1)S(1)}, u32[]{:S(2)}, u32[]{:S(2)}) async-start(bf16[4,64,1024]{2,1,0:T(8,128)(2,1)} %bitcast.25), calls=%async_computation | async-start | bytes 1048576 | tf_op jit(solution)/shard_map/all_to_all | solution.py:29
  53.4 30.2 %all-to-all-start.3 = ((f32[32,8,128]{2,1,0:T(8,128)}), f32[32,8,128]{2,1,0:T(8,128)S(1)}, u32[]{:S(2)}, u32[]{:S(2)}) async-start(f32[32,8,128]{2,1,0:T(8,128)} %broadcast_in_dim.14), calls=%async_computation.3 | async-start | bytes 262144 | tf_op jit(solution)/shard_map/all_to_all | solution.py:29
  86.0 1.2 %copy-start = (f32[256,1024]{1,0:T(8,128)S(1)}, f32[256,1024]{1,0:T(8,128)}, u32[]{:S(2)}) copy-start(f32[256,1024]{1,0:T(8,128)} %base_ref.1) | copy-start | bytes 3145732
  87.2 1.0 %copy-start.1 = (bf16[1,256,1024]{2,1,0:T(8,128)(2,1)S(1)}, bf16[1,256,1024]{2,1,0:T(8,128)(2,1)}, u32[]{:S(2)}) copy-start(bf16[1,256,1024]{2,1,0:T(8,128)(2,1)} %param.4) | copy-start | bytes 1572868

commit v6 on v1

--- a/solution.py
+++ b/solution.py
@@ -60,7 +60,7 @@
 
 def decoded_deltas(base_weights, replica_copy):
     rows, columns = base_weights.shape
-    tall = 64
+    tall = rows // 2
     spec = pl.BlockSpec((tall, columns), lambda i: (i, 0))
     return pl.pallas_call(
         encode_kernel,
@@ -87,6 +87,8 @@
     replica_copy = inner_weights[0]
     decoded = decoded_deltas(base_weights, replica_copy)
     arrived = exchanged(decoded.reshape(replicas, owned_rows, columns), REPLICA)
+    blended = blend_share * replica_copy.astype(jnp.float32) + (1.0 - blend_share) * base_weights
+    arrived, blended = lax.optimization_barrier((arrived, blended))
     outer_grad = arrived.astype(jnp.float32).sum(axis=0) / replicas
     squares = to_everyone(partial_squares(outer_grad), PLANE).sum(axis=0)
     grad_sq = to_everyone(squares, RING).sum()
@@ -96,9 +98,8 @@
     step = outer_rate * (step_term + outer_momentum * new_momentum)
     steps = to_everyone((step * step_unit).astype(jnp.float16), REPLICA)
     steps = steps.reshape(local_rows, columns).astype(jnp.float32) * (1.0 / step_unit)
-    new_base = base_weights - steps
-    blended = blend_share * replica_copy.astype(jnp.float32) + (1.0 - blend_share) * new_base
-    return (new_base, new_momentum, blended.astype(jnp.bfloat16)[None])
+    new_inner = (blended - (1.0 - blend_share) * steps).astype(jnp.bfloat16)
+    return (base_weights - steps, new_momentum, new_inner[None])
 
 
 def solution(mesh):

time: 85.5 us -> 83.9 us (0.981)
  blocking collectives: 75.8 us -> 53.1 us
  waiting for transfers between devices: 0 us -> 13.2 us
  starting transfers between devices: 0 us -> 9.34 us
  local copies, waits for them, and re-layouts: 0.98 us -> 0.08 us
  Pallas kernels: 3.9 us -> 3 us
    all_to_all x4 -> x3, blocking collectives: 75.8 us -> 53.1 us  [exchanged(): return lax.all_to_all(blocks, axis, split_axis=0, concat_axis=0, tiled=True)]
    all_to_all x0 -> x1, waiting for transfers between devices: none -> 13.2 us  [exchanged(): return lax.all_to_all(blocks, axis, split_axis=0, concat_axis=0, tiled=True)]
    all_to_all x0 -> x1, starting transfers between devices: none -> 9.34 us  [exchanged(): return lax.all_to_all(blocks, axis, split_axis=0, concat_axis=0, tiled=True)]
    convert_element_type x0 -> x1, other arithmetic: none -> 1.6 us  [shards(): new_inner = (blended - (1.0 - blend_share) * steps).astype(jnp.bfloat16)]
    broadcast_in_dim x1 -> x0, other arithmetic: 1.41 us -> none  [shards(): return (new_base, new_momentum, blended.astype(jnp.bfloat16)[None])]
    pallas_call x1, Pallas kernels: 3.9 us -> 3 us  [decoded_deltas(): pl.pallas_call(encode_kernel, grid=(rows // tall,), in_specs=[spec, spec]...]
    unnamed x6, local copies, waits for them, and re-layouts: 0.91 us -> 0.01 us
  transfers between devices with their start and end apart: 0 -> 1, of which waited for: 0 -> 1; matrix products, arithmetic and copies ran while one was open for 0% -> 0% of each run, Pallas kernels for 0% -> 0%
where the time goes in v6:
time: 83.9 us; the launch traced here: 83.5 us
  blocking collectives  53.1 us (63%)
  waiting for transfers between devices  13.2 us (16%)
  starting transfers between devices  9.34 us (11%)
  other arithmetic  3.44 us (4%)
  Pallas kernels  3 us (4%)
  between operations  1.39 us (2%)
    all_to_all x3, blocking collectives, exchanged(): return lax.all_to_all(blocks, axis, split_axis=0, concat_axis=0, tiled=True)  53.1 us
    all_to_all x1, waiting for transfers between devices, exchanged(): return lax.all_to_all(blocks, axis, split_axis=0, concat_axis=0, tiled=True)  13.2 us
    all_to_all x1, starting transfers between devices, exchanged(): return lax.all_to_all(blocks, axis, split_axis=0, concat_axis=0, tiled=True)  9.34 us
    pallas_call x1, Pallas kernels, decoded_deltas(): pl.pallas_call(encode_kernel, grid=(rows // tall,), in_specs=[spec, spec]...  3 us
  transfers between devices with their start and end apart: 1, of which 1 were waited for; matrix products, arithmetic and copies ran while one was open for 0% of the time, Pallas kernels for 0%

profile of v6, /device:TPU:8, one launch (start us, length us, event | category | flops | bytes accessed | tf_op | source)
XLA Modules:
  0.0 83.5 jit_solution(16795278354487290444)
XLA Ops:
  0.6 0.0 copy-start.1
  0.6 3.0 %shard_map.58 = bf16[256,1024]{1,0:T(8,128)(2,1)} custom-call(f32[256,1024]{1,0:T(8,128)} %base_ref.1, bf16[256,1024]{1,0:T(8,128)(2,1)} %bitcast.12), custom_call_target="tpu_custom_call" | custom-call | flops 5242880 | bytes 2097152 | tf_op jit(solution)/shard_map/pallas_call | solution.py:65
  3.6 0.0 copy-start
  3.6 9.3 %all-to-all-start = ((bf16[16,16,1024]{2,1,0:T(8,128)(2,1)}), bf16[16,16,1024]{2,1,0:T(8,128)(2,1)S(1)}, u32[]{:S(2)}, u32[]{:S(2)}) async-start(bf16[16,16,1024]{2,1,0:T(8,128)(2,1)} %bitcast.13), calls=%async_computation | async-start | bytes 1048576 | tf_op jit(solution)/shard_map/all_to_all | solution.py:30
  13.0 0.0 copy-done.1
  13.0 0.0 copy-done
  13.0 0.2 add_multiply_fusion
  13.2 13.2 %all-to-all-done = bf16[16,16,1024]{2,1,0:T(8,128)(2,1)S(1)} async-done(((bf16[16,16,1024]{2,1,0:T(8,128)(2,1)}), bf16[16,16,1024]{2,1,0:T(8,128)(2,1)S(1)}, u32[]{:S(2)}, u32[]{:S(2)}) %all-to-all-start) | async-done | bytes 524320 | tf_op jit(solution)/shard_map/all_to_all | solution.py:30
  26.4 0.1 convert_reduce_fusion
  26.5 22.1 %all_to_all.20 = f32[32,8,128]{2,1,0:T(8,128)S(1)} all-to-all(f32[32,8,128]{2,1,0:T(8,128)S(1)} %broadcast_in_dim.12), channel_id=1, replica_groups=mesh['replica_0'=4,'replica_1'=4,'fsdp_0'=8,'fsdp_1'=2,'fsdp_2'=2] {'rep..., dimensions={0} | all-to-all | bytes 262144 | tf_op jit(solution)/shard_map/all_to_all | solution.py:30
  48.6 11.5 %all_to_all.21 = f32[16,8,128]{2,1,0:T(8,128)S(1)} all-to-all(f32[16,8,128]{2,1,0:T(8,128)S(1)} %broadcast_in_dim.13), channel_id=1, replica_groups=mesh['replica_0'=4,'replica_1'=4,'fsdp_0'=8,'fsdp_1'=2,'fsdp_2'=2] {'fsd..., dimensions={0} | all-to-all | bytes 131072 | tf_op jit(solution)/shard_map/all_to_all | solution.py:30
  60.1 0.0 copy-start.2
  60.1 0.6 reduce_sum.39
  61.4 0.0 copy-done.2
  61.4 0.6 multiply_convert_fusion
  62.1 0.1 broadcast_in_dim.14
  62.1 19.5 %all_to_all.22 = f16[16,16,1024]{2,1,0:T(8,128)(2,1)S(1)} all-to-all(f16[16,16,1024]{2,1,0:T(8,128)(2,1)S(1)} %broadcast_in_dim.14), channel_id=1, replica_groups=mesh['replica_0'=4,'replica_1'=4,'fsdp_0'=8,'fsdp_1'=2,'fsdp_2'=2] {'rep..., dimensions={0} | all-to-all | bytes 1048576 | tf_op jit(solution)/shard_map/all_to_all | solution.py:30
  81.7 0.3 convert_multiply_fusion
  81.9 1.6 %fusion = (bf16[256,1024]{1,0:T(8,128)(2,1)}, f32[256,1024]{1,0:T(8,128)}) fusion(f32[256,1024]{1,0:T(8,128)S(1)} %add_multiply_fusion, f32[16,16,1024]{2,1,0:T(8,128)S(1)} %get-tuple-element.9, f32[256,1024]{1,0:T(8,128)S(1)} %copy-done, f32[16,16,1024]{2,1,0:T(8,128)S(1)} %get-tuple-element.10), kind=kLoop, calls=%fused_computation.3 | loop fusion | flops 786432 | bytes 5767168 | tf_op jit(solution)/shard_map/convert_element_type | solution.py:101
  (4 shorter events, 0.1 us)
Async XLA Ops:
  0.6 12.4 %copy-start.1 = (bf16[1,256,1024]{2,1,0:T(8,128)(2,1)S(1)}, bf16[1,256,1024]{2,1,0:T(8,128)(2,1)}, u32[]{:S(2)}) copy-start(bf16[1,256,1024]{2,1,0:T(8,128)(2,1)} %param.4) | copy-start | bytes 1572868
  3.6 9.3 %copy-start = (f32[256,1024]{1,0:T(8,128)S(1)}, f32[256,1024]{1,0:T(8,128)}, u32[]{:S(2)}) copy-start(f32[256,1024]{1,0:T(8,128)} %base_ref.1) | copy-start | bytes 3145732
  3.6 22.8 %all-to-all-start = ((bf16[16,16,1024]{2,1,0:T(8,128)(2,1)}), bf16[16,16,1024]{2,1,0:T(8,128)(2,1)S(1)}, u32[]{:S(2)}, u32[]{:S(2)}) async-start(bf16[16,16,1024]{2,1,0:T(8,128)(2,1)} %bitcast.13), calls=%async_computation | async-start | bytes 1048576 | tf_op jit(solution)/shard_map/all_to_all | solution.py:30
  60.1 1.3 %copy-start.2 = (f32[16,1024]{1,0:T(8,128)S(1)}, f32[16,1024]{1,0:T(8,128)}, u32[]{:S(2)}) copy-start(f32[16,1024]{1,0:T(8,128)} %param.5) | copy-start | bytes 196612

commit v7 on v4

--- a/solution.py
+++ b/solution.py
@@ -58,7 +58,7 @@
 
 def decoded_deltas(base_weights, replica_copy):
     rows, columns = base_weights.shape
-    tall = 64
+    tall = rows // 2
     spec = pl.BlockSpec((tall, columns), lambda i: (i, 0))
     return pl.pallas_call(
         encode_kernel,
@@ -87,24 +87,7 @@
 
 
 def gathered(value, axis):
-    size, place = lax.axis_size(axis), lax.axis_index(axis)
-    seen = [value] + [
-        lax.ppermute(value, axis, [(i, (i + far) % size) for i in range(size)])
-        for far in range(1, size)
-    ]
-    ordered = []
-    for at in range(size):
-        block = seen[0]
-        for far in range(1, size):
-            block = jnp.where(lax.rem(place - at + size, size) == far, seen[far], block)
-        ordered.append(block)
-    return jnp.stack(ordered)
-
-
-def beside(task, value):
-    shape = jax.eval_shape(task, value)
-    held = value.reshape(-1)[0].astype(jnp.float32) < 1e30
-    return lax.cond(held, task, lambda v: jnp.zeros(shape.shape, shape.dtype), value)
+    return lax.all_gather(value, axis, axis=0, tiled=False)
 
 
 def shards(base_weights, inner_weights, momentum):
@@ -114,25 +97,22 @@
     replica_copy = inner_weights[0]
     together = lax.optimization_barrier
 
-    decoded, momenta = together(
-        (decoded_deltas(base_weights, replica_copy), in_half(momentum, momentum_unit))
-    )
+    decoded, momenta = together((decoded_deltas(base_weights, replica_copy), momentum))
     arrived = exchanged(decoded.reshape(replicas, owned_rows, columns), REPLICA)
-    momenta = beside(lambda v: gathered(v, REPLICA[0]), momenta)
+    momenta = gathered(in_half(momenta, momentum_unit), REPLICA[0])
     arrived, momenta = together((arrived, momenta))
     outer_grad = arrived.astype(jnp.float32).sum(axis=0) / replicas
 
     grads, momenta = together((in_half(outer_grad, grad_unit), momenta))
     grads = to_everyone(grads, REPLICA).reshape(local_rows, columns)
-    momenta = beside(lambda v: gathered(v, REPLICA[1]), momenta)
-    grads, momenta = together((grads, momenta))
+    momenta = gathered(momenta, REPLICA[1])
+    momenta = jnp.swapaxes(momenta, 0, 1).reshape(local_rows, columns)
+    start = base_weights - (outer_rate * outer_momentum * outer_momentum) * from_half(
+        momenta, momentum_unit
+    )
+    grads, start = together((grads, start))
 
     squares = to_everyone(partial_squares(from_half(grads, grad_unit)), FSDP)
-    momenta = jnp.swapaxes(momenta, 0, 1).reshape(local_rows, columns)
-    start = together(
-        base_weights
-        - (outer_rate * outer_momentum * outer_momentum) * from_half(momenta, momentum_unit)
-    )
     grad_sq = squares.sum()
     clip_factor = jnp.minimum(1.0, clip_rms / jnp.sqrt(grad_sq / (D * KVW) + epsilon))
     new_momentum = outer_momentum * momentum + clip_factor * outer_grad

time: 85.7 us -> 87.5 us (1.021)
  the two profiles are of different devices: /device:TPU:16 before, /device:TPU:1 now
where the time goes in v7:
time: 87.5 us; the launch traced here: 87 us
  blocking collectives  63.9 us (73%)
  starting transfers between devices  13.3 us (15%)
  other arithmetic  3.38 us (4%)
  Pallas kernels  2.94 us (3%)
  local copies, waits for them, and re-layouts  2.09 us (2%)
  between operations  1.42 us (2%)
    all_to_all x1, blocking collectives, exchanged(): return lax.all_to_all(blocks, axis, split_axis=0, concat_axis=0, tiled=True)  32.6 us
    all_gather x2, blocking collectives, gathered(): return lax.all_gather(value, axis, axis=0, tiled=False)  31.3 us
    all_to_all x2, starting transfers between devices, exchanged(): return lax.all_to_all(blocks, axis, split_axis=0, concat_axis=0, tiled=True)  13.3 us
    pallas_call x1, Pallas kernels, decoded_deltas(): pl.pallas_call(encode_kernel, grid=(rows // tall,), in_specs=[spec, spec]...  2.94 us
  transfers between devices with their start and end apart: 2, of which 0 were waited for; matrix products, arithmetic and copies ran while one was open for 0% of the time, Pallas kernels for 0%

profile of v7, /device:TPU:1, one launch (start us, length us, event | category | flops | bytes accessed | tf_op | source)
XLA Modules:
  0.0 87.0 jit_solution(17083107507178189993)
XLA Ops:
  0.6 2.9 %shard_map.58 = bf16[256,1024]{1,0:T(8,128)(2,1)} custom-call(f32[256,1024]{1,0:T(8,128)} %base_ref.1, bf16[256,1024]{1,0:T(8,128)(2,1)} %bitcast.20), custom_call_target="tpu_custom_call" | custom-call | flops 5242880 | bytes 2097152 | tf_op jit(solution)/shard_map/pallas_call | solution.py:63
  3.6 0.0 copy-start.2
  3.6 8.1 %all-to-all-start = ((bf16[16,16,1024]{2,1,0:T(8,128)(2,1)}), bf16[16,16,1024]{2,1,0:T(8,128)(2,1)S(1)}, u32[]{:S(2)}, u32[]{:S(2)}) async-start(bf16[16,16,1024]{2,1,0:T(8,128)(2,1)} %bitcast.19), calls=%async_computation | async-start | bytes 1048576 | tf_op jit(solution)/shard_map/all_to_all | solution.py:28
  11.7 0.0 copy-done.2
  11.7 18.1 %all-gather = f16[64,1024]{1,0:T(8,128)(2,1)S(1)} all-gather(f16[16,1024]{1,0:T(8,128)(2,1)S(1)} %multiply_convert_fusion.2), channel_id=2, replica_groups=mesh['replica_0'=4,'replica_1'=4,'fsdp_0'=8,'fsdp_1'=2,'fsdp_2'=2] {'rep..., dimensions={0}, use_global_device_ids=true | all-gather | bytes 163840 | tf_op jit(solution)/shard_map/all_gather | solution.py:90
  29.9 0.0 all-to-all-done
  29.9 0.1 convert_reduce_fusion
  30.0 0.9 broadcast_in_dim.9
  30.8 5.2 %all-to-all-start.1 = ((f16[16,16,1024]{2,1,0:T(8,128)(2,1)}), f16[16,16,1024]{2,1,0:T(8,128)(2,1)S(1)}, u32[]{:S(2)}, u32[]{:S(2)}) async-start(f16[16,16,1024]{2,1,0:T(8,128)(2,1)} %broadcast_in_dim.9), calls=%async_computation.1 | async-start | bytes 1048576 | tf_op jit(solution)/shard_map/all_to_all | solution.py:28
  36.1 13.2 %all-gather.1 = f16[16,16,1024]{2,1,0:T(8,128)(2,1)S(1)} all-gather(f16[4,16,1024]{2,1,0:T(8,128)(2,1)S(1)} %bitcast.21), channel_id=3, replica_groups=mesh['replica_0'=4,'replica_1'=4,'fsdp_0'=8,'fsdp_1'=2,'fsdp_2'=2] {'rep..., dimensions={0}, use_global_device_ids=true | all-gather | bytes 655360 | tf_op jit(solution)/shard_map/all_gather | solution.py:90
  49.2 0.1 convert_multiply_fusion.2
  49.4 0.0 copy-start
  49.4 0.1 copy.8
  49.5 1.1 %copy-done = f32[256,1024]{1,0:T(8,128)S(1)} copy-done((f32[256,1024]{1,0:T(8,128)S(1)}, f32[256,1024]{1,0:T(8,128)}, u32[]{:S(2)}) %copy-start) | copy-done | bytes 1048600
  50.6 0.2 bitcast_subtract_fusion
  50.8 0.0 all-to-all-done.1
  50.8 0.0 copy-start.1
  50.8 0.3 fusion.2
  51.1 32.6 %all_to_all.15 = f32[32,8,128]{2,1,0:T(8,128)S(1)} all-to-all(f32[32,8,128]{2,1,0:T(8,128)S(1)} %broadcast_in_dim.10), channel_id=1, replica_groups=mesh['replica_0'=4,'replica_1'=4,'fsdp_0'=8,'fsdp_1'=2,'fsdp_2'=2] {'fsd..., dimensions={0} | all-to-all | bytes 262144 | tf_op jit(solution)/shard_map/all_to_all | solution.py:28
  83.7 0.6 reduce_sum.29
  85.0 0.6 multiply_add_fusion
  85.6 0.0 copy-done.1
  85.6 1.4 %fusion.4 = (bf16[1,256,1024]{2,1,0:T(8,128)(2,1)}, f32[256,1024]{1,0:T(8,128)}) fusion(bf16[1,256,1024]{2,1,0:T(8,128)(2,1)S(1)} %copy-done.1, f32[256,1024]{1,0:T(8,128)S(1)} %bitcast_subtract_fusion, f16[256,1024]{1,0:T(8,128)(2,1)S(1)} %bitcast.17, f32[]{:T(128)S(6)} %mul_shard_map.3), kind=kLoop, calls=%fused_computation.10 | loop fusion | flops 1835008 | bytes 3670020 | tf_op jit(solution)/shard_map/broadcast_in_dim | solution.py:122
  (3 shorter events, 0.0 us)
Async XLA Ops:
  3.6 8.1 %copy-start.2 = (f32[16,1024]{1,0:T(8,128)S(1)}, f32[16,1024]{1,0:T(8,128)}, u32[]{:S(2)}) copy-start(f32[16,1024]{1,0:T(8,128)} %param.5) | copy-start | bytes 196612
  3.6 26.3 %all-to-all-start = ((bf16[16,16,1024]{2,1,0:T(8,128)(2,1)}), bf16[16,16,1024]{2,1,0:T(8,128)(2,1)S(1)}, u32[]{:S(2)}, u32[]{:S(2)}) async-start(bf16[16,16,1024]{2,1,0:T(8,128)(2,1)} %bitcast.19), calls=%async_computation | async-start | bytes 1048576 | tf_op jit(solution)/shard_map/all_to_all | solution.py:28
  30.8 20.0 %all-to-all-start.1 = ((f16[16,16,1024]{2,1,0:T(8,128)(2,1)}), f16[16,16,1024]{2,1,0:T(8,128)(2,1)S(1)}, u32[]{:S(2)}, u32[]{:S(2)}) async-start(f16[16,16,1024]{2,1,0:T(8,128)(2,1)} %broadcast_in_dim.9), calls=%async_computation.1 | async-start | bytes 1048576 | tf_op jit(solution)/shard_map/all_to_all | solution.py:28
  49.4 1.2 %copy-start = (f32[256,1024]{1,0:T(8,128)S(1)}, f32[256,1024]{1,0:T(8,128)}, u32[]{:S(2)}) copy-start(f32[256,1024]{1,0:T(8,128)} %base_ref.1) | copy-start | bytes 3145732
  50.8 34.8 %copy-start.1 = (bf16[1,256,1024]{2,1,0:T(8,128)(2,1)S(1)}, bf16[1,256,1024]{2,1,0:T(8,128)(2,1)}, u32[]{:S(2)}) copy-start(bf16[1,256,1024]{2,1,0:T(8,128)(2,1)} %param.4) | copy-start | bytes 1572868

commit v8 on v6

--- a/solution.py
+++ b/solution.py
@@ -12,8 +12,8 @@
 REPLICA = ("replica_0", "replica_1")
 FSDP = ("fsdp_0", "fsdp_1", "fsdp_2")
 FSDP_REPLICA = ("fsdp_0", "fsdp_1", "fsdp_2", "replica_0", "replica_1")
+RING = ("fsdp_1", "replica_0", "fsdp_2")
 PLANE = ("replica_1", "fsdp_0")
-RING = ("fsdp_1", "replica_0", "fsdp_2")
 
 code_limit = 448.0
 outer_rate = 0.7
@@ -74,10 +74,15 @@
     )(base_weights, replica_copy)
 
 
-def partial_squares(value):
+def lane_squares(value):
     rows, columns = value.shape
     tiles = (value * value).reshape(rows // 8, 8, columns // 128, 128)
-    return tiles.sum(axis=(0, 2))
+    return tiles.sum(axis=(0, 1, 2))[None]
+
+
+def lane_total(lanes, columns):
+    ones = jnp.ones((lanes.shape[1], columns), lanes.dtype)
+    return lax.dot(lanes, ones, precision=lax.Precision.HIGHEST)
 
 
 def shards(base_weights, inner_weights, momentum):
@@ -90,14 +95,16 @@
     blended = blend_share * replica_copy.astype(jnp.float32) + (1.0 - blend_share) * base_weights
     arrived, blended = lax.optimization_barrier((arrived, blended))
     outer_grad = arrived.astype(jnp.float32).sum(axis=0) / replicas
-    squares = to_everyone(partial_squares(outer_grad), PLANE).sum(axis=0)
-    grad_sq = to_everyone(squares, RING).sum()
+    squares = to_everyone(lane_squares(outer_grad), RING).sum(axis=0)
+    squares = to_everyone(squares, PLANE).sum(axis=0)
+    grad_sq = lane_total(squares, columns)
     clip_factor = jnp.minimum(1.0, clip_rms / jnp.sqrt(grad_sq / (D * KVW) + epsilon))
     step_term = clip_factor * outer_grad
     new_momentum = outer_momentum * momentum + step_term
     step = outer_rate * (step_term + outer_momentum * new_momentum)
     steps = to_everyone((step * step_unit).astype(jnp.float16), REPLICA)
-    steps = steps.reshape(local_rows, columns).astype(jnp.float32) * (1.0 / step_unit)
+    steps = lax.optimization_barrier(steps.reshape(local_rows, columns))
+    steps = steps.astype(jnp.float32) * (1.0 / step_unit)
     new_inner = (blended - (1.0 - blend_share) * steps).astype(jnp.bfloat16)
     return (base_weights - steps, new_momentum, new_inner[None])
 

time: 83.9 us -> 80.4 us (0.958)
  blocking collectives: 53.1 us -> 50.3 us
  other arithmetic: 3.44 us -> 2.51 us
    all_to_all x3, blocking collectives: 53.1 us -> 50.3 us  [exchanged(): return lax.all_to_all(blocks, axis, split_axis=0, concat_axis=0, tiled=True)]
    convert_element_type x1 -> x0, other arithmetic: 1.6 us -> none  [shards(): new_inner = (blended - (1.0 - blend_share) * steps).astype(jnp.bfloat16)]
    broadcast_in_dim x0 -> x1, other arithmetic: none -> 1.51 us  [shards(): return (base_weights - steps, new_momentum, new_inner[None])]
where the time goes in v8:
time: 80.4 us; the launch traced here: 80 us
  blocking collectives  50.3 us (63%)
  waiting for transfers between devices  13.2 us (16%)
  starting transfers between devices  9.34 us (12%)
  Pallas kernels  3 us (4%)
  other arithmetic  2.51 us (3%)
    all_to_all x3, blocking collectives, exchanged(): return lax.all_to_all(blocks, axis, split_axis=0, concat_axis=0, tiled=True)  50.3 us
    all_to_all x1, waiting for transfers between devices, exchanged(): return lax.all_to_all(blocks, axis, split_axis=0, concat_axis=0, tiled=True)  13.2 us
    all_to_all x1, starting transfers between devices, exchanged(): return lax.all_to_all(blocks, axis, split_axis=0, concat_axis=0, tiled=True)  9.34 us
    pallas_call x1, Pallas kernels, decoded_deltas(): pl.pallas_call(encode_kernel, grid=(rows // tall,), in_specs=[spec, spec]...  3 us
  transfers between devices with their start and end apart: 1, of which 1 were waited for; matrix products, arithmetic and copies ran while one was open for 0% of the time, Pallas kernels for 0%

profile of v8, /device:TPU:8, one launch (start us, length us, event | category | flops | bytes accessed | tf_op | source)
XLA Modules:
  0.0 80.0 jit_solution(6916212853284517920)
XLA Ops:
  0.6 0.0 copy-start.1
  0.6 3.0 %shard_map.58 = bf16[256,1024]{1,0:T(8,128)(2,1)} custom-call(f32[256,1024]{1,0:T(8,128)} %base_ref.1, bf16[256,1024]{1,0:T(8,128)(2,1)} %bitcast.14), custom_call_target="tpu_custom_call" | custom-call | flops 5242880 | bytes 2097152 | tf_op jit(solution)/shard_map/pallas_call | solution.py:65
  3.6 0.0 copy-start
  3.6 9.3 %all-to-all-start = ((bf16[16,16,1024]{2,1,0:T(8,128)(2,1)}), bf16[16,16,1024]{2,1,0:T(8,128)(2,1)S(1)}, u32[]{:S(2)}, u32[]{:S(2)}) async-start(bf16[16,16,1024]{2,1,0:T(8,128)(2,1)} %bitcast.15), calls=%async_computation | async-start | bytes 1048576 | tf_op jit(solution)/shard_map/all_to_all | solution.py:30
  13.0 0.0 copy-done.1
  13.0 0.0 copy-done
  13.0 0.2 add_multiply_fusion
  13.2 13.2 %all-to-all-done = bf16[16,16,1024]{2,1,0:T(8,128)(2,1)S(1)} async-done(((bf16[16,16,1024]{2,1,0:T(8,128)(2,1)}), bf16[16,16,1024]{2,1,0:T(8,128)(2,1)S(1)}, u32[]{:S(2)}, u32[]{:S(2)}) %all-to-all-start) | async-done | bytes 524320 | tf_op jit(solution)/shard_map/all_to_all | solution.py:30
  26.4 0.1 convert_reduce_fusion
  26.5 11.1 %all_to_all.20 = f32[16,1,128]{2,1,0:T(1,128)S(1)} all-to-all(f32[16,1,128]{2,1,0:T(1,128)S(1)} %broadcast_in_dim.16), channel_id=1, replica_groups=mesh['replica_0'=4,'replica_1'=4,'fsdp_0'=8,'fsdp_1'=2,'fsdp_2'=2] {'fsd..., dimensions={0} | all-to-all | bytes 16384 | tf_op jit(solution)/shard_map/all_to_all | solution.py:30
  37.7 21.5 %all_to_all.21 = f32[32,1,128]{2,1,0:T(1,128)S(1)} all-to-all(f32[32,1,128]{2,1,0:T(1,128)S(1)} %broadcast_in_dim.17), channel_id=1, replica_groups=mesh['replica_0'=4,'replica_1'=4,'fsdp_0'=8,'fsdp_1'=2,'fsdp_2'=2] {'rep..., dimensions={0} | all-to-all | bytes 32768 | tf_op jit(solution)/shard_map/all_to_all | solution.py:30
  59.3 0.0 copy-start.2
  59.3 0.2 fusion.4
  59.5 0.6 copy-done.2
  60.1 0.6 multiply_convert_fusion
  60.7 0.1 broadcast_in_dim.19
  60.8 17.7 %all_to_all.22 = f16[16,16,1024]{2,1,0:T(8,128)(2,1)S(1)} all-to-all(f16[16,16,1024]{2,1,0:T(8,128)(2,1)S(1)} %broadcast_in_dim.19), channel_id=1, replica_groups=mesh['replica_0'=4,'replica_1'=4,'fsdp_0'=8,'fsdp_1'=2,'fsdp_2'=2] {'rep..., dimensions={0} | all-to-all | bytes 1048576 | tf_op jit(solution)/shard_map/all_to_all | solution.py:30
  78.5 1.5 %fusion.3 = (bf16[1,256,1024]{2,1,0:T(8,128)(2,1)}, f32[256,1024]{1,0:T(8,128)}) fusion(f32[256,1024]{1,0:T(8,128)S(1)} %add_multiply_fusion, f16[256,1024]{1,0:T(8,128)(2,1)S(1)} %bitcast.16, f32[256,1024]{1,0:T(8,128)S(1)} %copy-done), kind=kLoop, calls=%fused_computation.7 | loop fusion | flops 1572864 | bytes 4194304 | tf_op jit(solution)/shard_map/broadcast_in_dim | solution.py:109
  (7 shorter events, 0.1 us)
Async XLA Ops:
  0.6 12.4 %copy-start.1 = (bf16[1,256,1024]{2,1,0:T(8,128)(2,1)S(1)}, bf16[1,256,1024]{2,1,0:T(8,128)(2,1)}, u32[]{:S(2)}) copy-start(bf16[1,256,1024]{2,1,0:T(8,128)(2,1)} %param.4) | copy-start | bytes 1572868
  3.6 9.3 %copy-start = (f32[256,1024]{1,0:T(8,128)S(1)}, f32[256,1024]{1,0:T(8,128)}, u32[]{:S(2)}) copy-start(f32[256,1024]{1,0:T(8,128)} %base_ref.1) | copy-start | bytes 3145732
  3.6 22.8 %all-to-all-start = ((bf16[16,16,1024]{2,1,0:T(8,128)(2,1)}), bf16[16,16,1024]{2,1,0:T(8,128)(2,1)S(1)}, u32[]{:S(2)}, u32[]{:S(2)}) async-start(bf16[16,16,1024]{2,1,0:T(8,128)(2,1)} %bitcast.15), calls=%async_computation | async-start | bytes 1048576 | tf_op jit(solution)/shard_map/all_to_all | solution.py:30
  59.3 0.8 %copy-start.2 = (f32[16,1024]{1,0:T(8,128)S(1)}, f32[16,1024]{1,0:T(8,128)}, u32[]{:S(2)}) copy-start(f32[16,1024]{1,0:T(8,128)} %param.5) | copy-start | bytes 196612

commit v9 on v8

--- a/solution.py
+++ b/solution.py
@@ -93,14 +93,15 @@
     decoded = decoded_deltas(base_weights, replica_copy)
     arrived = exchanged(decoded.reshape(replicas, owned_rows, columns), REPLICA)
     blended = blend_share * replica_copy.astype(jnp.float32) + (1.0 - blend_share) * base_weights
-    arrived, blended = lax.optimization_barrier((arrived, blended))
+    kept = outer_momentum * momentum
+    arrived, blended, kept = lax.optimization_barrier((arrived, blended, kept))
     outer_grad = arrived.astype(jnp.float32).sum(axis=0) / replicas
     squares = to_everyone(lane_squares(outer_grad), RING).sum(axis=0)
     squares = to_everyone(squares, PLANE).sum(axis=0)
     grad_sq = lane_total(squares, columns)
     clip_factor = jnp.minimum(1.0, clip_rms / jnp.sqrt(grad_sq / (D * KVW) + epsilon))
     step_term = clip_factor * outer_grad
-    new_momentum = outer_momentum * momentum + step_term
+    new_momentum = kept + step_term
     step = outer_rate * (step_term + outer_momentum * new_momentum)
     steps = to_everyone((step * step_unit).astype(jnp.float16), REPLICA)
     steps = lax.optimization_barrier(steps.reshape(local_rows, columns))

time: 80.4 us -> 79.7 us (level)
  no operation moved by 1% of the time
where the time goes in v9:
time: 79.7 us; the launch traced here: 79.4 us
  blocking collectives  50.3 us (63%)
  waiting for transfers between devices  13.2 us (17%)
  starting transfers between devices  9.34 us (12%)
  Pallas kernels  3 us (4%)
  other arithmetic  2.44 us (3%)
    all_to_all x3, blocking collectives, exchanged(): return lax.all_to_all(blocks, axis, split_axis=0, concat_axis=0, tiled=True)  50.3 us
    all_to_all x1, waiting for transfers between devices, exchanged(): return lax.all_to_all(blocks, axis, split_axis=0, concat_axis=0, tiled=True)  13.2 us
    all_to_all x1, starting transfers between devices, exchanged(): return lax.all_to_all(blocks, axis, split_axis=0, concat_axis=0, tiled=True)  9.34 us
    pallas_call x1, Pallas kernels, decoded_deltas(): pl.pallas_call(encode_kernel, grid=(rows // tall,), in_specs=[spec, spec]...  3 us
  transfers between devices with their start and end apart: 1, of which 1 were waited for; matrix products, arithmetic and copies ran while one was open for 0% of the time, Pallas kernels for 0%

profile of v9, /device:TPU:8, one launch (start us, length us, event | category | flops | bytes accessed | tf_op | source)
XLA Modules:
  0.0 79.4 jit_solution(6931379379617574347)
XLA Ops:
  0.6 0.0 copy-start.2
  0.6 0.0 copy-start.1
  0.7 3.0 %shard_map.58 = bf16[256,1024]{1,0:T(8,128)(2,1)} custom-call(f32[256,1024]{1,0:T(8,128)} %base_ref.1, bf16[256,1024]{1,0:T(8,128)(2,1)} %bitcast.14), custom_call_target="tpu_custom_call" | custom-call | flops 5242880 | bytes 2097152 | tf_op jit(solution)/shard_map/pallas_call | solution.py:65
  3.7 0.0 copy-start
  3.7 9.3 %all-to-all-start = ((bf16[16,16,1024]{2,1,0:T(8,128)(2,1)}), bf16[16,16,1024]{2,1,0:T(8,128)(2,1)S(1)}, u32[]{:S(2)}, u32[]{:S(2)}) async-start(bf16[16,16,1024]{2,1,0:T(8,128)(2,1)} %bitcast.15), calls=%async_computation | async-start | bytes 1048576 | tf_op jit(solution)/shard_map/all_to_all | solution.py:30
  13.0 0.0 copy-done.2
  13.0 0.0 copy-done.1
  13.0 0.0 copy-done
  13.0 0.1 add_multiply_fusion
  13.2 13.2 %all-to-all-done = bf16[16,16,1024]{2,1,0:T(8,128)(2,1)S(1)} async-done(((bf16[16,16,1024]{2,1,0:T(8,128)(2,1)}), bf16[16,16,1024]{2,1,0:T(8,128)(2,1)S(1)}, u32[]{:S(2)}, u32[]{:S(2)}) %all-to-all-start) | async-done | bytes 524320 | tf_op jit(solution)/shard_map/all_to_all | solution.py:30
  26.4 0.1 convert_reduce_fusion
  26.6 11.1 %all_to_all.20 = f32[16,1,128]{2,1,0:T(1,128)S(1)} all-to-all(f32[16,1,128]{2,1,0:T(1,128)S(1)} %broadcast_in_dim.16), channel_id=1, replica_groups=mesh['replica_0'=4,'replica_1'=4,'fsdp_0'=8,'fsdp_1'=2,'fsdp_2'=2] {'fsd..., dimensions={0} | all-to-all | bytes 16384 | tf_op jit(solution)/shard_map/all_to_all | solution.py:30
  37.7 21.5 %all_to_all.21 = f32[32,1,128]{2,1,0:T(1,128)S(1)} all-to-all(f32[32,1,128]{2,1,0:T(1,128)S(1)} %broadcast_in_dim.17), channel_id=1, replica_groups=mesh['replica_0'=4,'replica_1'=4,'fsdp_0'=8,'fsdp_1'=2,'fsdp_2'=2] {'rep..., dimensions={0} | all-to-all | bytes 32768 | tf_op jit(solution)/shard_map/all_to_all | solution.py:30
  59.3 0.2 fusion.4
  59.5 0.7 multiply_convert_fusion
  60.2 0.1 broadcast_in_dim.19
  60.2 17.7 %all_to_all.22 = f16[16,16,1024]{2,1,0:T(8,128)(2,1)S(1)} all-to-all(f16[16,16,1024]{2,1,0:T(8,128)(2,1)S(1)} %broadcast_in_dim.19), channel_id=1, replica_groups=mesh['replica_0'=4,'replica_1'=4,'fsdp_0'=8,'fsdp_1'=2,'fsdp_2'=2] {'rep..., dimensions={0} | all-to-all | bytes 1048576 | tf_op jit(solution)/shard_map/all_to_all | solution.py:30
  77.9 1.5 %fusion.3 = (bf16[1,256,1024]{2,1,0:T(8,128)(2,1)}, f32[256,1024]{1,0:T(8,128)}) fusion(f32[256,1024]{1,0:T(8,128)S(1)} %add_multiply_fusion, f16[256,1024]{1,0:T(8,128)(2,1)S(1)} %bitcast.16, f32[256,1024]{1,0:T(8,128)S(1)} %copy-done), kind=kLoop, calls=%fused_computation.7 | loop fusion | flops 1572864 | bytes 4194304 | tf_op jit(solution)/shard_map/broadcast_in_dim | solution.py:110
  (8 shorter events, 0.1 us)
Async XLA Ops:
  0.6 12.4 %copy-start.2 = (f32[16,1024]{1,0:T(8,128)S(1)}, f32[16,1024]{1,0:T(8,128)}, u32[]{:S(2)}) copy-start(f32[16,1024]{1,0:T(8,128)} %param.5) | copy-start | bytes 196612
  0.6 12.4 %copy-start.1 = (bf16[1,256,1024]{2,1,0:T(8,128)(2,1)S(1)}, bf16[1,256,1024]{2,1,0:T(8,128)(2,1)}, u32[]{:S(2)}) copy-start(bf16[1,256,1024]{2,1,0:T(8,128)(2,1)} %param.4) | copy-start | bytes 1572868
  3.7 9.4 %copy-start = (f32[256,1024]{1,0:T(8,128)S(1)}, f32[256,1024]{1,0:T(8,128)}, u32[]{:S(2)}) copy-start(f32[256,1024]{1,0:T(8,128)} %base_ref.1) | copy-start | bytes 3145732
  3.7 22.8 %all-to-all-start = ((bf16[16,16,1024]{2,1,0:T(8,128)(2,1)}), bf16[16,16,1024]{2,1,0:T(8,128)(2,1)S(1)}, u32[]{:S(2)}, u32[]{:S(2)}) async-start(bf16[16,16,1024]{2,1,0:T(8,128)(2,1)} %bitcast.15), calls=%async_computation | async-start | bytes 1048576 | tf_op jit(solution)/shard_map/all_to_all | solution.py:30

commit v10 on v9

--- a/solution.py
+++ b/solution.py
@@ -74,6 +74,54 @@
     )(base_weights, replica_copy)
 
 
+def outputs_kernel(chunk, base_ref, blended_ref, steps_ref, kept_ref, grad_ref, clip_ref, *refs):
+    out_refs, held_refs, sems = refs[:3], refs[3:6], refs[6]
+    base_held, momentum_held, inner_held = held_refs
+
+    def copy(which, part, rows):
+        return pltpu.make_async_copy(
+            held_refs[which].at[rows], out_refs[which].at[rows], sems.at[which, part]
+        )
+
+    copies = []
+    momentum_held[...] = kept_ref[...] + clip_ref[...] * grad_ref[...]
+    copies.append(copy(1, 0, pl.ds(0, momentum_held.shape[0])))
+    copies[-1].start()
+    for part in range(base_held.shape[0] // chunk):
+        rows = pl.ds(part * chunk, chunk)
+        steps = steps_ref[rows]
+        base_held[rows] = base_ref[rows] - steps
+        copies.append(copy(0, part, rows))
+        copies[-1].start()
+        inner_held[rows] = (blended_ref[rows] - (1.0 - blend_share) * steps).astype(jnp.bfloat16)
+        copies.append(copy(2, part, rows))
+        copies[-1].start()
+    for each in copies:
+        each.wait()
+
+
+def outputs(base_weights, blended, steps, kept, outer_grad, clip_factor):
+    rows, columns = base_weights.shape
+    chunk = rows // 4
+    shapes = (
+        jax.ShapeDtypeStruct((rows, columns), jnp.float32),
+        jax.ShapeDtypeStruct(kept.shape, jnp.float32),
+        jax.ShapeDtypeStruct((rows, columns), jnp.bfloat16),
+    )
+    return pl.pallas_call(
+        lambda *refs: outputs_kernel(chunk, *refs),
+        in_specs=[pl.BlockSpec(memory_space=pltpu.VMEM)] * 6,
+        out_specs=[pl.BlockSpec(memory_space=pl.ANY)] * 3,
+        out_shape=shapes,
+        scratch_shapes=[pltpu.VMEM(each.shape, each.dtype) for each in shapes]
+        + [pltpu.SemaphoreType.DMA((3, 4))],
+        compiler_params=pltpu.CompilerParams(vmem_limit_bytes=8 * 2**20),
+        cost_estimate=pl.CostEstimate(
+            flops=4 * rows * columns, bytes_accessed=18 * rows * columns, transcendentals=0
+        ),
+    )(base_weights, blended, steps, kept, outer_grad, clip_factor)
+
+
 def lane_squares(value):
     rows, columns = value.shape
     tiles = (value * value).reshape(rows // 8, 8, columns // 128, 128)
@@ -101,13 +149,13 @@
     grad_sq = lane_total(squares, columns)
     clip_factor = jnp.minimum(1.0, clip_rms / jnp.sqrt(grad_sq / (D * KVW) + epsilon))
     step_term = clip_factor * outer_grad
-    new_momentum = kept + step_term
-    step = outer_rate * (step_term + outer_momentum * new_momentum)
+    step = outer_rate * (step_term + outer_momentum * (kept + step_term))
     steps = to_everyone((step * step_unit).astype(jnp.float16), REPLICA)
-    steps = lax.optimization_barrier(steps.reshape(local_rows, columns))
-    steps = steps.astype(jnp.float32) * (1.0 / step_unit)
-    new_inner = (blended - (1.0 - blend_share) * steps).astype(jnp.bfloat16)
-    return (base_weights - steps, new_momentum, new_inner[None])
+    steps = steps.reshape(local_rows, columns).astype(jnp.float32) * (1.0 / step_unit)
+    new_base, new_momentum, new_inner = outputs(
+        base_weights, blended, steps, kept, outer_grad, clip_factor
+    )
+    return (new_base, new_momentum, new_inner[None])
 
 
 def solution(mesh):

time: 79.7 us -> 79 us (level)
  other arithmetic: 2.44 us -> 0.52 us
  Pallas kernels: 3 us -> 4.28 us
    broadcast_in_dim x1 -> x0, other arithmetic: 1.46 us -> none  [shards(): return (base_weights - steps, new_momentum, new_inner[None])]
    pallas_call x0 -> x1, Pallas kernels: none -> 1.28 us  [outputs(): pl.pallas_call(lambda *refs: outputs_kernel(chunk, *refs), in_specs=[pl.B...]
where the time goes in v10:
time: 79 us; the launch traced here: 78.7 us
  blocking collectives  50.3 us (64%)
  waiting for transfers between devices  13.2 us (17%)
  starting transfers between devices  9.34 us (12%)
  Pallas kernels  4.28 us (5%)
    all_to_all x3, blocking collectives, exchanged(): return lax.all_to_all(blocks, axis, split_axis=0, concat_axis=0, tiled=True)  50.3 us
    all_to_all x1, waiting for transfers between devices, exchanged(): return lax.all_to_all(blocks, axis, split_axis=0, concat_axis=0, tiled=True)  13.2 us
    all_to_all x1, starting transfers between devices, exchanged(): return lax.all_to_all(blocks, axis, split_axis=0, concat_axis=0, tiled=True)  9.34 us
    pallas_call x1, Pallas kernels, decoded_deltas(): pl.pallas_call(encode_kernel, grid=(rows // tall,), in_specs=[spec, spec]...  3 us
  transfers between devices with their start and end apart: 1, of which 1 were waited for; matrix products, arithmetic and copies ran while one was open for 0% of the time, Pallas kernels for 0%

profile of v10, /device:TPU:8, one launch (start us, length us, event | category | flops | bytes accessed | tf_op | source)
XLA Modules:
  0.0 78.7 jit_solution(15992431858074271986)
XLA Ops:
  0.6 0.0 copy-start.2
  0.6 0.0 copy-start.1
  0.7 3.0 %shard_map.58 = bf16[256,1024]{1,0:T(8,128)(2,1)} custom-call(f32[256,1024]{1,0:T(8,128)} %refs_0_.1, bf16[256,1024]{1,0:T(8,128)(2,1)} %bitcast.16), custom_call_target="tpu_custom_call" | custom-call | flops 5242880 | bytes 2097152 | tf_op jit(solution)/shard_map/pallas_call | solution.py:65
  3.7 0.0 copy-start
  3.7 9.3 %all-to-all-start = ((bf16[16,16,1024]{2,1,0:T(8,128)(2,1)}), bf16[16,16,1024]{2,1,0:T(8,128)(2,1)S(1)}, u32[]{:S(2)}, u32[]{:S(2)}) async-start(bf16[16,16,1024]{2,1,0:T(8,128)(2,1)} %bitcast.17), calls=%async_computation | async-start | bytes 1048576 | tf_op jit(solution)/shard_map/all_to_all | solution.py:30
  13.0 0.0 copy-done.2
  13.0 0.0 copy-done.1
  13.0 0.0 copy-done
  13.0 0.2 add_multiply_fusion.refs_1_
  13.2 13.2 %all-to-all-done = bf16[16,16,1024]{2,1,0:T(8,128)(2,1)S(1)} async-done(((bf16[16,16,1024]{2,1,0:T(8,128)(2,1)}), bf16[16,16,1024]{2,1,0:T(8,128)(2,1)S(1)}, u32[]{:S(2)}, u32[]{:S(2)}) %all-to-all-start) | async-done | bytes 524320 | tf_op jit(solution)/shard_map/all_to_all | solution.py:30
  26.4 0.1 convert_reduce_fusion
  26.6 11.1 %all_to_all.20 = f32[16,1,128]{2,1,0:T(1,128)S(1)} all-to-all(f32[16,1,128]{2,1,0:T(1,128)S(1)} %broadcast_in_dim.16), channel_id=1, replica_groups=mesh['replica_0'=4,'replica_1'=4,'fsdp_0'=8,'fsdp_1'=2,'fsdp_2'=2] {'fsd..., dimensions={0} | all-to-all | bytes 16384 | tf_op jit(solution)/shard_map/all_to_all | solution.py:30
  37.7 21.5 %all_to_all.21 = f32[32,1,128]{2,1,0:T(1,128)S(1)} all-to-all(f32[32,1,128]{2,1,0:T(1,128)S(1)} %broadcast_in_dim.17), channel_id=1, replica_groups=mesh['replica_0'=4,'replica_1'=4,'fsdp_0'=8,'fsdp_1'=2,'fsdp_2'=2] {'rep..., dimensions={0} | all-to-all | bytes 32768 | tf_op jit(solution)/shard_map/all_to_all | solution.py:30
  59.3 0.2 fusion
  59.6 0.1 broadcast_in_dim.19
  59.6 17.7 %all_to_all.22 = f16[16,16,1024]{2,1,0:T(8,128)(2,1)S(1)} all-to-all(f16[16,16,1024]{2,1,0:T(8,128)(2,1)S(1)} %broadcast_in_dim.19), channel_id=1, replica_groups=mesh['replica_0'=4,'replica_1'=4,'fsdp_0'=8,'fsdp_1'=2,'fsdp_2'=2] {'rep..., dimensions={0} | all-to-all | bytes 1048576 | tf_op jit(solution)/shard_map/all_to_all | solution.py:30
  77.3 0.1 convert_multiply_fusion
  77.4 1.3 %shard_map.59 = (f32[256,1024]{1,0:T(8,128)}, f32[16,1024]{1,0:T(8,128)}, bf16[256,1024]{1,0:T(8,128)(2,1)}) custom-call(f32[256,1024]{1,0:T(8,128)S(1)} %copy-done, f32[256,1024]{1,0:T(8,128)S(1)} %add_multiply_fusion.refs_1_, f32[256,1024]{1,0:T(8,128)S(1)} %bitcast.14, f32[16,1024]{1,0:T(8,128)S(1)} %broadcast_multiply_fusion.1.refs_3_, ...), custom_call_target="tpu_custom_call" | custom-call | flops 1048576 | bytes 4718592 | tf_op jit(solution)/shard_map/pallas_call | solution.py:111
  (9 shorter events, 0.2 us)
Async XLA Ops:
  0.6 12.4 %copy-start.2 = (f32[16,1024]{1,0:T(8,128)S(1)}, f32[16,1024]{1,0:T(8,128)}, u32[]{:S(2)}) copy-start(f32[16,1024]{1,0:T(8,128)} %param.5) | copy-start | bytes 196612
  0.6 12.4 %copy-start.1 = (bf16[1,256,1024]{2,1,0:T(8,128)(2,1)S(1)}, bf16[1,256,1024]{2,1,0:T(8,128)(2,1)}, u32[]{:S(2)}) copy-start(bf16[1,256,1024]{2,1,0:T(8,128)(2,1)} %param.4) | copy-start | bytes 1572868
  3.7 9.4 %copy-start = (f32[256,1024]{1,0:T(8,128)S(1)}, f32[256,1024]{1,0:T(8,128)}, u32[]{:S(2)}) copy-start(f32[256,1024]{1,0:T(8,128)} %refs_0_.1) | copy-start | bytes 3145732
  3.7 22.8 %all-to-all-start = ((bf16[16,16,1024]{2,1,0:T(8,128)(2,1)}), bf16[16,16,1024]{2,1,0:T(8,128)(2,1)S(1)}, u32[]{:S(2)}, u32[]{:S(2)}) async-start(bf16[16,16,1024]{2,1,0:T(8,128)(2,1)} %bitcast.17), calls=%async_computation | async-start | bytes 1048576 | tf_op jit(solution)/shard_map/all_to_all | solution.py:30

commit v11 on v10

--- a/solution.py
+++ b/solution.py
@@ -36,45 +36,69 @@
 
 
 def smallest_scale(peaks):
-    target = peaks * (1.0 / code_limit)
-    spread = target * (2.0**23 + 1.0)
-    scale = spread - (spread - target)
-    scale = jnp.where(code_limit * scale < peaks, 2.0 * scale, scale)
-    return jnp.where(code_limit * (0.5 * scale) >= peaks, 0.5 * scale, scale)
+    spread = peaks * (2.0**23 + 1.0)
+    near = spread - (spread - peaks)
+    return jnp.where(peaks <= (code_limit / 512.0) * near, 0.5 * near, near)
 
 
-def encode_kernel(base_ref, inner_ref, decoded_ref):
-    for at in range(0, base_ref.shape[1], BLOCK):
-        columns = pl.ds(at, BLOCK)
-        deltas = base_ref[:, columns] - inner_ref[:, columns].astype(jnp.float32)
-        magnitude = jnp.abs(deltas)
-        scale = smallest_scale(jnp.max(magnitude, axis=1, keepdims=True) + epsilon)
-        beyond = deltas * (1.0 + 2.0**-23)
-        spread = beyond * (2.0**20 + 1.0)
-        normal = spread - (spread - beyond)
-        anchor = scale * (1.5 * 2.0**14)
-        small = (beyond + anchor) - anchor
-        decoded = jnp.where(magnitude < scale * smallest_normal, small, normal)
-        decoded_ref[:, columns] = decoded.astype(decoded_ref.dtype)
+def encoded(base_block, inner_block):
+    deltas = base_block - inner_block.astype(jnp.float32)
+    magnitude = jnp.abs(deltas)
+    scale = smallest_scale(jnp.max(magnitude, axis=1, keepdims=True) + epsilon)
+    beyond = deltas * (1.0 + 2.0**-23)
+    spread = beyond * (2.0**20 + 1.0)
+    normal = spread - (spread - beyond)
+    anchor = scale * (1.5 * 2.0**6)
+    small = (beyond + anchor) - anchor
+    return jnp.where(magnitude < scale * (smallest_normal / 256.0), small, normal)
+
+
+def encode_kernel(chunk, base_hbm, inner_hbm, decoded_ref, base_ref, inner_ref, sems):
+    parts = range(base_ref.shape[0] // chunk)
+
+    def arriving(part):
+        rows = pl.ds(part * chunk, chunk)
+        return [
+            pltpu.make_async_copy(source.at[rows], target.at[rows], sems.at[which, part])
+            for which, (source, target) in enumerate(
+                [(base_hbm, base_ref), (inner_hbm, inner_ref)]
+            )
+        ]
+
+    for part in parts:
+        for each in arriving(part):
+            each.start()
+    for part in parts:
+        for each in arriving(part):
+            each.wait()
+        rows = pl.ds(part * chunk, chunk)
+        for at in range(0, base_ref.shape[1], BLOCK):
+            lanes = pl.ds(at, BLOCK)
+            decoded = encoded(base_ref[rows, lanes], inner_ref[rows, lanes])
+            decoded_ref[rows, lanes] = decoded.astype(decoded_ref.dtype)
 
 
 def decoded_deltas(base_weights, replica_copy):
     rows, columns = base_weights.shape
-    tall = rows // 2
-    spec = pl.BlockSpec((tall, columns), lambda i: (i, 0))
+    chunk = rows // 4
     return pl.pallas_call(
-        encode_kernel,
-        grid=(rows // tall,),
-        in_specs=[spec, spec],
-        out_specs=spec,
-        out_shape=jax.ShapeDtypeStruct((rows, columns), jnp.bfloat16),
+        lambda *refs: encode_kernel(chunk, *refs),
+        in_specs=[pl.BlockSpec(memory_space=pltpu.HBM)] * 2,
+        out_specs=[pl.BlockSpec(memory_space=pltpu.VMEM)] * 3,
+        out_shape=[
+            jax.ShapeDtypeStruct((rows, columns), jnp.bfloat16),
+            jax.ShapeDtypeStruct((rows, columns), jnp.float32),
+            jax.ShapeDtypeStruct((rows, columns), jnp.bfloat16),
+        ],
+        scratch_shapes=[pltpu.SemaphoreType.DMA((2, 4))],
+        compiler_params=pltpu.CompilerParams(vmem_limit_bytes=51 * 2**20),
         cost_estimate=pl.CostEstimate(
             flops=20 * rows * columns, bytes_accessed=8 * rows * columns, transcendentals=0
         ),
     )(base_weights, replica_copy)
 
 
-def outputs_kernel(chunk, base_ref, blended_ref, steps_ref, kept_ref, grad_ref, clip_ref, *refs):
+def outputs_kernel(chunk, base_ref, inner_ref, steps_ref, kept_ref, grad_ref, clip_ref, *refs):
     out_refs, held_refs, sems = refs[:3], refs[3:6], refs[6]
     base_held, momentum_held, inner_held = held_refs
 
@@ -89,18 +113,19 @@
     copies[-1].start()
     for part in range(base_held.shape[0] // chunk):
         rows = pl.ds(part * chunk, chunk)
-        steps = steps_ref[rows]
-        base_held[rows] = base_ref[rows] - steps
+        new_base = base_ref[rows] - steps_ref[rows]
+        base_held[rows] = new_base
         copies.append(copy(0, part, rows))
         copies[-1].start()
-        inner_held[rows] = (blended_ref[rows] - (1.0 - blend_share) * steps).astype(jnp.bfloat16)
+        kept_share = blend_share * inner_ref[rows].astype(jnp.float32)
+        inner_held[rows] = (kept_share + (1.0 - blend_share) * new_base).astype(jnp.bfloat16)
         copies.append(copy(2, part, rows))
         copies[-1].start()
     for each in copies:
         each.wait()
 
 
-def outputs(base_weights, blended, steps, kept, outer_grad, clip_factor):
+def outputs(base_weights, replica_copy, steps, kept, outer_grad, clip_factor):
     rows, columns = base_weights.shape
     chunk = rows // 4
     shapes = (
@@ -119,7 +144,7 @@
         cost_estimate=pl.CostEstimate(
             flops=4 * rows * columns, bytes_accessed=18 * rows * columns, transcendentals=0
         ),
-    )(base_weights, blended, steps, kept, outer_grad, clip_factor)
+    )(base_weights, replica_copy, steps, kept, outer_grad, clip_factor)
 
 
 def lane_squares(value):
@@ -137,12 +162,10 @@
     replicas = lax.axis_size(REPLICA)
     local_rows, columns = base_weights.shape
     owned_rows = local_rows // replicas
-    replica_copy = inner_weights[0]
-    decoded = decoded_deltas(base_weights, replica_copy)
+    decoded, base_weights, replica_copy = decoded_deltas(base_weights, inner_weights[0])
     arrived = exchanged(decoded.reshape(replicas, owned_rows, columns), REPLICA)
-    blended = blend_share * replica_copy.astype(jnp.float32) + (1.0 - blend_share) * base_weights
+    arrived, momentum = lax.optimization_barrier((arrived, momentum))
     kept = outer_momentum * momentum
-    arrived, blended, kept = lax.optimization_barrier((arrived, blended, kept))
     outer_grad = arrived.astype(jnp.float32).sum(axis=0) / replicas
     squares = to_everyone(lane_squares(outer_grad), RING).sum(axis=0)
     squares = to_everyone(squares, PLANE).sum(axis=0)
@@ -153,7 +176,7 @@
     steps = to_everyone((step * step_unit).astype(jnp.float16), REPLICA)
     steps = steps.reshape(local_rows, columns).astype(jnp.float32) * (1.0 / step_unit)
     new_base, new_momentum, new_inner = outputs(
-        base_weights, blended, steps, kept, outer_grad, clip_factor
+        base_weights, replica_copy, steps, kept, outer_grad, clip_factor
     )
     return (new_base, new_momentum, new_inner[None])
 

time: 79 us -> 79.4 us (level)
  blocking collectives: 50.3 us -> 72.8 us
  waiting for transfers between devices: 13.2 us -> 0 us
  starting transfers between devices: 9.34 us -> 0 us
  local copies, waits for them, and re-layouts: 0.09 us -> 1.72 us
  Pallas kernels: 4.28 us -> 3.31 us
    all_to_all x3 -> x4, blocking collectives: 50.3 us -> 72.8 us  [exchanged(): return lax.all_to_all(blocks, axis, split_axis=0, concat_axis=0, tiled=True)]
    all_to_all x1 -> x0, waiting for transfers between devices: 13.2 us -> none  [exchanged(): return lax.all_to_all(blocks, axis, split_axis=0, concat_axis=0, tiled=True)]
    all_to_all x1 -> x0, starting transfers between devices: 9.34 us -> none  [exchanged(): return lax.all_to_all(blocks, axis, split_axis=0, concat_axis=0, tiled=True)]
    unnamed x6 -> x4, local copies, waits for them, and re-layouts: 0.01 us -> 1.64 us
    pallas_call x1, Pallas kernels: 3 us -> 2.02 us  [decoded_deltas(): pl.pallas_call(lambda *refs: encode_kernel(chunk, *refs), in_specs=[pl.Bl...]
  transfers between devices with their start and end apart: 1 -> 0, of which waited for: 1 -> 0; matrix products, arithmetic and copies ran while one was open for 0% -> 0% of each run, Pallas kernels for 0% -> 0%
where the time goes in v11:
time: 79.4 us; the launch traced here: 79 us
  blocking collectives  72.8 us (92%)
  Pallas kernels  3.31 us (4%)
  local copies, waits for them, and re-layouts  1.72 us (2%)
    all_to_all x4, blocking collectives, exchanged(): return lax.all_to_all(blocks, axis, split_axis=0, concat_axis=0, tiled=True)  72.8 us
    pallas_call x1, Pallas kernels, decoded_deltas(): pl.pallas_call(lambda *refs: encode_kernel(chunk, *refs), in_specs=[pl.Bl...  2.02 us
    unnamed x4, local copies, waits for them, and re-layouts  1.64 us

profile of v11, /device:TPU:8, one launch (start us, length us, event | category | flops | bytes accessed | tf_op | source)
XLA Modules:
  0.0 79.0 jit_solution(8903072163468128320)
XLA Ops:
  0.6 0.0 copy-start
  0.6 1.0 %copy-done = bf16[1,256,1024]{2,1,0:T(8,128)(2,1)S(1)} copy-done((bf16[1,256,1024]{2,1,0:T(8,128)(2,1)S(1)}, bf16[1,256,1024]{2,1,0:T(8,128)(2,1)}, u32[]{:S(2)}) %copy-start) | copy-done | bytes 524312
  1.7 2.0 %shard_map.58 = (bf16[256,1024]{1,0:T(8,128)(2,1)S(1)}, f32[256,1024]{1,0:T(8,128)S(1)}, bf16[256,1024]{1,0:T(8,128)(2,1)S(1)}) custom-call(f32[256,1024]{1,0:T(8,128)} %refs_0_.1, bf16[256,1024]{1,0:T(8,128)(2,1)S(1)} %bitcast.14), custom_call_target="tpu_custom_call" | custom-call | flops 5242880 | bytes 2097152 | tf_op jit(solution)/shard_map/pallas_call | solution.py:84
  3.7 22.4 %all_to_all.20 = bf16[16,16,1024]{2,1,0:T(8,128)(2,1)S(1)} all-to-all(bf16[16,16,1024]{2,1,0:T(8,128)(2,1)S(1)} %bitcast.15), channel_id=1, replica_groups=mesh['replica_0'=4,'replica_1'=4,'fsdp_0'=8,'fsdp_1'=2,'fsdp_2'=2] {'rep..., dimensions={0} | all-to-all | bytes 1048576 | tf_op jit(solution)/shard_map/all_to_all | solution.py:30
  26.1 0.1 convert_reduce_fusion
  26.3 11.1 %all_to_all.21 = f32[16,1,128]{2,1,0:T(1,128)S(1)} all-to-all(f32[16,1,128]{2,1,0:T(1,128)S(1)} %broadcast_in_dim.16), channel_id=1, replica_groups=mesh['replica_0'=4,'replica_1'=4,'fsdp_0'=8,'fsdp_1'=2,'fsdp_2'=2] {'fsd..., dimensions={0} | all-to-all | bytes 16384 | tf_op jit(solution)/shard_map/all_to_all | solution.py:30
  37.4 21.5 %all_to_all.22 = f32[32,1,128]{2,1,0:T(1,128)S(1)} all-to-all(f32[32,1,128]{2,1,0:T(1,128)S(1)} %broadcast_in_dim.17), channel_id=1, replica_groups=mesh['replica_0'=4,'replica_1'=4,'fsdp_0'=8,'fsdp_1'=2,'fsdp_2'=2] {'rep..., dimensions={0} | all-to-all | bytes 32768 | tf_op jit(solution)/shard_map/all_to_all | solution.py:30
  59.0 0.0 copy-start.1
  59.0 0.2 fusion
  59.2 0.6 copy-done.1
  59.8 0.1 broadcast_in_dim.19
  59.9 17.7 %all_to_all.23 = f16[16,16,1024]{2,1,0:T(8,128)(2,1)S(1)} all-to-all(f16[16,16,1024]{2,1,0:T(8,128)(2,1)S(1)} %broadcast_in_dim.19), channel_id=1, replica_groups=mesh['replica_0'=4,'replica_1'=4,'fsdp_0'=8,'fsdp_1'=2,'fsdp_2'=2] {'rep..., dimensions={0} | all-to-all | bytes 1048576 | tf_op jit(solution)/shard_map/all_to_all | solution.py:30
  77.6 0.1 convert_multiply_fusion
  77.7 1.3 %shard_map.59 = (f32[256,1024]{1,0:T(8,128)}, f32[16,1024]{1,0:T(8,128)}, bf16[256,1024]{1,0:T(8,128)(2,1)}) custom-call(f32[256,1024]{1,0:T(8,128)S(1)} %get-tuple-element.11.refs_0_, bf16[256,1024]{1,0:T(8,128)(2,1)S(1)} %get-tuple-element.12.refs_1_, f32[256,1024]{1,0:T(8,128)S(1)} %bitcast.13, f32[16,1024]{1,0:T(8,128)S(1)} %get-tuple-element.21.refs_3_, ...), custom_call_target="tpu_custom_call" | custom-call | flops 1048576 | bytes 4718592 | tf_op jit(solution)/shard_map/pallas_call | solution.py:136
  (8 shorter events, 0.1 us)
Async XLA Ops:
  0.6 1.0 %copy-start = (bf16[1,256,1024]{2,1,0:T(8,128)(2,1)S(1)}, bf16[1,256,1024]{2,1,0:T(8,128)(2,1)}, u32[]{:S(2)}) copy-start(bf16[1,256,1024]{2,1,0:T(8,128)(2,1)} %param.4) | copy-start | bytes 1572868
  59.0 0.8 %copy-start.1 = (f32[16,1024]{1,0:T(8,128)S(1)}, f32[16,1024]{1,0:T(8,128)}, u32[]{:S(2)}) copy-start(f32[16,1024]{1,0:T(8,128)} %param.5) | copy-start | bytes 196612

commit v12 on v11

--- a/solution.py
+++ b/solution.py
@@ -84,21 +84,21 @@
     return pl.pallas_call(
         lambda *refs: encode_kernel(chunk, *refs),
         in_specs=[pl.BlockSpec(memory_space=pltpu.HBM)] * 2,
-        out_specs=[pl.BlockSpec(memory_space=pltpu.VMEM)] * 3,
-        out_shape=[
-            jax.ShapeDtypeStruct((rows, columns), jnp.bfloat16),
-            jax.ShapeDtypeStruct((rows, columns), jnp.float32),
-            jax.ShapeDtypeStruct((rows, columns), jnp.bfloat16),
+        out_specs=pl.BlockSpec(memory_space=pltpu.VMEM),
+        out_shape=jax.ShapeDtypeStruct((rows, columns), jnp.bfloat16),
+        scratch_shapes=[
+            pltpu.VMEM((rows, columns), jnp.float32),
+            pltpu.VMEM((rows, columns), jnp.bfloat16),
+            pltpu.SemaphoreType.DMA((2, 4)),
         ],
-        scratch_shapes=[pltpu.SemaphoreType.DMA((2, 4))],
-        compiler_params=pltpu.CompilerParams(vmem_limit_bytes=51 * 2**20),
+        compiler_params=pltpu.CompilerParams(vmem_limit_bytes=53 * 2**20),
         cost_estimate=pl.CostEstimate(
             flops=20 * rows * columns, bytes_accessed=8 * rows * columns, transcendentals=0
         ),
     )(base_weights, replica_copy)
 
 
-def outputs_kernel(chunk, base_ref, inner_ref, steps_ref, kept_ref, grad_ref, clip_ref, *refs):
+def outputs_kernel(chunk, base_ref, blended_ref, steps_ref, kept_ref, grad_ref, clip_ref, *refs):
     out_refs, held_refs, sems = refs[:3], refs[3:6], refs[6]
     base_held, momentum_held, inner_held = held_refs
 
@@ -113,19 +113,18 @@
     copies[-1].start()
     for part in range(base_held.shape[0] // chunk):
         rows = pl.ds(part * chunk, chunk)
-        new_base = base_ref[rows] - steps_ref[rows]
-        base_held[rows] = new_base
+        steps = steps_ref[rows]
+        base_held[rows] = base_ref[rows] - steps
         copies.append(copy(0, part, rows))
         copies[-1].start()
-        kept_share = blend_share * inner_ref[rows].astype(jnp.float32)
-        inner_held[rows] = (kept_share + (1.0 - blend_share) * new_base).astype(jnp.bfloat16)
+        inner_held[rows] = (blended_ref[rows] - (1.0 - blend_share) * steps).astype(jnp.bfloat16)
         copies.append(copy(2, part, rows))
         copies[-1].start()
     for each in copies:
         each.wait()
 
 
-def outputs(base_weights, replica_copy, steps, kept, outer_grad, clip_factor):
+def outputs(base_weights, blended, steps, kept, outer_grad, clip_factor):
     rows, columns = base_weights.shape
     chunk = rows // 4
     shapes = (
@@ -144,7 +143,7 @@
         cost_estimate=pl.CostEstimate(
             flops=4 * rows * columns, bytes_accessed=18 * rows * columns, transcendentals=0
         ),
-    )(base_weights, replica_copy, steps, kept, outer_grad, clip_factor)
+    )(base_weights, blended, steps, kept, outer_grad, clip_factor)
 
 
 def lane_squares(value):
@@ -162,12 +161,18 @@
     replicas = lax.axis_size(REPLICA)
     local_rows, columns = base_weights.shape
     owned_rows = local_rows // replicas
-    decoded, base_weights, replica_copy = decoded_deltas(base_weights, inner_weights[0])
+    decoded = decoded_deltas(base_weights, inner_weights[0])
     arrived = exchanged(decoded.reshape(replicas, owned_rows, columns), REPLICA)
-    arrived, momentum = lax.optimization_barrier((arrived, momentum))
-    kept = outer_momentum * momentum
     outer_grad = arrived.astype(jnp.float32).sum(axis=0) / replicas
     squares = to_everyone(lane_squares(outer_grad), RING).sum(axis=0)
+    squares, base_weights, inner_weights, momentum = lax.optimization_barrier(
+        (squares, base_weights, inner_weights, momentum)
+    )
+    replica_copy = inner_weights[0].astype(jnp.float32)
+    blended = blend_share * replica_copy + (1.0 - blend_share) * base_weights
+    squares, blended, kept = lax.optimization_barrier(
+        (squares, blended, outer_momentum * momentum)
+    )
     squares = to_everyone(squares, PLANE).sum(axis=0)
     grad_sq = lane_total(squares, columns)
     clip_factor = jnp.minimum(1.0, clip_rms / jnp.sqrt(grad_sq / (D * KVW) + epsilon))
@@ -176,7 +181,7 @@
     steps = to_everyone((step * step_unit).astype(jnp.float16), REPLICA)
     steps = steps.reshape(local_rows, columns).astype(jnp.float32) * (1.0 / step_unit)
     new_base, new_momentum, new_inner = outputs(
-        base_weights, replica_copy, steps, kept, outer_grad, clip_factor
+        base_weights, blended, steps, kept, outer_grad, clip_factor
     )
     return (new_base, new_momentum, new_inner[None])
 

time: 79.4 us -> 78.2 us (0.985)
  local copies, waits for them, and re-layouts: 1.72 us -> 0.09 us
    unnamed x4 -> x6, local copies, waits for them, and re-layouts: 1.64 us -> 0.02 us
where the time goes in v12:
time: 78.2 us; the launch traced here: 77.9 us
  blocking collectives  73 us (93%)
  Pallas kernels  3.32 us (4%)
    all_to_all x4, blocking collectives, exchanged(): return lax.all_to_all(blocks, axis, split_axis=0, concat_axis=0, tiled=True)  73 us
    pallas_call x1, Pallas kernels, decoded_deltas(): pl.pallas_call(lambda *refs: encode_kernel(chunk, *refs), in_specs=[pl.Bl...  2.05 us

profile of v12, /device:TPU:8, one launch (start us, length us, event | category | flops | bytes accessed | tf_op | source)
XLA Modules:
  0.0 77.9 jit_solution(10426353115023230048)
XLA Ops:
  0.6 2.0 %shard_map.58 = bf16[256,1024]{1,0:T(8,128)(2,1)S(1)} custom-call(f32[256,1024]{1,0:T(8,128)} %refs_0_.2, bf16[256,1024]{1,0:T(8,128)(2,1)} %bitcast.21), custom_call_target="tpu_custom_call" | custom-call | flops 5242880 | bytes 2097152 | tf_op jit(solution)/shard_map/pallas_call | solution.py:84
  2.7 0.0 copy-start
  2.7 22.6 %all_to_all.20 = bf16[16,16,1024]{2,1,0:T(8,128)(2,1)S(1)} all-to-all(bf16[16,16,1024]{2,1,0:T(8,128)(2,1)S(1)} %bitcast.19), channel_id=1, replica_groups=mesh['replica_0'=4,'replica_1'=4,'fsdp_0'=8,'fsdp_1'=2,'fsdp_2'=2] {'rep..., dimensions={0} | all-to-all | bytes 1048576 | tf_op jit(solution)/shard_map/all_to_all | solution.py:30
  25.3 0.0 copy-start.1
  25.3 0.1 convert_reduce_fusion
  25.3 0.0 copy-start.2
  25.4 11.3 %all_to_all.21 = f32[16,1,128]{2,1,0:T(1,128)S(1)} all-to-all(f32[16,1,128]{2,1,0:T(1,128)S(1)} %broadcast_in_dim.16), channel_id=1, replica_groups=mesh['replica_0'=4,'replica_1'=4,'fsdp_0'=8,'fsdp_1'=2,'fsdp_2'=2] {'fsd..., dimensions={0} | all-to-all | bytes 16384 | tf_op jit(solution)/shard_map/all_to_all | solution.py:30
  36.7 0.0 copy-done.2
  36.7 0.0 copy-done
  36.7 0.0 copy-done.1
  36.7 0.2 fusion.refs_1_
  36.9 21.5 %all_to_all.22 = f32[32,1,128]{2,1,0:T(1,128)S(1)} all-to-all(f32[32,1,128]{2,1,0:T(1,128)S(1)} %broadcast_in_dim.17), channel_id=1, replica_groups=mesh['replica_0'=4,'replica_1'=4,'fsdp_0'=8,'fsdp_1'=2,'fsdp_2'=2] {'rep..., dimensions={0} | all-to-all | bytes 32768 | tf_op jit(solution)/shard_map/all_to_all | solution.py:30
  58.5 0.2 fusion.1
  58.8 0.1 broadcast_in_dim.19
  58.8 17.7 %all_to_all.23 = f16[16,16,1024]{2,1,0:T(8,128)(2,1)S(1)} all-to-all(f16[16,16,1024]{2,1,0:T(8,128)(2,1)S(1)} %broadcast_in_dim.19), channel_id=1, replica_groups=mesh['replica_0'=4,'replica_1'=4,'fsdp_0'=8,'fsdp_1'=2,'fsdp_2'=2] {'rep..., dimensions={0} | all-to-all | bytes 1048576 | tf_op jit(solution)/shard_map/all_to_all | solution.py:30
  76.5 0.1 convert_multiply_fusion
  76.6 1.3 %shard_map.59 = (f32[256,1024]{1,0:T(8,128)}, f32[16,1024]{1,0:T(8,128)}, bf16[256,1024]{1,0:T(8,128)(2,1)}) custom-call(f32[256,1024]{1,0:T(8,128)S(1)} %copy-done, f32[256,1024]{1,0:T(8,128)S(1)} %fusion.refs_1_, f32[256,1024]{1,0:T(8,128)S(1)} %bitcast.18, f32[16,1024]{1,0:T(8,128)S(1)} %broadcast_multiply_fusion.refs_3_, ...), custom_call_target="tpu_custom_call" | custom-call | flops 1048576 | bytes 4718592 | tf_op jit(solution)/shard_map/pallas_call | solution.py:135
  (9 shorter events, 0.2 us)
Async XLA Ops:
  2.7 34.0 %copy-start = (f32[256,1024]{1,0:T(8,128)S(1)}, f32[256,1024]{1,0:T(8,128)}, u32[]{:S(2)}) copy-start(f32[256,1024]{1,0:T(8,128)} %refs_0_.2) | copy-start | bytes 3145732
  25.3 11.5 %copy-start.1 = (bf16[1,256,1024]{2,1,0:T(8,128)(2,1)S(1)}, bf16[1,256,1024]{2,1,0:T(8,128)(2,1)}, u32[]{:S(2)}) copy-start(bf16[1,256,1024]{2,1,0:T(8,128)(2,1)} %param.4) | copy-start | bytes 1572868
  25.3 11.3 %copy-start.2 = (f32[16,1024]{1,0:T(8,128)S(1)}, f32[16,1024]{1,0:T(8,128)}, u32[]{:S(2)}) copy-start(f32[16,1024]{1,0:T(8,128)} %param.5) | copy-start | bytes 196612

commit v13 on v12

--- a/solution.py
+++ b/solution.py
@@ -126,7 +126,7 @@
 
 def outputs(base_weights, blended, steps, kept, outer_grad, clip_factor):
     rows, columns = base_weights.shape
-    chunk = rows // 4
+    chunk = rows // 2
     shapes = (
         jax.ShapeDtypeStruct((rows, columns), jnp.float32),
         jax.ShapeDtypeStruct(kept.shape, jnp.float32),
@@ -138,7 +138,7 @@
         out_specs=[pl.BlockSpec(memory_space=pl.ANY)] * 3,
         out_shape=shapes,
         scratch_shapes=[pltpu.VMEM(each.shape, each.dtype) for each in shapes]
-        + [pltpu.SemaphoreType.DMA((3, 4))],
+        + [pltpu.SemaphoreType.DMA((3, 2))],
         compiler_params=pltpu.CompilerParams(vmem_limit_bytes=8 * 2**20),
         cost_estimate=pl.CostEstimate(
             flops=4 * rows * columns, bytes_accessed=18 * rows * columns, transcendentals=0

time: 78.2 us -> 78.2 us (level)
  no operation moved by 1% of the time
where the time goes in v13:
time: 78.2 us; the launch traced here: 77.9 us
  blocking collectives  73 us (93%)
  Pallas kernels  3.31 us (4%)
    all_to_all x4, blocking collectives, exchanged(): return lax.all_to_all(blocks, axis, split_axis=0, concat_axis=0, tiled=True)  73 us
    pallas_call x1, Pallas kernels, decoded_deltas(): pl.pallas_call(lambda *refs: encode_kernel(chunk, *refs), in_specs=[pl.Bl...  2.05 us

profile of v13, /device:TPU:8, one launch (start us, length us, event | category | flops | bytes accessed | tf_op | source)
XLA Modules:
  0.0 77.9 jit_solution(4508664841921273271)
XLA Ops:
  0.6 2.0 %shard_map.58 = bf16[256,1024]{1,0:T(8,128)(2,1)S(1)} custom-call(f32[256,1024]{1,0:T(8,128)} %refs_0_.2, bf16[256,1024]{1,0:T(8,128)(2,1)} %bitcast.21), custom_call_target="tpu_custom_call" | custom-call | flops 5242880 | bytes 2097152 | tf_op jit(solution)/shard_map/pallas_call | solution.py:84
  2.7 0.0 copy-start
  2.7 22.6 %all_to_all.20 = bf16[16,16,1024]{2,1,0:T(8,128)(2,1)S(1)} all-to-all(bf16[16,16,1024]{2,1,0:T(8,128)(2,1)S(1)} %bitcast.19), channel_id=1, replica_groups=mesh['replica_0'=4,'replica_1'=4,'fsdp_0'=8,'fsdp_1'=2,'fsdp_2'=2] {'rep..., dimensions={0} | all-to-all | bytes 1048576 | tf_op jit(solution)/shard_map/all_to_all | solution.py:30
  25.3 0.0 copy-start.1
  25.3 0.1 convert_reduce_fusion
  25.3 0.0 copy-start.2
  25.4 11.3 %all_to_all.21 = f32[16,1,128]{2,1,0:T(1,128)S(1)} all-to-all(f32[16,1,128]{2,1,0:T(1,128)S(1)} %broadcast_in_dim.16), channel_id=1, replica_groups=mesh['replica_0'=4,'replica_1'=4,'fsdp_0'=8,'fsdp_1'=2,'fsdp_2'=2] {'fsd..., dimensions={0} | all-to-all | bytes 16384 | tf_op jit(solution)/shard_map/all_to_all | solution.py:30
  36.7 0.0 copy-done.2
  36.7 0.0 copy-done
  36.7 0.0 copy-done.1
  36.7 0.2 fusion.refs_1_
  36.9 21.5 %all_to_all.22 = f32[32,1,128]{2,1,0:T(1,128)S(1)} all-to-all(f32[32,1,128]{2,1,0:T(1,128)S(1)} %broadcast_in_dim.17), channel_id=1, replica_groups=mesh['replica_0'=4,'replica_1'=4,'fsdp_0'=8,'fsdp_1'=2,'fsdp_2'=2] {'rep..., dimensions={0} | all-to-all | bytes 32768 | tf_op jit(solution)/shard_map/all_to_all | solution.py:30
  58.5 0.2 fusion.1
  58.8 0.1 broadcast_in_dim.19
  58.8 17.7 %all_to_all.23 = f16[16,16,1024]{2,1,0:T(8,128)(2,1)S(1)} all-to-all(f16[16,16,1024]{2,1,0:T(8,128)(2,1)S(1)} %broadcast_in_dim.19), channel_id=1, replica_groups=mesh['replica_0'=4,'replica_1'=4,'fsdp_0'=8,'fsdp_1'=2,'fsdp_2'=2] {'rep..., dimensions={0} | all-to-all | bytes 1048576 | tf_op jit(solution)/shard_map/all_to_all | solution.py:30
  76.5 0.1 convert_multiply_fusion
  76.6 1.3 %shard_map.59 = (f32[256,1024]{1,0:T(8,128)}, f32[16,1024]{1,0:T(8,128)}, bf16[256,1024]{1,0:T(8,128)(2,1)}) custom-call(f32[256,1024]{1,0:T(8,128)S(1)} %copy-done, f32[256,1024]{1,0:T(8,128)S(1)} %fusion.refs_1_, f32[256,1024]{1,0:T(8,128)S(1)} %bitcast.18, f32[16,1024]{1,0:T(8,128)S(1)} %broadcast_multiply_fusion.refs_3_, ...), custom_call_target="tpu_custom_call" | custom-call | flops 1048576 | bytes 4718592 | tf_op jit(solution)/shard_map/pallas_call | solution.py:135
  (9 shorter events, 0.2 us)
Async XLA Ops:
  2.7 34.0 %copy-start = (f32[256,1024]{1,0:T(8,128)S(1)}, f32[256,1024]{1,0:T(8,128)}, u32[]{:S(2)}) copy-start(f32[256,1024]{1,0:T(8,128)} %refs_0_.2) | copy-start | bytes 3145732
  25.3 11.5 %copy-start.1 = (bf16[1,256,1024]{2,1,0:T(8,128)(2,1)S(1)}, bf16[1,256,1024]{2,1,0:T(8,128)(2,1)}, u32[]{:S(2)}) copy-start(bf16[1,256,1024]{2,1,0:T(8,128)(2,1)} %param.4) | copy-start | bytes 1572868
  25.3 11.3 %copy-start.2 = (f32[16,1024]{1,0:T(8,128)S(1)}, f32[16,1024]{1,0:T(8,128)}, u32[]{:S(2)}) copy-start(f32[16,1024]{1,0:T(8,128)} %param.5) | copy-start | bytes 196612

commit v14 on v13

--- a/solution.py
+++ b/solution.py
@@ -12,8 +12,8 @@
 REPLICA = ("replica_0", "replica_1")
 FSDP = ("fsdp_0", "fsdp_1", "fsdp_2")
 FSDP_REPLICA = ("fsdp_0", "fsdp_1", "fsdp_2", "replica_0", "replica_1")
-RING = ("fsdp_1", "replica_0", "fsdp_2")
-PLANE = ("replica_1", "fsdp_0")
+RING = ("fsdp_0", "fsdp_2")
+PLANE = ("replica_1", "fsdp_1", "replica_0")
 
 code_limit = 448.0
 outer_rate = 0.7

time: 78.2 us -> 78.2 us (level)
  no operation moved by 1% of the time
where the time goes in v14:
time: 78.2 us; the launch traced here: 77.9 us
  blocking collectives  73 us (93%)
  Pallas kernels  3.31 us (4%)
    all_to_all x4, blocking collectives, exchanged(): return lax.all_to_all(blocks, axis, split_axis=0, concat_axis=0, tiled=True)  73 us
    pallas_call x1, Pallas kernels, decoded_deltas(): pl.pallas_call(lambda *refs: encode_kernel(chunk, *refs), in_specs=[pl.Bl...  2.05 us

profile of v14, /device:TPU:8, one launch (start us, length us, event | category | flops | bytes accessed | tf_op | source)
XLA Modules:
  0.0 77.9 jit_solution(6961565805426272944)
XLA Ops:
  0.6 2.0 %shard_map.58 = bf16[256,1024]{1,0:T(8,128)(2,1)S(1)} custom-call(f32[256,1024]{1,0:T(8,128)} %refs_0_.2, bf16[256,1024]{1,0:T(8,128)(2,1)} %bitcast.21), custom_call_target="tpu_custom_call" | custom-call | flops 5242880 | bytes 2097152 | tf_op jit(solution)/shard_map/pallas_call | solution.py:84
  2.7 0.0 copy-start
  2.7 22.6 %all_to_all.20 = bf16[16,16,1024]{2,1,0:T(8,128)(2,1)S(1)} all-to-all(bf16[16,16,1024]{2,1,0:T(8,128)(2,1)S(1)} %bitcast.19), channel_id=1, replica_groups=mesh['replica_0'=4,'replica_1'=4,'fsdp_0'=8,'fsdp_1'=2,'fsdp_2'=2] {'rep..., dimensions={0} | all-to-all | bytes 1048576 | tf_op jit(solution)/shard_map/all_to_all | solution.py:30
  25.3 0.0 copy-start.1
  25.3 0.1 convert_reduce_fusion
  25.3 0.0 copy-start.2
  25.4 17.9 %all_to_all.21 = f32[16,1,128]{2,1,0:T(1,128)S(1)} all-to-all(f32[16,1,128]{2,1,0:T(1,128)S(1)} %broadcast_in_dim.16), channel_id=1, replica_groups=mesh['replica_0'=4,'replica_1'=4,'fsdp_0'=8,'fsdp_1'=2,'fsdp_2'=2] {'fsd..., dimensions={0} | all-to-all | bytes 16384 | tf_op jit(solution)/shard_map/all_to_all | solution.py:30
  43.3 0.0 copy-done.2
  43.3 0.0 copy-done
  43.3 0.0 copy-done.1
  43.3 0.2 fusion.refs_1_
  43.6 15.0 %all_to_all.22 = f32[32,1,128]{2,1,0:T(1,128)S(1)} all-to-all(f32[32,1,128]{2,1,0:T(1,128)S(1)} %broadcast_in_dim.17), channel_id=1, replica_groups=mesh['replica_0'=4,'replica_1'=4,'fsdp_0'=8,'fsdp_1'=2,'fsdp_2'=2] {'rep..., dimensions={0} | all-to-all | bytes 32768 | tf_op jit(solution)/shard_map/all_to_all | solution.py:30
  58.6 0.2 fusion.1
  58.8 0.1 broadcast_in_dim.19
  58.9 17.6 %all_to_all.23 = f16[16,16,1024]{2,1,0:T(8,128)(2,1)S(1)} all-to-all(f16[16,16,1024]{2,1,0:T(8,128)(2,1)S(1)} %broadcast_in_dim.19), channel_id=1, replica_groups=mesh['replica_0'=4,'replica_1'=4,'fsdp_0'=8,'fsdp_1'=2,'fsdp_2'=2] {'rep..., dimensions={0} | all-to-all | bytes 1048576 | tf_op jit(solution)/shard_map/all_to_all | solution.py:30
  76.5 0.1 convert_multiply_fusion
  76.6 1.3 %shard_map.59 = (f32[256,1024]{1,0:T(8,128)}, f32[16,1024]{1,0:T(8,128)}, bf16[256,1024]{1,0:T(8,128)(2,1)}) custom-call(f32[256,1024]{1,0:T(8,128)S(1)} %copy-done, f32[256,1024]{1,0:T(8,128)S(1)} %fusion.refs_1_, f32[256,1024]{1,0:T(8,128)S(1)} %bitcast.18, f32[16,1024]{1,0:T(8,128)S(1)} %broadcast_multiply_fusion.refs_3_, ...), custom_call_target="tpu_custom_call" | custom-call | flops 1048576 | bytes 4718592 | tf_op jit(solution)/shard_map/pallas_call | solution.py:135
  (9 shorter events, 0.2 us)
Async XLA Ops:
  2.7 40.6 %copy-start = (f32[256,1024]{1,0:T(8,128)S(1)}, f32[256,1024]{1,0:T(8,128)}, u32[]{:S(2)}) copy-start(f32[256,1024]{1,0:T(8,128)} %refs_0_.2) | copy-start | bytes 3145732
  25.3 18.1 %copy-start.1 = (bf16[1,256,1024]{2,1,0:T(8,128)(2,1)S(1)}, bf16[1,256,1024]{2,1,0:T(8,128)(2,1)}, u32[]{:S(2)}) copy-start(bf16[1,256,1024]{2,1,0:T(8,128)(2,1)} %param.4) | copy-start | bytes 1572868
  25.3 18.0 %copy-start.2 = (f32[16,1024]{1,0:T(8,128)S(1)}, f32[16,1024]{1,0:T(8,128)}, u32[]{:S(2)}) copy-start(f32[16,1024]{1,0:T(8,128)} %param.5) | copy-start | bytes 196612

commit v15 on v13

--- a/solution.py
+++ b/solution.py
@@ -12,7 +12,8 @@
 REPLICA = ("replica_0", "replica_1")
 FSDP = ("fsdp_0", "fsdp_1", "fsdp_2")
 FSDP_REPLICA = ("fsdp_0", "fsdp_1", "fsdp_2", "replica_0", "replica_1")
-RING = ("fsdp_1", "replica_0", "fsdp_2")
+CORES = "fsdp_2"
+RING = ("fsdp_1", "replica_0")
 PLANE = ("replica_1", "fsdp_0")
 
 code_limit = 448.0
@@ -164,7 +165,8 @@
     decoded = decoded_deltas(base_weights, inner_weights[0])
     arrived = exchanged(decoded.reshape(replicas, owned_rows, columns), REPLICA)
     outer_grad = arrived.astype(jnp.float32).sum(axis=0) / replicas
-    squares = to_everyone(lane_squares(outer_grad), RING).sum(axis=0)
+    squares = lax.psum(lane_squares(outer_grad), CORES)
+    squares = to_everyone(squares, RING).sum(axis=0)
     squares, base_weights, inner_weights, momentum = lax.optimization_barrier(
         (squares, base_weights, inner_weights, momentum)
     )

time: 78.2 us -> 79.5 us (1.017)
  blocking collectives: 73 us -> 74.3 us
    psum x0 -> x1, blocking collectives: none -> 2.6 us  [shards(): squares = lax.psum(lane_squares(outer_grad), CORES)]
    all_to_all x4, blocking collectives: 73 us -> 71.7 us  [exchanged(): return lax.all_to_all(blocks, axis, split_axis=0, concat_axis=0, tiled=True)]
where the time goes in v15:
time: 79.5 us; the launch traced here: 79.2 us
  blocking collectives  74.3 us (93%)
  Pallas kernels  3.31 us (4%)
    all_to_all x4, blocking collectives, exchanged(): return lax.all_to_all(blocks, axis, split_axis=0, concat_axis=0, tiled=True)  71.7 us
    psum x1, blocking collectives, shards(): squares = lax.psum(lane_squares(outer_grad), CORES)  2.6 us
    pallas_call x1, Pallas kernels, decoded_deltas(): pl.pallas_call(lambda *refs: encode_kernel(chunk, *refs), in_specs=[pl.Bl...  2.05 us

profile of v15, /device:TPU:8, one launch (start us, length us, event | category | flops | bytes accessed | tf_op | source)
XLA Modules:
  0.0 79.2 jit_solution(1520463417479392699)
XLA Ops:
  0.6 2.0 %shard_map.58 = bf16[256,1024]{1,0:T(8,128)(2,1)S(1)} custom-call(f32[256,1024]{1,0:T(8,128)} %refs_0_.2, bf16[256,1024]{1,0:T(8,128)(2,1)} %bitcast.21), custom_call_target="tpu_custom_call" | custom-call | flops 5242880 | bytes 2097152 | tf_op jit(solution)/shard_map/pallas_call | solution.py:85
  2.7 0.0 copy-start
  2.7 22.6 %all_to_all.20 = bf16[16,16,1024]{2,1,0:T(8,128)(2,1)S(1)} all-to-all(bf16[16,16,1024]{2,1,0:T(8,128)(2,1)S(1)} %bitcast.19), channel_id=1, replica_groups=mesh['replica_0'=4,'replica_1'=4,'fsdp_0'=8,'fsdp_1'=2,'fsdp_2'=2] {'rep..., dimensions={0} | all-to-all | bytes 1048576 | tf_op jit(solution)/shard_map/all_to_all | solution.py:31
  25.3 0.0 copy-start.1
  25.3 0.1 convert_reduce_fusion
  25.3 0.0 copy-start.2
  25.4 2.6 %psum.10 = f32[128]{0:T(128)S(1)} all-reduce(f32[128]{0:T(128)S(1)} %bitcast_reduce_fusion), channel_id=1, replica_groups=mesh['replica_0'=4,'replica_1'=4,'fsdp_0'=8,'fsdp_1'=2,'fsdp_2'=2] {'fsd..., use_global_device_ids=true, to_apply=%region_3.0 | all-reduce | flops 128 | bytes 1024 | tf_op jit(solution)/shard_map/psum | solution.py:168
  28.0 11.1 %all_to_all.21 = f32[8,1,128]{2,1,0:T(1,128)S(1)} all-to-all(f32[8,1,128]{2,1,0:T(1,128)S(1)} %broadcast_in_dim.19), channel_id=1, replica_groups=mesh['replica_0'=4,'replica_1'=4,'fsdp_0'=8,'fsdp_1'=2,'fsdp_2'=2] {'fsd..., dimensions={0} | all-to-all | bytes 8192 | tf_op jit(solution)/shard_map/all_to_all | solution.py:31
  39.1 0.0 copy-done.2
  39.2 0.0 copy-done
  39.2 0.0 copy-done.1
  39.2 0.2 fusion.refs_1_
  39.4 21.5 %all_to_all.22 = f32[32,1,128]{2,1,0:T(1,128)S(1)} all-to-all(f32[32,1,128]{2,1,0:T(1,128)S(1)} %broadcast_in_dim.20), channel_id=1, replica_groups=mesh['replica_0'=4,'replica_1'=4,'fsdp_0'=8,'fsdp_1'=2,'fsdp_2'=2] {'rep..., dimensions={0} | all-to-all | bytes 32768 | tf_op jit(solution)/shard_map/all_to_all | solution.py:31
  61.0 0.2 fusion.1
  61.2 0.1 broadcast_in_dim.22
  61.3 16.5 %all_to_all.23 = f16[16,16,1024]{2,1,0:T(8,128)(2,1)S(1)} all-to-all(f16[16,16,1024]{2,1,0:T(8,128)(2,1)S(1)} %broadcast_in_dim.22), channel_id=1, replica_groups=mesh['replica_0'=4,'replica_1'=4,'fsdp_0'=8,'fsdp_1'=2,'fsdp_2'=2] {'rep..., dimensions={0} | all-to-all | bytes 1048576 | tf_op jit(solution)/shard_map/all_to_all | solution.py:31
  77.8 0.1 convert_multiply_fusion
  77.9 1.3 %shard_map.59 = (f32[256,1024]{1,0:T(8,128)}, f32[16,1024]{1,0:T(8,128)}, bf16[256,1024]{1,0:T(8,128)(2,1)}) custom-call(f32[256,1024]{1,0:T(8,128)S(1)} %copy-done, f32[256,1024]{1,0:T(8,128)S(1)} %fusion.refs_1_, f32[256,1024]{1,0:T(8,128)S(1)} %bitcast.18, f32[16,1024]{1,0:T(8,128)S(1)} %broadcast_multiply_fusion.refs_3_, ...), custom_call_target="tpu_custom_call" | custom-call | flops 1048576 | bytes 4718592 | tf_op jit(solution)/shard_map/pallas_call | solution.py:136
  (9 shorter events, 0.2 us)
Async XLA Ops:
  2.7 36.5 %copy-start = (f32[256,1024]{1,0:T(8,128)S(1)}, f32[256,1024]{1,0:T(8,128)}, u32[]{:S(2)}) copy-start(f32[256,1024]{1,0:T(8,128)} %refs_0_.2) | copy-start | bytes 3145732
  25.3 13.9 %copy-start.1 = (bf16[1,256,1024]{2,1,0:T(8,128)(2,1)S(1)}, bf16[1,256,1024]{2,1,0:T(8,128)(2,1)}, u32[]{:S(2)}) copy-start(bf16[1,256,1024]{2,1,0:T(8,128)(2,1)} %param.4) | copy-start | bytes 1572868
  25.3 13.8 %copy-start.2 = (f32[16,1024]{1,0:T(8,128)S(1)}, f32[16,1024]{1,0:T(8,128)}, u32[]{:S(2)}) copy-start(f32[16,1024]{1,0:T(8,128)} %param.5) | copy-start | bytes 196612

commit v16 on v13

--- a/solution.py
+++ b/solution.py
@@ -126,7 +126,7 @@
 
 def outputs(base_weights, blended, steps, kept, outer_grad, clip_factor):
     rows, columns = base_weights.shape
-    chunk = rows // 2
+    chunk = rows
     shapes = (
         jax.ShapeDtypeStruct((rows, columns), jnp.float32),
         jax.ShapeDtypeStruct(kept.shape, jnp.float32),
@@ -138,7 +138,7 @@
         out_specs=[pl.BlockSpec(memory_space=pl.ANY)] * 3,
         out_shape=shapes,
         scratch_shapes=[pltpu.VMEM(each.shape, each.dtype) for each in shapes]
-        + [pltpu.SemaphoreType.DMA((3, 2))],
+        + [pltpu.SemaphoreType.DMA((3, 1))],
         compiler_params=pltpu.CompilerParams(vmem_limit_bytes=8 * 2**20),
         cost_estimate=pl.CostEstimate(
             flops=4 * rows * columns, bytes_accessed=18 * rows * columns, transcendentals=0

time: 78.2 us -> 78.2 us (level)
  no operation moved by 1% of the time
where the time goes in v16:
time: 78.2 us; the launch traced here: 78 us
  blocking collectives  73 us (93%)
  Pallas kernels  3.36 us (4%)
    all_to_all x4, blocking collectives, exchanged(): return lax.all_to_all(blocks, axis, split_axis=0, concat_axis=0, tiled=True)  73 us
    pallas_call x1, Pallas kernels, decoded_deltas(): pl.pallas_call(lambda *refs: encode_kernel(chunk, *refs), in_specs=[pl.Bl...  2.05 us

profile of v16, /device:TPU:8, one launch (start us, length us, event | category | flops | bytes accessed | tf_op | source)
XLA Modules:
  0.0 78.0 jit_solution(17585710510284335635)
XLA Ops:
  0.6 2.0 %shard_map.58 = bf16[256,1024]{1,0:T(8,128)(2,1)S(1)} custom-call(f32[256,1024]{1,0:T(8,128)} %refs_0_.2, bf16[256,1024]{1,0:T(8,128)(2,1)} %bitcast.21), custom_call_target="tpu_custom_call" | custom-call | flops 5242880 | bytes 2097152 | tf_op jit(solution)/shard_map/pallas_call | solution.py:84
  2.7 0.0 copy-start
  2.7 22.6 %all_to_all.20 = bf16[16,16,1024]{2,1,0:T(8,128)(2,1)S(1)} all-to-all(bf16[16,16,1024]{2,1,0:T(8,128)(2,1)S(1)} %bitcast.19), channel_id=1, replica_groups=mesh['replica_0'=4,'replica_1'=4,'fsdp_0'=8,'fsdp_1'=2,'fsdp_2'=2] {'rep..., dimensions={0} | all-to-all | bytes 1048576 | tf_op jit(solution)/shard_map/all_to_all | solution.py:30
  25.3 0.0 copy-start.1
  25.3 0.1 convert_reduce_fusion
  25.3 0.0 copy-start.2
  25.4 11.3 %all_to_all.21 = f32[16,1,128]{2,1,0:T(1,128)S(1)} all-to-all(f32[16,1,128]{2,1,0:T(1,128)S(1)} %broadcast_in_dim.16), channel_id=1, replica_groups=mesh['replica_0'=4,'replica_1'=4,'fsdp_0'=8,'fsdp_1'=2,'fsdp_2'=2] {'fsd..., dimensions={0} | all-to-all | bytes 16384 | tf_op jit(solution)/shard_map/all_to_all | solution.py:30
  36.7 0.0 copy-done.2
  36.7 0.0 copy-done
  36.7 0.0 copy-done.1
  36.7 0.2 fusion.refs_1_
  36.9 21.5 %all_to_all.22 = f32[32,1,128]{2,1,0:T(1,128)S(1)} all-to-all(f32[32,1,128]{2,1,0:T(1,128)S(1)} %broadcast_in_dim.17), channel_id=1, replica_groups=mesh['replica_0'=4,'replica_1'=4,'fsdp_0'=8,'fsdp_1'=2,'fsdp_2'=2] {'rep..., dimensions={0} | all-to-all | bytes 32768 | tf_op jit(solution)/shard_map/all_to_all | solution.py:30
  58.5 0.2 fusion.1
  58.8 0.1 broadcast_in_dim.19
  58.8 17.7 %all_to_all.23 = f16[16,16,1024]{2,1,0:T(8,128)(2,1)S(1)} all-to-all(f16[16,16,1024]{2,1,0:T(8,128)(2,1)S(1)} %broadcast_in_dim.19), channel_id=1, replica_groups=mesh['replica_0'=4,'replica_1'=4,'fsdp_0'=8,'fsdp_1'=2,'fsdp_2'=2] {'rep..., dimensions={0} | all-to-all | bytes 1048576 | tf_op jit(solution)/shard_map/all_to_all | solution.py:30
  76.5 0.1 convert_multiply_fusion
  76.6 1.3 %shard_map.59 = (f32[256,1024]{1,0:T(8,128)}, f32[16,1024]{1,0:T(8,128)}, bf16[256,1024]{1,0:T(8,128)(2,1)}) custom-call(f32[256,1024]{1,0:T(8,128)S(1)} %copy-done, f32[256,1024]{1,0:T(8,128)S(1)} %fusion.refs_1_, f32[256,1024]{1,0:T(8,128)S(1)} %bitcast.18, f32[16,1024]{1,0:T(8,128)S(1)} %broadcast_multiply_fusion.refs_3_, ...), custom_call_target="tpu_custom_call" | custom-call | flops 1048576 | bytes 4718592 | tf_op jit(solution)/shard_map/pallas_call | solution.py:135
  (9 shorter events, 0.2 us)
Async XLA Ops:
  2.7 34.0 %copy-start = (f32[256,1024]{1,0:T(8,128)S(1)}, f32[256,1024]{1,0:T(8,128)}, u32[]{:S(2)}) copy-start(f32[256,1024]{1,0:T(8,128)} %refs_0_.2) | copy-start | bytes 3145732
  25.3 11.5 %copy-start.1 = (bf16[1,256,1024]{2,1,0:T(8,128)(2,1)S(1)}, bf16[1,256,1024]{2,1,0:T(8,128)(2,1)}, u32[]{:S(2)}) copy-start(bf16[1,256,1024]{2,1,0:T(8,128)(2,1)} %param.4) | copy-start | bytes 1572868
  25.3 11.3 %copy-start.2 = (f32[16,1024]{1,0:T(8,128)S(1)}, f32[16,1024]{1,0:T(8,128)}, u32[]{:S(2)}) copy-start(f32[16,1024]{1,0:T(8,128)} %param.5) | copy-start | bytes 196612

commit v17 on v13

--- a/solution.py
+++ b/solution.py
@@ -80,7 +80,7 @@
 
 def decoded_deltas(base_weights, replica_copy):
     rows, columns = base_weights.shape
-    chunk = rows // 4
+    chunk = rows // 2
     return pl.pallas_call(
         lambda *refs: encode_kernel(chunk, *refs),
         in_specs=[pl.BlockSpec(memory_space=pltpu.HBM)] * 2,
@@ -89,7 +89,7 @@
         scratch_shapes=[
             pltpu.VMEM((rows, columns), jnp.float32),
             pltpu.VMEM((rows, columns), jnp.bfloat16),
-            pltpu.SemaphoreType.DMA((2, 4)),
+            pltpu.SemaphoreType.DMA((2, 2)),
         ],
         compiler_params=pltpu.CompilerParams(vmem_limit_bytes=53 * 2**20),
         cost_estimate=pl.CostEstimate(

time: 78.2 us -> 78.2 us (level)
  no operation moved by 1% of the time
where the time goes in v17:
time: 78.2 us; the launch traced here: 77.9 us
  blocking collectives  73 us (93%)
  Pallas kernels  3.31 us (4%)
    all_to_all x4, blocking collectives, exchanged(): return lax.all_to_all(blocks, axis, split_axis=0, concat_axis=0, tiled=True)  73 us
    pallas_call x1, Pallas kernels, decoded_deltas(): pl.pallas_call(lambda *refs: encode_kernel(chunk, *refs), in_specs=[pl.Bl...  2.05 us

profile of v17, /device:TPU:8, one launch (start us, length us, event | category | flops | bytes accessed | tf_op | source)
XLA Modules:
  0.0 77.9 jit_solution(4946759662716571984)
XLA Ops:
  0.6 2.0 %shard_map.58 = bf16[256,1024]{1,0:T(8,128)(2,1)S(1)} custom-call(f32[256,1024]{1,0:T(8,128)} %refs_0_.2, bf16[256,1024]{1,0:T(8,128)(2,1)} %bitcast.21), custom_call_target="tpu_custom_call" | custom-call | flops 5242880 | bytes 2097152 | tf_op jit(solution)/shard_map/pallas_call | solution.py:84
  2.7 0.0 copy-start
  2.7 22.6 %all_to_all.20 = bf16[16,16,1024]{2,1,0:T(8,128)(2,1)S(1)} all-to-all(bf16[16,16,1024]{2,1,0:T(8,128)(2,1)S(1)} %bitcast.19), channel_id=1, replica_groups=mesh['replica_0'=4,'replica_1'=4,'fsdp_0'=8,'fsdp_1'=2,'fsdp_2'=2] {'rep..., dimensions={0} | all-to-all | bytes 1048576 | tf_op jit(solution)/shard_map/all_to_all | solution.py:30
  25.3 0.0 copy-start.1
  25.3 0.1 convert_reduce_fusion
  25.3 0.0 copy-start.2
  25.4 11.3 %all_to_all.21 = f32[16,1,128]{2,1,0:T(1,128)S(1)} all-to-all(f32[16,1,128]{2,1,0:T(1,128)S(1)} %broadcast_in_dim.16), channel_id=1, replica_groups=mesh['replica_0'=4,'replica_1'=4,'fsdp_0'=8,'fsdp_1'=2,'fsdp_2'=2] {'fsd..., dimensions={0} | all-to-all | bytes 16384 | tf_op jit(solution)/shard_map/all_to_all | solution.py:30
  36.7 0.0 copy-done.2
  36.7 0.0 copy-done
  36.7 0.0 copy-done.1
  36.7 0.2 fusion.refs_1_
  36.9 21.5 %all_to_all.22 = f32[32,1,128]{2,1,0:T(1,128)S(1)} all-to-all(f32[32,1,128]{2,1,0:T(1,128)S(1)} %broadcast_in_dim.17), channel_id=1, replica_groups=mesh['replica_0'=4,'replica_1'=4,'fsdp_0'=8,'fsdp_1'=2,'fsdp_2'=2] {'rep..., dimensions={0} | all-to-all | bytes 32768 | tf_op jit(solution)/shard_map/all_to_all | solution.py:30
  58.5 0.2 fusion.1
  58.8 0.1 broadcast_in_dim.19
  58.8 17.7 %all_to_all.23 = f16[16,16,1024]{2,1,0:T(8,128)(2,1)S(1)} all-to-all(f16[16,16,1024]{2,1,0:T(8,128)(2,1)S(1)} %broadcast_in_dim.19), channel_id=1, replica_groups=mesh['replica_0'=4,'replica_1'=4,'fsdp_0'=8,'fsdp_1'=2,'fsdp_2'=2] {'rep..., dimensions={0} | all-to-all | bytes 1048576 | tf_op jit(solution)/shard_map/all_to_all | solution.py:30
  76.5 0.1 convert_multiply_fusion
  76.6 1.3 %shard_map.59 = (f32[256,1024]{1,0:T(8,128)}, f32[16,1024]{1,0:T(8,128)}, bf16[256,1024]{1,0:T(8,128)(2,1)}) custom-call(f32[256,1024]{1,0:T(8,128)S(1)} %copy-done, f32[256,1024]{1,0:T(8,128)S(1)} %fusion.refs_1_, f32[256,1024]{1,0:T(8,128)S(1)} %bitcast.18, f32[16,1024]{1,0:T(8,128)S(1)} %broadcast_multiply_fusion.refs_3_, ...), custom_call_target="tpu_custom_call" | custom-call | flops 1048576 | bytes 4718592 | tf_op jit(solution)/shard_map/pallas_call | solution.py:135
  (9 shorter events, 0.2 us)
Async XLA Ops:
  2.7 34.0 %copy-start = (f32[256,1024]{1,0:T(8,128)S(1)}, f32[256,1024]{1,0:T(8,128)}, u32[]{:S(2)}) copy-start(f32[256,1024]{1,0:T(8,128)} %refs_0_.2) | copy-start | bytes 3145732
  25.3 11.5 %copy-start.1 = (bf16[1,256,1024]{2,1,0:T(8,128)(2,1)S(1)}, bf16[1,256,1024]{2,1,0:T(8,128)(2,1)}, u32[]{:S(2)}) copy-start(bf16[1,256,1024]{2,1,0:T(8,128)(2,1)} %param.4) | copy-start | bytes 1572868
  25.3 11.3 %copy-start.2 = (f32[16,1024]{1,0:T(8,128)S(1)}, f32[16,1024]{1,0:T(8,128)}, u32[]{:S(2)}) copy-start(f32[16,1024]{1,0:T(8,128)} %param.5) | copy-start | bytes 196612
